TPU v7x, 32 devices: a whole 2x2x4 slice. The times are simulated.
32 devices in a mesh: grp: 2 (over y), band: 4 (over z), sect: 4 (over x, core).
Axes of the slice: x: 2, y: 2, z: 4, core: 2. Of those that a mesh axis runs over, the one named last changes fastest.
Arguments:
- features: bfloat16 [4, 24, 96, 2048], P('grp', 'band', None, 'sect'), parts along dimension 0, may hold values from -16 to 16
- low_level: bfloat16 [4, 24, 96, 256], P('grp', 'band'), parts along dimension 0, may hold values from -6 to 6
- land_mask: int32 [4, 24], P('grp', 'band'), parts along dimension 0, may hold values from 0 to 1, as said below
- weight_one: bfloat16 [2048, 256], P('sect'), may hold values from -0.125 to 0.125
- weight_dilated: bfloat16 [3, 3, 3, 2048, 256], P(None, None, None, 'sect'), may hold values from -0.046875 to 0.046875
- bias_branch: float32 [4, 256], replicated, may hold values from -3 to 3
- weight_pool: bfloat16 [2048, 256], P('sect'), may hold values from -0.125 to 0.125
- bias_pool: float32 [256], replicated, may hold values from -3 to 3
- weight_project: bfloat16 [1280, 256], replicated, may hold values from -0.15625 to 0.15625
- bias_project: float32 [256], replicated, may hold values from -3 to 3
- weight_reduce: bfloat16 [256, 48], replicated, may hold values from -0.375 to 0.375
- bias_reduce: float32 [48], replicated, may hold values from -3 to 3
- weight_merging: bfloat16 [3, 3, 304, 256], replicated, may hold values from -0.109375 to 0.109375
- bias_merging: float32 [256], replicated, may hold values from -3 to 3
Outputs:
- merged_map: bfloat16 [4, 24, 96, 256], P('grp', 'band'), parts along dimension 0
There are 2 independent parts, one for each index of `grp`. A program takes and returns all parts, laid end to end along the dimension named above; an argument that names none is the same for every part. Nothing has to cross between parts.
Inputs may be any that keep to these rules, and one draw needn't show every extreme that they name: `land_mask`: in every image each aligned block of 6 rows holds at most 4 ones and at least 2 ones, its first and last rows always being ones; in every image some block holds exactly 4.
All inputs are finite; a program needn't handle non-finite values.
Results may differ from a plain program's by a relative error of at most 0.012.
Values may be sent and summed in bfloat16 or wider, within the bound.
No kernel may reach another device: no remote copies, remote signals or barrier semaphores. Data moves between devices by JAX's collectives and lax.ppermute only.
A program may use at most 64 MiB of HBM per device.

v0:
```python
import jax
import jax.numpy as jnp
from jax import lax
from jax.sharding import PartitionSpec as P

DILATIONS = (12, 24, 36)
PADDING = 36
PRECISE = lax.Precision.HIGHEST


def from_behind(value, axis, by):
    count = lax.axis_size(axis)
    pairs = [(i, i + by) for i in range(count) if 0 <= i + by < count]
    return lax.ppermute(value, axis, pairs)


def extended(block, sides, width):
    for axis, dim in sides:
        count = lax.axis_size(axis)
        forward = [(i, i + 1) for i in range(count - 1)]
        backward = [(target, source) for source, target in forward]
        low = lax.ppermute(
            lax.slice_in_dim(block, block.shape[dim] - width, None, axis=dim), axis, forward
        )
        high = lax.ppermute(lax.slice_in_dim(block, 0, width, axis=dim), axis, backward)
        block = jnp.concatenate([low, block, high], axis=dim)
    return block


def extend_rows(features):
    row_count = features.shape[1]
    reach_bands = min((PADDING + row_count - 1) // row_count, lax.axis_size("band") - 1)
    upper_blocks = []
    lower_blocks = []
    moving_up = features
    moving_down = features
    for hop_index in range(reach_bands):
        moving_up = from_behind(moving_up, "band", 1)
        moving_down = from_behind(moving_down, "band", -1)
        upper_blocks.insert(0, moving_up)
        lower_blocks.append(moving_down)
    margin = reach_bands * row_count
    stacked = jnp.concatenate(upper_blocks + [features] + lower_blocks, axis=1)
    if margin >= PADDING:
        stacked = stacked[:, margin - PADDING : margin + row_count + PADDING]
    else:
        stacked = jnp.pad(stacked, ((0, 0), (PADDING - margin, PADDING - margin), (0, 0), (0, 0)))
    return jnp.pad(stacked, ((0, 0), (0, 0), (PADDING, PADDING), (0, 0)))


def branch_terms(window, select_rows, weight_one, weight_dilated, live_rows, col_count):
    batches = window.shape[0]
    channels = window.shape[3]
    centre = select_rows(0)[:, :, PADDING : PADDING + col_count].reshape(-1, channels)
    partials = [jnp.dot(centre, weight_one, preferred_element_type=jnp.float32)]
    for branch_index, dilation in enumerate(DILATIONS):
        running = jnp.zeros((centre.shape[0], weight_one.shape[1]), jnp.float32)
        for row_tap in range(3):
            band_rows = select_rows(dilation * (row_tap - 1))
            for col_tap in range(3):
                left = PADDING + dilation * (col_tap - 1)
                tap_rows = band_rows[:, :, left : left + col_count].reshape(-1, channels)
                running = running + jnp.dot(
                    tap_rows,
                    weight_dilated[branch_index, row_tap, col_tap],
                    preferred_element_type=jnp.float32,
                )
        partials.append(running)
    return jnp.concatenate(partials, axis=1).reshape(batches, live_rows, col_count, -1)


def pool_context(features, weight_pool, bias_pool, row_count, col_count):
    local_sum = jnp.sum(features, axis=(1, 2), dtype=jnp.float32)
    cell_count = row_count * lax.axis_size("band") * col_count
    weight_full = weight_pool.astype(jnp.float32)
    average = lax.psum(local_sum, "band") / cell_count
    pre_relu = lax.psum(jnp.dot(average, weight_full, precision=PRECISE), "sect")
    return jax.nn.relu(pre_relu + bias_pool)


def shards(
    features,
    low_level,
    land_mask,
    weight_one,
    weight_dilated,
    bias_branch,
    weight_pool,
    bias_pool,
    weight_project,
    bias_project,
    weight_reduce,
    bias_reduce,
    weight_merging,
    bias_merging,
):
    batches, row_count, col_count, channels = features.shape
    branch_width = weight_project.shape[1]
    window = extend_rows(features)
    pooled = pool_context(features, weight_pool, bias_pool, row_count, col_count)
    context = jnp.dot(
        pooled, weight_project[4 * branch_width :].astype(jnp.float32), precision=PRECISE
    )
    row_mask = land_mask.astype(jnp.float32)

    def select_rows(offset):
        return window[:, PADDING + offset : PADDING + offset + row_count]

    partials = branch_terms(window, select_rows, weight_one, weight_dilated, row_count, col_count)
    flat_terms = partials.astype(jnp.bfloat16).reshape(-1, partials.shape[3])
    summed_cells = lax.psum_scatter(flat_terms, "sect", scatter_dimension=0, tiled=True).astype(
        jnp.float32
    )
    share_cells = summed_cells.shape[0]
    first_cell = lax.axis_index("sect") * share_cells
    branch_cells = jax.nn.relu(summed_cells + bias_branch.reshape(-1)).astype(jnp.bfloat16)
    projected_cells = jnp.dot(
        branch_cells, weight_project[: 4 * branch_width], preferred_element_type=jnp.float32
    )
    cell_ids = first_cell + lax.broadcasted_iota(jnp.int32, (share_cells,), 0)
    batch_of = cell_ids // (row_count * col_count)
    batch_onehot = (batch_of[:, None] == lax.broadcasted_iota(jnp.int32, (1, batches), 1)).astype(
        jnp.float32
    )
    context_cells = jnp.dot(batch_onehot, context, precision=PRECISE)
    keep_all = jnp.broadcast_to(row_mask[:, :, None], (batches, row_count, col_count)).reshape(-1)
    keep_cells = lax.dynamic_slice_in_dim(keep_all, first_cell, share_cells, 0)
    out_cells = (
        jax.nn.relu(projected_cells + context_cells + bias_project) * keep_cells[:, None]
    ).astype(jnp.bfloat16)
    project_out = lax.all_gather(out_cells, "sect", axis=0, tiled=True).reshape(
        batches, row_count, col_count, branch_width
    )
    low_reduced = (
        jax.nn.relu(
            jnp.dot(
                low_level.reshape(-1, low_level.shape[3]),
                weight_reduce,
                preferred_element_type=jnp.float32,
            )
            + bias_reduce
        )
        .astype(jnp.bfloat16)
        .reshape(batches, row_count, col_count, -1)
    )
    joined = jnp.concatenate([project_out, low_reduced], axis=3)
    framed = extended(joined, (("band", 1),), 1)
    framed = jnp.pad(framed, ((0, 0), (0, 0), (1, 1), (0, 0)))
    running = jnp.zeros((batches * row_count * col_count, weight_merging.shape[3]), jnp.float32)
    for row_tap in range(3):
        for col_tap in range(3):
            tap_rows = framed[
                :, row_tap : row_tap + row_count, col_tap : col_tap + col_count
            ].reshape(-1, joined.shape[3])
            running = running + jnp.dot(
                tap_rows, weight_merging[row_tap, col_tap], preferred_element_type=jnp.float32
            )
    merged_map = (
        jax.nn.relu(running + bias_merging).reshape(batches, row_count, col_count, -1)
        * row_mask[:, :, None, None]
    )
    return merged_map.astype(jnp.bfloat16)


def solution(mesh):
    in_specs = (
        P("grp", "band", None, "sect"),
        P("grp", "band", None, None),
        P("grp", "band"),
        P("sect", None),
        P(None, None, None, "sect", None),
        P(),
        P("sect", None),
        P(),
        P(),
        P(),
        P(),
        P(),
        P(),
        P(),
    )
    out_specs = P("grp", "band", None, None)
    return jax.shard_map(shards, mesh=mesh, in_specs=in_specs, out_specs=out_specs, check_vma=False)
```

profile of v0, /device:TPU:0, one launch (start us, length us, event | category | flops | bytes accessed | tf_op | source)
XLA Modules:
  0.0 206.0 jit_solution(5829789880484812974)
XLA Ops:
  6.5 5.1 %collective-permute-start = (bf16[2,6,96,512]{3,2,1,0:T(8,128)(2,1)}, bf16[2,6,96,512]{3,2,1,0:T(8,128)(2,1)S(1)}, u32[]{:S(2)}, u32[]{:S(2)}) collective-permute-start(bf16[2,6,96,512]{3,2,1,0:T(8,128)(2,1)} %param.14), channel_id=1, source_target_pairs={{0,4},{4,8},{8,12},{1,5},{5,9},{9,13},{2,6},{6,10},{10,14},{3,7},{... | collective-permute-start | bytes 3538952 | tf_op jit(solution)/shard_map/ppermute | solution.py:14
  11.7 1.3 collective-permute-start.3
  13.0 24.1 %collective-permute-done = bf16[2,6,96,512]{3,2,1,0:T(8,128)(2,1)S(1)} collective-permute-done((bf16[2,6,96,512]{3,2,1,0:T(8,128)(2,1)}, bf16[2,6,96,512]{3,2,1,0:T(8,128)(2,1)S(1)}, u32[]{:S(2)}, u32[]{:S(2)}) %collective-permute-start) | collective-permute-done | bytes 1179680 | tf_op jit(solution)/shard_map/ppermute | solution.py:14
  37.1 4.3 %collective-permute-start.1 = (bf16[2,6,96,512]{3,2,1,0:T(8,128)(2,1)S(1)}, bf16[2,6,96,512]{3,2,1,0:T(8,128)(2,1)S(1)}, u32[]{:S(2)}, u32[]{:S(2)}) collective-permute-start(bf16[2,6,96,512]{3,2,1,0:T(8,128)(2,1)S(1)} %collective-permute-done), channel_id=1, source_target_pairs={{0,4},{4,8},{8,12},{1,5},{5,9},{9,13},{2,6},{6,10},{10,14},{3,7},{... | collective-permute-start | bytes 3538952 | tf_op jit(solution)/shard_map/ppermute | solution.py:14
  41.5 2.4 %fusion.43 = f32[1152,256]{1,0:T(8,128)} fusion(bf16[3,3,3,512,256]{4,3,2,1,0:T(8,128)(2,1)} %param.18), kind=kOutput, calls=%fused_computation.92 | convolution fusion | flops 301989888 | bytes 1441792 | tf_op jit(solution)/shard_map/dot_general | solution.py:63
  43.9 2.5 %fusion.41 = f32[1152,256]{1,0:T(8,128)} fusion(bf16[3,3,3,512,256]{4,3,2,1,0:T(8,128)(2,1)} %param.18), kind=kOutput, calls=%fused_computation.90 | convolution fusion | flops 301989888 | bytes 1441792 | tf_op jit(solution)/shard_map/dot_general | solution.py:63
  46.5 1.3 convolution_convert_fusion
  47.8 1.5 collective-permute-start.4
  49.3 2.5 %fusion.39 = f32[1152,256]{1,0:T(8,128)} fusion(bf16[3,3,3,512,256]{4,3,2,1,0:T(8,128)(2,1)} %param.18), kind=kOutput, calls=%fused_computation.88 | convolution fusion | flops 301989888 | bytes 1441792 | tf_op jit(solution)/shard_map/dot_general | solution.py:63
  51.8 2.5 %fusion.78 = f32[1152,256]{1,0:T(8,128)} fusion(bf16[1152,512]{1,0:T(8,128)(2,1)S(1)} %bitcast.182, bf16[3,3,3,512,256]{4,3,2,1,0:T(8,128)(2,1)} %param.18), kind=kOutput, calls=%fused_computation.127 | convolution fusion | flops 301989888 | bytes 2621440 | tf_op jit(solution)/shard_map/dot_general | solution.py:63
  54.3 11.4 %collective-permute-done.1 = bf16[2,6,96,512]{3,2,1,0:T(8,128)(2,1)S(1)} collective-permute-done((bf16[2,6,96,512]{3,2,1,0:T(8,128)(2,1)S(1)}, bf16[2,6,96,512]{3,2,1,0:T(8,128)(2,1)S(1)}, u32[]{:S(2)}, u32[]{:S(2)}) %collective-permute-start.1) | collective-permute-done | bytes 1179680 | tf_op jit(solution)/shard_map/ppermute | solution.py:14
  65.7 4.4 %collective-permute-start.2 = (bf16[2,6,96,512]{3,2,1,0:T(8,128)(2,1)S(1)}, bf16[2,6,96,512]{3,2,1,0:T(8,128)(2,1)S(1)}, u32[]{:S(2)}, u32[]{:S(2)}) collective-permute-start(bf16[2,6,96,512]{3,2,1,0:T(8,128)(2,1)S(1)} %collective-permute-done.1), channel_id=1, source_target_pairs={{0,4},{4,8},{8,12},{1,5},{5,9},{9,13},{2,6},{6,10},{10,14},{3,7},{... | collective-permute-start | bytes 3538952 | tf_op jit(solution)/shard_map/ppermute | solution.py:14
  70.2 2.5 %fusion.37 = f32[1152,256]{1,0:T(8,128)} fusion(bf16[3,3,3,512,256]{4,3,2,1,0:T(8,128)(2,1)} %param.18), kind=kOutput, calls=%fused_computation.86 | convolution fusion | flops 301989888 | bytes 1441792 | tf_op jit(solution)/shard_map/dot_general | solution.py:63
  72.7 1.5 fusion.64
  74.2 1.5 fusion.51
  75.7 0.8 collective-permute-done.4
  76.5 1.3 collective-permute-start.5
  77.7 1.5 fusion.84
  79.2 1.6 fusion.73
  80.8 12.7 %collective-permute-done.2 = bf16[2,6,96,512]{3,2,1,0:T(8,128)(2,1)S(1)} collective-permute-done((bf16[2,6,96,512]{3,2,1,0:T(8,128)(2,1)S(1)}, bf16[2,6,96,512]{3,2,1,0:T(8,128)(2,1)S(1)}, u32[]{:S(2)}, u32[]{:S(2)}) %collective-permute-start.2) | collective-permute-done | bytes 1179680 | tf_op jit(solution)/shard_map/ppermute | solution.py:14
  94.0 9.9 %collective-permute-done.5 = bf16[2,6,96,512]{3,2,1,0:T(8,128)(2,1)S(1)} collective-permute-done((bf16[2,6,96,512]{3,2,1,0:T(8,128)(2,1)S(1)}, bf16[2,6,96,512]{3,2,1,0:T(8,128)(2,1)S(1)}, u32[]{:S(2)}, u32[]{:S(2)}) %collective-permute-start.5) | collective-permute-done | bytes 1179680 | tf_op jit(solution)/shard_map/ppermute | solution.py:14
  104.1 12.3 %pad_slice_fusion.11 = (bf16[2,6,96,512]{3,2,1,0:T(8,128)(2,1)S(1)}, bf16[2,6,96,512]{3,2,1,0:T(8,128)(2,1)S(1)}, bf16[2,6,96,512]{3,2,1,0:T(8,128)(2,1)}, bf16[...) fusion(bf16[2,42,96,512]{3,2,1,0:T(8,128)(2,1)S(1)} %constant_d, ...), kind=kLoop, calls=%fused_computation.11 | loop fusion | bytes 29491200 | tf_op jit(solution)/shard_map/slice | solution.py:62
  116.4 1.8 fusion.80
  118.7 0.8 copy-done.5
  120.0 0.8 copy-done.4
  121.3 0.8 copy-done.3
  124.5 0.8 copy-done.12
  126.1 0.8 copy-done.9
  128.2 0.8 copy-done.11
  129.8 0.8 copy-done.8
  131.9 0.8 copy-done.10
  133.5 0.8 copy-done.7
  135.6 0.6 copy-done.15
  136.2 1.8 pad_maximum_fusion
  138.1 0.6 copy-done.24
  139.1 9.9 %psum.14 = f32[2,512]{1,0:T(2,128)S(1)} all-reduce(f32[2,512]{1,0:T(2,128)S(1)} %convert_reduce_fusion), channel_id=1, replica_groups=mesh['grp'=2,'band'=4,'sect'=4] {'band'}, use_global_device_ids=true, to_apply=%region_2.3 | all-reduce | flops 1024 | bytes 8192 | tf_op jit(solution)/shard_map/psum | solution.py:76
  149.2 5.7 %psum.15 = f32[2,256]{1,0:T(2,128)S(1)} all-reduce(f32[2,256]{1,0:T(2,128)S(1)} %fusion.137), channel_id=1, replica_groups=mesh['grp'=2,'band'=4,'sect'=4] {'sect'}, use_global_device_ids=true, to_apply=%region_3.4 | all-reduce | flops 512 | bytes 4096 | tf_op jit(solution)/shard_map/psum | solution.py:77
  155.4 16.0 %reduce-scatter.2.cloned.1.call-done = bf16[288,1024]{1,0:T(8,128)(2,1)} async-done(((bf16[1152,1024]{1,0:T(8,128)(2,1)}), bf16[288,1024]{1,0:T(8,128)(2,1)}) %reduce-scatter.2.cloned.1.call-update) | async-done | bytes 589840 | tf_op jit(solution)/shard_map/reduce_scatter | solution.py:111
  171.4 1.4 fusion.34
  173.2 7.3 %all_gather.3 = bf16[1152,256]{1,0:T(8,128)(2,1)S(1)} all-gather(bf16[288,256]{1,0:T(8,128)(2,1)S(1)} %fusion.30), channel_id=1, replica_groups=mesh['grp'=2,'band'=4,'sect'=4] {'sect'}, dimensions={0}, use_global_device_ids=true | all-gather | bytes 737280 | tf_op jit(solution)/shard_map/all_gather | solution.py:131
  180.5 3.4 %collective-permute-start.6 = (bf16[2,1,96,304]{3,2,1,0:T(8,128)(2,1)S(1)}, bf16[2,1,96,304]{3,2,1,0:T(8,128)(2,1)S(1)}, u32[]{:S(2)}, u32[]{:S(2)}) collective-permute-start(bf16[2,1,96,304]{3,2,1,0:T(8,128)(2,1)S(1)} %get-tuple-element.31), channel_id=1, source_target_pairs={{0,4},{4,8},{8,12},{1,5},{5,9},{9,13},{2,6},{6,10},{10,14},{3,7},{... | collective-permute-start | bytes 350216 | tf_op jit(solution)/shard_map/ppermute | solution.py:22
  183.9 1.3 collective-permute-start.7
  185.2 2.3 %collective-permute-done.6 = bf16[2,1,96,304]{3,2,1,0:T(8,128)(2,1)S(1)} collective-permute-done((bf16[2,1,96,304]{3,2,1,0:T(8,128)(2,1)S(1)}, bf16[2,1,96,304]{3,2,1,0:T(8,128)(2,1)S(1)}, u32[]{:S(2)}, u32[]{:S(2)}) %collective-permute-start.6) | collective-permute-done | bytes 116768 | tf_op jit(solution)/shard_map/ppermute | solution.py:22
  187.5 4.1 %collective-permute-done.7 = bf16[2,1,96,304]{3,2,1,0:T(8,128)(2,1)S(1)} collective-permute-done((bf16[2,1,96,304]{3,2,1,0:T(8,128)(2,1)S(1)}, bf16[2,1,96,304]{3,2,1,0:T(8,128)(2,1)S(1)}, u32[]{:S(2)}, u32[]{:S(2)}) %collective-permute-start.7) | collective-permute-done | bytes 116768 | tf_op jit(solution)/shard_map/ppermute | solution.py:25
  191.7 0.5 select_maximum_fusion
  192.2 0.8 fusion.153
  193.0 0.5 copy-done.16
  198.2 1.0 multiply_convert_fusion
  (99 shorter events, 16.7 us)
Async XLA Ops:
  6.5 148.5 %copy-start = (bf16[2,6,96,256]{3,2,1,0:T(8,128)(2,1)S(1)}, bf16[2,6,96,256]{3,2,1,0:T(8,128)(2,1)}, u32[]{:S(2)}) copy-start(bf16[2,6,96,256]{3,2,1,0:T(8,128)(2,1)} %param.15) | copy-start | bytes 1769476
  6.5 164.9 %reduce-scatter.2.cloned.1.call-start = ((), (), s32[]{:S(2)}) async-start(), calls=%async_computation.1 | async-start | bytes 2949120 | tf_op jit(solution)/shard_map/reduce_scatter | solution.py:111
  6.5 30.6 %collective-permute-start = (bf16[2,6,96,512]{3,2,1,0:T(8,128)(2,1)}, bf16[2,6,96,512]{3,2,1,0:T(8,128)(2,1)S(1)}, u32[]{:S(2)}, u32[]{:S(2)}) collective-permute-start(bf16[2,6,96,512]{3,2,1,0:T(8,128)(2,1)} %param.14), channel_id=1, source_target_pairs={{0,4},{4,8},{8,12},{1,5},{5,9},{9,13},{2,6},{6,10},{10,14},{3,7},{... | collective-permute-start | bytes 3538952 | tf_op jit(solution)/shard_map/ppermute | solution.py:14
  11.7 36.1 %collective-permute-start.3 = (bf16[2,6,96,512]{3,2,1,0:T(8,128)(2,1)}, bf16[2,6,96,512]{3,2,1,0:T(8,128)(2,1)S(1)}, u32[]{:S(2)}, u32[]{:S(2)}) collective-permute-start(bf16[2,6,96,512]{3,2,1,0:T(8,128)(2,1)} %param.14), channel_id=1, source_target_pairs={{4,0},{8,4},{12,8},{5,1},{9,5},{13,9},{6,2},{10,6},{14,10},{7,3},{... | collective-permute-start | bytes 3538952 | tf_op jit(solution)/shard_map/ppermute | solution.py:14
  37.1 28.6 %collective-permute-start.1 = (bf16[2,6,96,512]{3,2,1,0:T(8,128)(2,1)S(1)}, bf16[2,6,96,512]{3,2,1,0:T(8,128)(2,1)S(1)}, u32[]{:S(2)}, u32[]{:S(2)}) collective-permute-start(bf16[2,6,96,512]{3,2,1,0:T(8,128)(2,1)S(1)} %collective-permute-done), channel_id=1, source_target_pairs={{0,4},{4,8},{8,12},{1,5},{5,9},{9,13},{2,6},{6,10},{10,14},{3,7},{... | collective-permute-start | bytes 3538952 | tf_op jit(solution)/shard_map/ppermute | solution.py:14
  43.9 2.6 %copy-start.1 = (bf16[2,6,96,512]{3,2,1,0:T(8,128)(2,1)S(1)}, bf16[2,6,96,512]{3,2,1,0:T(8,128)(2,1)}, u32[]{:S(2)}) copy-start(bf16[2,6,96,512]{3,2,1,0:T(8,128)(2,1)} %param.14) | copy-start | bytes 3538948
  43.9 2.6 %copy-start.22 = (bf16[512,256]{1,0:T(8,128)(2,1)S(1)}, bf16[512,256]{1,0:T(8,128)(2,1)}, u32[]{:S(2)}) copy-start(bf16[512,256]{1,0:T(8,128)(2,1)} %param.17) | copy-start | bytes 786436
  46.5 26.2 %copy-start.2 = (bf16[3,3,3,512,256]{4,3,2,1,0:T(8,128)(2,1)S(1)}, bf16[3,3,3,512,256]{4,3,2,1,0:T(8,128)(2,1)}, u32[]{:S(2)}) copy-start(bf16[3,3,3,512,256]{4,3,2,1,0:T(8,128)(2,1)} %param.18) | copy-start | bytes 21233668
  47.8 28.7 %collective-permute-start.4 = (bf16[2,6,96,512]{3,2,1,0:T(8,128)(2,1)S(1)}, bf16[2,6,96,512]{3,2,1,0:T(8,128)(2,1)S(1)}, u32[]{:S(2)}, u32[]{:S(2)}) collective-permute-start(bf16[2,6,96,512]{3,2,1,0:T(8,128)(2,1)S(1)} %collective-permute-done.3), channel_id=1, source_target_pairs={{4,0},{8,4},{12,8},{5,1},{9,5},{13,9},{6,2},{10,6},{14,10},{7,3},{... | collective-permute-start | bytes 3538952 | tf_op jit(solution)/shard_map/ppermute | solution.py:14
  65.7 27.8 %collective-permute-start.2 = (bf16[2,6,96,512]{3,2,1,0:T(8,128)(2,1)S(1)}, bf16[2,6,96,512]{3,2,1,0:T(8,128)(2,1)S(1)}, u32[]{:S(2)}, u32[]{:S(2)}) collective-permute-start(bf16[2,6,96,512]{3,2,1,0:T(8,128)(2,1)S(1)} %collective-permute-done.1), channel_id=1, source_target_pairs={{0,4},{4,8},{8,12},{1,5},{5,9},{9,13},{2,6},{6,10},{10,14},{3,7},{... | collective-permute-start | bytes 3538952 | tf_op jit(solution)/shard_map/ppermute | solution.py:14
  76.5 27.5 %collective-permute-start.5 = (bf16[2,6,96,512]{3,2,1,0:T(8,128)(2,1)S(1)}, bf16[2,6,96,512]{3,2,1,0:T(8,128)(2,1)S(1)}, u32[]{:S(2)}, u32[]{:S(2)}) collective-permute-start(bf16[2,6,96,512]{3,2,1,0:T(8,128)(2,1)S(1)} %collective-permute-done.4), channel_id=1, source_target_pairs={{4,0},{8,4},{12,8},{5,1},{9,5},{13,9},{6,2},{10,6},{14,10},{7,3},{... | collective-permute-start | bytes 3538952 | tf_op jit(solution)/shard_map/ppermute | solution.py:14
  116.4 1.8 copy-start.6
  118.3 1.3 copy-start.5
  119.5 1.3 copy-start.4
  120.8 1.3 copy-start.3
  124.0 1.3 copy-start.12
  124.0 1.6 copy-start.13
  125.6 1.3 copy-start.9
  125.6 1.6 copy-start.14
  127.7 1.3 copy-start.11
  127.7 1.6 copy-start.18
  129.3 1.3 copy-start.8
  129.3 1.6 copy-start.19
  131.4 1.3 copy-start.10
  131.4 1.6 copy-start.17
  133.0 1.3 copy-start.7
  133.0 1.6 copy-start.20
  135.1 1.1 copy-start.15
  138.0 0.7 copy-start.24
  138.0 0.7 copy-start.28
  138.0 11.0 %copy-start.21 = (bf16[512,256]{1,0:T(8,128)(2,1)S(1)}, bf16[512,256]{1,0:T(8,128)(2,1)}, u32[]{:S(2)}) copy-start(bf16[512,256]{1,0:T(8,128)(2,1)} %param.20) | copy-start | bytes 786436
  138.0 16.9 %copy-start.23 = (bf16[1280,256]{1,0:T(8,128)(2,1)S(1)}, bf16[1280,256]{1,0:T(8,128)(2,1)}, u32[]{:S(2)}) copy-start(bf16[1280,256]{1,0:T(8,128)(2,1)} %param.22) | copy-start | bytes 1966084
  138.0 16.9 %copy-start.25 = (f32[256]{0:T(256)S(1)}, f32[256]{0:T(256)}, u32[]{:S(2)}) copy-start(f32[256]{0:T(256)} %param.21) | copy-start | bytes 3076
  138.0 17.0 %copy-start.29 = (bf16[256,48]{0,1:T(8,128)(2,1)S(1)}, bf16[256,48]{0,1:T(8,128)(2,1)}, u32[]{:S(2)}) copy-start(bf16[256,48]{0,1:T(8,128)(2,1)} %param.24) | copy-start | bytes 73732
  138.0 17.0 %copy-start.30 = (f32[48]{0:T(128)S(1)}, f32[48]{0:T(128)}, u32[]{:S(2)}) copy-start(f32[48]{0:T(128)} %param.25) | copy-start | bytes 580
  155.4 17.4 %copy-start.26 = (f32[256]{0:T(256)S(1)}, f32[256]{0:T(256)}, u32[]{:S(2)}) copy-start(f32[256]{0:T(256)} %param.23) | copy-start | bytes 3076
  180.5 7.0 %collective-permute-start.6 = (bf16[2,1,96,304]{3,2,1,0:T(8,128)(2,1)S(1)}, bf16[2,1,96,304]{3,2,1,0:T(8,128)(2,1)S(1)}, u32[]{:S(2)}, u32[]{:S(2)}) collective-permute-start(bf16[2,1,96,304]{3,2,1,0:T(8,128)(2,1)S(1)} %get-tuple-element.31), channel_id=1, source_target_pairs={{0,4},{4,8},{8,12},{1,5},{5,9},{9,13},{2,6},{6,10},{10,14},{3,7},{... | collective-permute-start | bytes 350216 | tf_op jit(solution)/shard_map/ppermute | solution.py:22
  183.9 7.7 %collective-permute-start.7 = (bf16[2,1,96,304]{3,2,1,0:T(8,128)(2,1)S(1)}, bf16[2,1,96,304]{3,2,1,0:T(8,128)(2,1)S(1)}, u32[]{:S(2)}, u32[]{:S(2)}) collective-permute-start(bf16[2,1,96,304]{3,2,1,0:T(8,128)(2,1)S(1)} %get-tuple-element.32), channel_id=1, source_target_pairs={{4,0},{8,4},{12,8},{5,1},{9,5},{13,9},{6,2},{10,6},{14,10},{7,3},{... | collective-permute-start | bytes 350216 | tf_op jit(solution)/shard_map/ppermute | solution.py:25
  192.2 1.4 copy-start.16
  197.0 0.7 copy-start.27
Sparse Core Ops, SparseCore 0:
  138.1 33.2 reduce-scatter.1
where the time goes:
time: 207 us; the launch traced here: 206 us
  waiting for transfers between devices  81.5 us (39%)
  matrix products  36 us (17%)
  local copies, waits for them, and re-layouts  25.2 us (12%)
  blocking collectives  22.9 us (11%)
  starting transfers between devices  22.7 us (11%)
  between operations  14 us (7%)
  other arithmetic  3.7 us (2%)
    ppermute x6, waiting for transfers between devices, from_behind(): return lax.ppermute(value, axis, pairs)  59 us
    dot_general x27, matrix products, branch_terms(): jnp.dot(tap_rows, weight_dilated[branch_index, row_tap, col_tap], preferr...  28.3 us
    ppermute x6, starting transfers between devices, from_behind(): return lax.ppermute(value, axis, pairs)  18 us
    reduce_scatter x1, waiting for transfers between devices, shards(): lax.psum_scatter(flat_terms, 'sect', scatter_dimension=0, tiled=True)  16 us
    slice x1, local copies, waits for them, and re-layouts, branch_terms(): tap_rows = band_rows[:, :, left:left + col_count].reshape(-1, channels)  12.3 us
    unnamed x69, local copies, waits for them, and re-layouts  11.7 us
    psum x1, blocking collectives, pool_context(): average = lax.psum(local_sum, 'band') / cell_count  9.89 us
    all_gather x1, blocking collectives, shards(): lax.all_gather(out_cells, 'sect', axis=0, tiled=True)  7.34 us
  transfers between devices with their start and end apart: 9, of which 8 were waited for; matrix products, arithmetic and copies ran while one was open for 10% of the time, Pallas kernels for 0%

commit v1 on v0

--- a/solution.py
+++ b/solution.py
@@ -1,11 +1,519 @@
+import functools
+
 import jax
 import jax.numpy as jnp
 from jax import lax
+from jax.experimental import pallas as pl
+from jax.experimental.pallas import tpu as pltpu
 from jax.sharding import PartitionSpec as P
 
 DILATIONS = (12, 24, 36)
 PADDING = 36
 PRECISE = lax.Precision.HIGHEST
+ROW_BLOCK = 6
+MOST_LAND = 4
+VMEM_LIMIT = 50 * 2 ** 20
+F32 = jnp.float32
+BF16 = jnp.bfloat16
+VMEM = pl.BlockSpec(memory_space=pltpu.VMEM)
+SMEM = pl.BlockSpec(memory_space=pltpu.SMEM)
+ANY = pl.BlockSpec(memory_space=pl.ANY)
+
+
+def call(body, outs, in_specs, scratch, flops, bytes_accessed):
+    return pl.pallas_call(
+        body,
+        out_shape=outs,
+        in_specs=in_specs,
+        out_specs=jax.tree.map(lambda _: VMEM, outs),
+        scratch_shapes=scratch,
+        compiler_params=pltpu.CompilerParams(vmem_limit_bytes=VMEM_LIMIT),
+        cost_estimate=pl.CostEstimate(
+            flops=flops, bytes_accessed=bytes_accessed, transcendentals=0
+        ),
+    )
+
+
+def reversed_bits(value, bits):
+    return sum(((value >> bit) & 1) << (bits - 1 - bit) for bit in range(bits))
+
+
+def fill_slots(mask_ref, slots_ref, batches, row_count):
+    for image in range(batches):
+        inner = range(1, row_count - 1)
+        lives = {row: (mask_ref[image, row] > 0).astype(jnp.int32) for row in inner}
+        land_total = sum(lives.values())
+        land_before, sea_before = 0, 0
+        chosen = [0] * (MOST_LAND - 2)
+        for row in inner:
+            live = lives[row]
+            rank = jnp.where(live > 0, land_before, land_total + sea_before)
+            chosen = [
+                value + row * (rank == slot).astype(jnp.int32)
+                for slot, value in enumerate(chosen)
+            ]
+            land_before = land_before + live
+            sea_before = sea_before + (1 - live)
+        base = image * MOST_LAND
+        slots_ref[base] = jnp.int32(0)
+        for slot, value in enumerate(chosen):
+            slots_ref[base + 1 + slot] = value
+        slots_ref[base + MOST_LAND - 1] = jnp.int32(row_count - 1)
+
+
+def split_three(value):
+    high = value.astype(BF16)
+    rest = value - high.astype(F32)
+    middle = rest.astype(BF16)
+    low = (rest - middle.astype(F32)).astype(BF16)
+    return high, middle, low
+
+
+def precise_dot(value, weight):
+    return sum(jnp.dot(part, weight, preferred_element_type=F32) for part in split_three(value))
+
+
+def shifted(value, by, columns):
+    column = lax.broadcasted_iota(jnp.int32, value.shape, 0) % columns
+    moved = pltpu.roll(value, by % value.shape[0], 0)
+    inside = column >= by if by > 0 else column < columns + by
+    return jnp.where(inside, moved, 0.0)
+
+
+class Plan:
+    def __init__(self, batches, row_count, columns, bands, sects):
+        self.batches, self.row_count, self.columns = batches, row_count, columns
+        self.bands, self.sects = bands, sects
+        self.bits = sects.bit_length() - 1
+        self.share_rows = batches * MOST_LAND // sects
+        self.share = self.share_rows * columns
+        self.terms = []
+        for branch, dilation in enumerate(DILATIONS):
+            hop = dilation // row_count
+            if hop >= bands:
+                continue
+            up = [(b, b + hop) for b in range(bands - hop)]
+            down = [(target, source) for source, target in up]
+            if 2 * hop >= bands:
+                self.terms.append((branch, hop, None, up + down))
+            else:
+                self.terms.append((branch, hop, 0, up))
+                self.terms.append((branch, hop, 2, down))
+
+    def tap_columns(self, dilation):
+        return [1] + ([0, 2] if dilation < self.columns else [])
+
+
+def branch_kernel(plan, place_ref, mask_ref, far_mask_ref, features_ref, one_ref, dilated_ref, *refs):
+    terms = len(plan.terms)
+    outs = refs[: 2 + (2 if terms else 0)]
+    slots_ref, rows_ref, weights_ref, row_sems, weight_sems = refs[len(outs) :]
+    columns, width = plan.columns, one_ref.shape[1]
+    half = plan.sects // 2 * plan.share
+    sect, band = place_ref[0], place_ref[1]
+
+    def fetch_rows(group, mask):
+        fill_slots(mask, slots_ref, plan.batches, plan.row_count)
+        copies = []
+        for position in range(plan.sects):
+            owner = sect ^ reversed_bits(position, plan.bits)
+            for row in range(plan.share_rows):
+                place = owner * plan.share_rows + row
+                image = lax.div(place, MOST_LAND)
+                index = position * plan.share_rows + row
+                copies.append(
+                    pltpu.make_async_copy(
+                        features_ref.at[image, slots_ref[place]],
+                        rows_ref.at[group, pl.ds(index * columns, columns)],
+                        row_sems.at[group, index],
+                    )
+                )
+                copies[-1].start()
+        return copies
+
+    weight_copies = []
+
+    def fetch_weight(source):
+        index = len(weight_copies)
+        copy = pltpu.make_async_copy(source, weights_ref.at[index], weight_sems.at[index])
+        copy.start()
+        weight_copies.append(copy)
+
+    def product(group, index):
+        weight_copies[index].wait()
+        return jnp.dot(rows_ref[group], weights_ref[index], preferred_element_type=F32)
+
+    own_rows = fetch_rows(0, mask_ref)
+    fetch_weight(one_ref)
+    work = [(0, 0, None, [(0, 0)])]
+    for branch, dilation in enumerate(DILATIONS):
+        taps = []
+        for tap in plan.tap_columns(dilation):
+            taps.append((len(weight_copies), (1 - tap) * dilation))
+            fetch_weight(dilated_ref.at[branch, 1, tap])
+        work.append((0, branch + 1, None, taps))
+    term_rows = []
+    for term, (branch, hop, row_tap, _) in enumerate(plan.terms):
+        term_rows.append(fetch_rows(term + 1, far_mask_ref.at[term]))
+        if row_tap is None:
+            row_tap = jnp.where(band + hop < plan.bands, 0, 2)
+        taps = []
+        for tap in plan.tap_columns(DILATIONS[branch]):
+            taps.append((len(weight_copies), (1 - tap) * DILATIONS[branch]))
+            fetch_weight(dilated_ref.at[branch, row_tap, tap])
+        work.append((term + 1, None, term, taps))
+    for copy in own_rows:
+        copy.wait()
+    for group, branch, term, taps in work:
+        if term is not None:
+            for copy in term_rows[term]:
+                copy.wait()
+        total = product(group, taps[0][0])
+        for index, by in taps[1:]:
+            total = total + shifted(product(group, index), by, columns)
+        total = total.astype(BF16)
+        keep, send = outs[:2] if term is None else outs[2:]
+        place = branch if term is None else term
+        keep[:, pl.ds(place * width, width)] = total[:half]
+        send[:, pl.ds(place * width, width)] = total[half:]
+
+
+def branch_partials(plan, place, mask, far_mask, features, weight_one, weight_dilated):
+    terms = len(plan.terms)
+    channels, width = weight_one.shape
+    half = plan.sects // 2 * plan.share
+    own = jax.ShapeDtypeStruct((half, 4 * width), BF16)
+    outs = [own, own]
+    if terms:
+        far = jax.ShapeDtypeStruct((half, terms * width), BF16)
+        outs += [far, far]
+    weights = 1 + 9 + 3 * terms
+    scratch = [
+        pltpu.SMEM((plan.batches * MOST_LAND,), jnp.int32),
+        pltpu.VMEM((1 + terms, 2 * half, channels), BF16),
+        pltpu.VMEM((weights, channels, width), BF16),
+        pltpu.SemaphoreType.DMA((1 + terms, plan.batches * MOST_LAND)),
+        pltpu.SemaphoreType.DMA((weights,)),
+    ]
+    flops = 2 * weights * 2 * half * channels * width
+    return call(
+        functools.partial(branch_kernel, plan),
+        tuple(outs),
+        [SMEM, SMEM, SMEM, ANY, ANY, ANY],
+        scratch,
+        flops,
+        2 * (weights * channels * width + (1 + terms) * 2 * half * channels),
+    )(place, mask, far_mask, features, weight_one, weight_dilated)
+
+
+def pool_kernel(features_ref, weight_ref, out_ref):
+    batches, row_count, columns, channels = features_ref.shape
+    sums = [
+        jnp.sum(
+            features_ref[image].astype(F32).reshape(row_count * columns, channels),
+            axis=0,
+            keepdims=True,
+        )
+        for image in range(batches)
+    ]
+    row = lax.broadcasted_iota(jnp.int32, (out_ref.shape[0], channels), 0)
+    stacked = jnp.zeros((out_ref.shape[0], channels), F32)
+    for image, value in enumerate(sums):
+        stacked = jnp.where(row == image, value, stacked)
+    out_ref[...] = precise_dot(stacked, weight_ref[...])
+
+
+def low_kernel(place_ref, low_ref, first_ref, second_ref, reduce_ref, bias_reduce_ref, merging_ref, bias_ref, out_ref, framed_ref):
+    batches, row_count, columns, depth = low_ref.shape
+    band, bands = place_ref[1], place_ref[2]
+    wide = reduce_ref.shape[1]
+    reduced = wide // 3
+    even = band % 2 == 0
+
+    def reduce(rows):
+        value = jnp.dot(rows, reduce_ref[...], preferred_element_type=F32) + bias_reduce_ref[...]
+        value = jnp.maximum(value, 0.0).astype(BF16).astype(F32)
+        lane = lax.broadcasted_iota(jnp.int32, value.shape, 1)
+        return jnp.where(
+            lane < reduced,
+            shifted(value, 1, columns),
+            jnp.where(lane < 2 * reduced, value, shifted(value, -1, columns)),
+        )
+
+    framed_ref[:, 1 : row_count + 1] = (
+        reduce(low_ref[...].reshape(-1, depth)).astype(BF16).reshape(batches, row_count, columns, wide)
+    )
+    first = reduce(first_ref[...].reshape(-1, depth))
+    second = reduce(second_ref[...].reshape(-1, depth))
+    above = jnp.where(even, second, first) * jnp.where(band > 0, 1.0, 0.0)
+    below = jnp.where(even, first, second) * jnp.where(band < bands - 1, 1.0, 0.0)
+    framed_ref[:, 0] = above.astype(BF16).reshape(batches, columns, wide)
+    framed_ref[:, row_count + 1] = below.astype(BF16).reshape(batches, columns, wide)
+    for image in range(batches):
+        total = jnp.zeros((row_count * columns, out_ref.shape[3]), F32) + bias_ref[...]
+        for tap in range(3):
+            rows = framed_ref[image, tap : tap + row_count].reshape(-1, wide)
+            total = total + jnp.dot(rows, merging_ref[tap], preferred_element_type=F32)
+        out_ref[image] = total.reshape(row_count, columns, -1)
+
+
+def project_kernel(plan, place_ref, mask_ref, keep_ref, moved_ref, bias_branch_ref, pool_ref, bias_pool_ref, weight_ref, bias_ref, *refs):
+    far_refs = refs[: len(plan.terms)]
+    out_ref, edge_ref, slots_ref, context_ref = refs[len(plan.terms) :]
+    columns, width = plan.columns, weight_ref.shape[1]
+    sect = place_ref[0]
+    fill_slots(mask_ref, slots_ref, plan.batches, plan.row_count)
+    cells = plan.row_count * plan.bands * columns
+    pooled = jnp.maximum(pool_ref[...] / cells + bias_pool_ref[...], 0.0)
+    context_ref[...] = precise_dot(pooled, weight_ref[4 * width :]) + bias_ref[...]
+    total = jnp.zeros((plan.share, width), F32)
+    for branch in range(4):
+        lanes = pl.ds(branch * width, width)
+        value = keep_ref[:, lanes].astype(F32) + moved_ref[:, lanes].astype(F32)
+        for term, far in zip(plan.terms, far_refs):
+            if term[0] + 1 == branch:
+                value = value + far[...].astype(F32)
+        value = jnp.maximum(value + bias_branch_ref[pl.ds(branch, 1)], 0.0).astype(BF16)
+        total = total + jnp.dot(
+            value, weight_ref[pl.ds(branch * width, width)], preferred_element_type=F32
+        )
+    for row in range(plan.share_rows):
+        place = sect * plan.share_rows + row
+        image = lax.div(place, MOST_LAND)
+        keep = mask_ref[image, slots_ref[place]].astype(F32)
+        value = total[row * columns : (row + 1) * columns] + context_ref[pl.ds(image, 1)]
+        out_ref[pl.ds(row * columns, columns)] = (jnp.maximum(value, 0.0) * keep).astype(BF16)
+    at_top = lax.rem(sect * plan.share_rows, MOST_LAND) == 0
+
+    @pl.when(at_top)
+    def _():
+        edge_ref[...] = out_ref[pl.ds(0, columns)]
+
+    @pl.when(jnp.logical_not(at_top))
+    def _():
+        edge_ref[...] = out_ref[pl.ds(plan.share - columns, columns)]
+
+
+def merge_kernel(plan, place_ref, mask_ref, low_ref, weight_ref, *refs):
+    sects, columns = plan.sects, plan.columns
+    share_refs, edge_refs = refs[:sects], refs[sects : 2 * sects]
+    out_ref, slots_ref, rows_ref, halo_ref, total_ref = refs[2 * sects :]
+    width = weight_ref.shape[3]
+    sect = place_ref[0]
+    fill_slots(mask_ref, slots_ref, plan.batches, plan.row_count)
+
+    def spread(value):
+        wide = value.astype(F32)
+        return (
+            shifted(wide, 1, columns).astype(BF16),
+            value,
+            shifted(wide, -1, columns).astype(BF16),
+        )
+
+    def weight(tap):
+        return jnp.concatenate([weight_ref[tap, side, :width] for side in range(3)], axis=0)
+
+    total_ref[:, 1 : plan.row_count + 1] = low_ref[...]
+    tops, bottoms = [], []
+    for offset in range(sects):
+        for side, value in enumerate(spread(share_refs[offset][...])):
+            rows_ref[pl.ds(offset * plan.share, plan.share), pl.ds(side * width, width)] = value
+        for side, value in enumerate(spread(edge_refs[offset][...])):
+            halo_ref[pl.ds(offset * columns, columns), pl.ds(side * width, width)] = value
+    for tap in range(3):
+        taps = weight(tap)
+        result = jnp.dot(rows_ref[...], taps, preferred_element_type=F32)
+        if tap != 1:
+            halo = jnp.dot(halo_ref[...], taps, preferred_element_type=F32)
+        for offset in range(sects):
+            owner = sect ^ offset
+            for row in range(plan.share_rows):
+                place = owner * plan.share_rows + row
+                image = lax.div(place, MOST_LAND)
+                at = slots_ref[place] + 2 - tap
+                start = (offset * plan.share_rows + row) * columns
+                total_ref[image, at] = total_ref[image, at] + result[start : start + columns]
+            first = owner * plan.share_rows
+            image = lax.div(first, MOST_LAND)
+            top = lax.rem(first, MOST_LAND) == 0
+            bottom = lax.rem(first + plan.share_rows, MOST_LAND) == 0
+            if tap != 1:
+                piece = halo[offset * columns : (offset + 1) * columns]
+                at = 1 if tap == 0 else plan.row_count
+                factor = jnp.where(top if tap == 0 else bottom, 1.0, 0.0)
+                total_ref[image, at] = total_ref[image, at] + piece * factor
+    for image in range(plan.batches):
+        for row in range(plan.row_count):
+            keep = mask_ref[image, row].astype(F32)
+            out_ref[image, row] = (jnp.maximum(total_ref[image, row + 1], 0.0) * keep).astype(BF16)
+
+
+def swap(value, axis, pattern):
+    count = lax.axis_size(axis)
+    return lax.ppermute(value, axis, [(i, i ^ pattern) for i in range(count)])
+
+
+def add_halves(keep, moved):
+    total = (keep.astype(F32) + moved.astype(F32)).astype(BF16)
+    half = total.shape[0] // 2
+    return total[:half], total[half:]
+
+
+def swap_edges(edge, plan):
+    pairs = []
+    for image in range(plan.batches):
+        top = image * MOST_LAND // plan.share_rows
+        bottom = (image * MOST_LAND + MOST_LAND - 1) // plan.share_rows
+        for band in range(plan.bands - 1):
+            upper = band * plan.sects + bottom
+            lower = (band + 1) * plan.sects + top
+            pairs += [(upper, lower), (lower, upper)]
+    return lax.ppermute(edge, ("band", "sect"), pairs)
+
+
+def swap_low_edges(low_level, band, bands):
+    top, bottom = low_level[:, 0], low_level[:, -1]
+    even = band % 2 == 0
+    first_pairs = [(b, b ^ 1) for b in range(bands) if b ^ 1 < bands]
+    second_pairs = []
+    for b in range(1, bands - 1, 2):
+        second_pairs += [(b, b + 1), (b + 1, b)]
+    first = lax.ppermute(jnp.where(even, bottom, top), "band", first_pairs)
+    second = lax.ppermute(jnp.where(even, top, bottom), "band", second_pairs)
+    return first, second
+
+
+def fits(batches, row_count, columns, bands, sects):
+    slots = batches * MOST_LAND
+    return (
+        row_count == ROW_BLOCK
+        and all(dilation % row_count == 0 for dilation in DILATIONS)
+        and sects > 1
+        and sects & (sects - 1) == 0
+        and bands & (bands - 1) == 0
+        and slots % sects == 0
+        and MOST_LAND % (2 * (slots // sects)) == 0
+        and columns % 16 == 0
+        and batches <= 8
+    )
+
+
+def shards(
+    features,
+    low_level,
+    land_mask,
+    weight_one,
+    weight_dilated,
+    bias_branch,
+    weight_pool,
+    bias_pool,
+    weight_project,
+    bias_project,
+    weight_reduce,
+    bias_reduce,
+    weight_merging,
+    bias_merging,
+):
+    batches, row_count, columns, channels = features.shape
+    bands, sects = lax.axis_size("band"), lax.axis_size("sect")
+    plan = Plan(batches, row_count, columns, bands, sects)
+    width = weight_one.shape[1]
+    band, sect = lax.axis_index("band"), lax.axis_index("sect")
+    place = jnp.stack([sect, band, jnp.int32(bands)]).astype(jnp.int32)
+    far_masks = [
+        lax.ppermute(land_mask, "band", [(target, source) for source, target in pairs])
+        for _, _, _, pairs in plan.terms
+    ]
+    far_mask = jnp.stack(far_masks or [land_mask])
+    pieces = branch_partials(
+        plan, place, land_mask, far_mask, features, weight_one, weight_dilated
+    )
+    keep, send = pieces[:2]
+    far_keep, far_send = pieces[2:] if plan.terms else (None, None)
+    pool = call(
+        pool_kernel,
+        jax.ShapeDtypeStruct((8, width), F32),
+        [VMEM, VMEM],
+        [],
+        3 * 16 * channels * width,
+        2 * features.size,
+    )(features, weight_pool)
+    for bit in range(plan.bits):
+        pattern = 1 << bit
+        last = bit == plan.bits - 1
+        if plan.terms:
+            far_moved = swap(far_send, "sect", pattern)
+            if last:
+                far = (far_keep.astype(F32) + far_moved.astype(F32)).astype(BF16)
+            else:
+                far_keep, far_send = add_halves(far_keep, far_moved)
+        moved = swap(send, "sect", pattern)
+        if not last:
+            keep, send = add_halves(keep, moved)
+        pool = pool + swap(pool, "sect", pattern)
+    far_terms = [
+        lax.ppermute(far[:, term * width : (term + 1) * width], "band", pairs)
+        for term, (_, _, _, pairs) in enumerate(plan.terms)
+    ]
+    for bit in reversed(range(bands.bit_length() - 1)):
+        pool = pool + swap(pool, "band", 1 << bit)
+    first, second = swap_low_edges(low_level, band, bands)
+    reduced = weight_reduce.shape[1]
+    low_part = call(
+        low_kernel,
+        jax.ShapeDtypeStruct((batches, row_count, columns, weight_merging.shape[3]), F32),
+        [SMEM] + [VMEM] * 7,
+        [pltpu.VMEM((batches, row_count + 2, columns, 3 * reduced), BF16)],
+        2 * 3 * batches * row_count * columns * 256 * 256,
+        4 * low_level.size,
+    )(
+        place,
+        low_level,
+        first,
+        second,
+        jnp.concatenate([weight_reduce] * 3, axis=1),
+        jnp.concatenate([bias_reduce] * 3)[None],
+        weight_merging[:, :, width:].reshape(3, 3 * reduced, -1),
+        bias_merging[None],
+    )
+    share = jax.ShapeDtypeStruct((plan.share, width), BF16)
+    row = jax.ShapeDtypeStruct((columns, width), BF16)
+    out, edge = call(
+        functools.partial(project_kernel, plan),
+        (share, row),
+        [SMEM, SMEM] + [VMEM] * (7 + len(plan.terms)),
+        [pltpu.SMEM((batches * MOST_LAND,), jnp.int32), pltpu.VMEM((8, width), F32)],
+        2 * plan.share * 4 * width * width,
+        4 * plan.share * 4 * width + 2 * weight_project.size,
+    )(
+        place,
+        land_mask,
+        keep,
+        moved,
+        bias_branch,
+        pool,
+        bias_pool[None],
+        weight_project,
+        bias_project[None],
+        *far_terms,
+    )
+    halo = swap_edges(edge, plan)
+    shares = [out] + [swap(out, "sect", pattern) for pattern in range(1, sects)]
+    halos = [halo] + [swap(halo, "sect", pattern) for pattern in range(1, sects)]
+    live = batches * MOST_LAND * columns
+    return call(
+        functools.partial(merge_kernel, plan),
+        jax.ShapeDtypeStruct(low_part.shape, BF16),
+        [SMEM, SMEM] + [VMEM] * (2 + 2 * sects),
+        [
+            pltpu.SMEM((batches * MOST_LAND,), jnp.int32),
+            pltpu.VMEM((live, 3 * width), BF16),
+            pltpu.VMEM((sects * columns, 3 * width), BF16),
+            pltpu.VMEM((batches, row_count + 2, columns, width), F32),
+        ],
+        2 * 9 * live * width * width,
+        4 * low_part.size + 2 * weight_merging.size + 4 * live * width,
+    )(place, land_mask, low_part, weight_merging, *shares, *halos)
 
 
 def from_behind(value, axis, by):
@@ -78,7 +586,7 @@
     return jax.nn.relu(pre_relu + bias_pool)
 
 
-def shards(
+def general_shards(
     features,
     low_level,
     land_mask,
@@ -180,4 +688,13 @@
         P(),
     )
     out_specs = P("grp", "band", None, None)
-    return jax.shard_map(shards, mesh=mesh, in_specs=in_specs, out_specs=out_specs, check_vma=False)
+
+    def chosen(features, *others):
+        batches, row_count, columns, _ = features.shape
+        sizes = (batches, row_count, columns, mesh.shape["band"], mesh.shape["sect"])
+        body = shards if fits(*sizes) else general_shards
+        return body(features, *others)
+
+    return jax.shard_map(
+        chosen, mesh=mesh, in_specs=in_specs, out_specs=out_specs, check_vma=False
+    )

time: 207 us -> 65.4 us (0.32)
  waiting for transfers between devices: 81.5 us -> 16 us
  matrix products: 36 us -> 0 us
  blocking collectives: 22.9 us -> 0 us
  local copies, waits for them, and re-layouts: 25.2 us -> 4.63 us
  Pallas kernels: 0 us -> 15.2 us
  between operations: 14 us -> 0.23 us
  starting transfers between devices: 22.7 us -> 25.1 us
    ppermute x8 -> x19, waiting for transfers between devices: 65.4 us -> 16 us  [the longest x14 14.3 us: swap(): return lax.ppermute(value, axis, [(i, i ^ pattern) for i in range(count)])]
    dot_general x42 -> x0, matrix products: 36 us -> none  [the longest x27 28.3 us: branch_terms(): jnp.dot(tap_rows, weight_dilated[branch_index, row_tap, col_tap], preferr...]
    reduce_scatter x1 -> x0, waiting for transfers between devices: 16 us -> none  [shards(): lax.psum_scatter(flat_terms, 'sect', scatter_dimension=0, tiled=True)]
    psum x2 -> x0, blocking collectives: 15.6 us -> none  [the longest x1 9.89 us: pool_context(): average = lax.psum(local_sum, 'band') / cell_count]
    pallas_call x0 -> x5, Pallas kernels: none -> 15.2 us  [the longest x1 8.33 us: branch_partials(): call(functools.partial(branch_kernel, plan), tuple(outs), [SMEM, SMEM, SM...]
    slice x2 -> x3, local copies, waits for them, and re-layouts: 13.1 us -> 0.82 us  [the longest x2 0.81 us: add_halves(): return (total[:half], total[half:])]
    unnamed x69 -> x31, local copies, waits for them, and re-layouts: 11.7 us -> 3.81 us
    all_gather x1 -> x0, blocking collectives: 7.34 us -> none  [shards(): lax.all_gather(out_cells, 'sect', axis=0, tiled=True)]
  transfers between devices with their start and end apart: 9 -> 19, of which waited for: 8 -> 9; matrix products, arithmetic and copies ran while one was open for 10% -> 8% of each run, Pallas kernels for 0% -> 4%
where the time goes in v1:
time: 65.4 us; the launch traced here: 64.6 us
  starting transfers between devices  25.1 us (38%)
  waiting for transfers between devices  16 us (24%)
  Pallas kernels  15.2 us (23%)
  local copies, waits for them, and re-layouts  4.63 us (7%)
  other arithmetic  3.41 us (5%)
    ppermute x14, waiting for transfers between devices, swap(): return lax.ppermute(value, axis, [(i, i ^ pattern) for i in range(count)])  14.3 us
    ppermute x14, starting transfers between devices, swap(): return lax.ppermute(value, axis, [(i, i ^ pattern) for i in range(count)])  13.9 us
    pallas_call x1, Pallas kernels, branch_partials(): call(functools.partial(branch_kernel, plan), tuple(outs), [SMEM, SMEM, SM...  8.33 us
    ppermute x1, starting transfers between devices, shards(): lax.ppermute(land_mask, 'band', [(target, source) for source, target in p...  4.04 us
    unnamed x31, local copies, waits for them, and re-layouts  3.81 us
    pallas_call x1, Pallas kernels, shards(): call(functools.partial(merge_kernel, plan), jax.ShapeDtypeStruct(low_part...  3 us
    ppermute x1, starting transfers between devices, swap_low_edges(): first = lax.ppermute(jnp.where(even, bottom, top), 'band', first_pairs)  2.9 us
    ppermute x1, starting transfers between devices, shards(): lax.ppermute(far[:, term * width:(term + 1) * width], 'band', pairs)  2.83 us
  transfers between devices with their start and end apart: 19, of which 9 were waited for; matrix products, arithmetic and copies ran while one was open for 8% of the time, Pallas kernels for 4%

profile of v1, /device:TPU:0, one launch (start us, length us, event | category | flops | bytes accessed | tf_op | source)
XLA Modules:
  0.0 64.6 jit_solution(13914308372651560337)
XLA Ops:
  0.0 4.0 %collective-permute-start.2 = (s32[2,6]{1,0:T(2,128)}, s32[2,6]{1,0:T(2,128)S(1)}, u32[]{:S(2)}, u32[]{:S(2)}) collective-permute-start(s32[2,6]{1,0:T(2,128)} %mask_ref.5), channel_id=1, source_target_pairs={{8,0},{12,4},{0,8},{4,12},{9,1},{13,5},{1,9},{5,13},{10,2},{14,6},... | collective-permute-start | bytes 152 | tf_op jit(solution)/shard_map/ppermute | solution.py:424
  4.0 0.1 pad_add_fusion.place_ref
  4.1 1.7 %collective-permute-done.2 = s32[2,6]{1,0:T(2,128)S(1)} collective-permute-done((s32[2,6]{1,0:T(2,128)}, s32[2,6]{1,0:T(2,128)S(1)}, u32[]{:S(2)}, u32[]{:S(2)}) %collective-permute-start.2) | collective-permute-done | bytes 80 | tf_op jit(solution)/shard_map/ppermute | solution.py:424
  5.8 1.3 %copy-done.1 = bf16[2,6,96,512]{3,2,1,0:T(8,128)(2,1)S(1)} copy-done((bf16[2,6,96,512]{3,2,1,0:T(8,128)(2,1)S(1)}, bf16[2,6,96,512]{3,2,1,0:T(8,128)(2,1)}, u32[]{:S(2)}) %copy-start.1) | copy-done | bytes 1179672
  7.1 0.7 %copy-done.9 = s32[2,6]{1,0:T(2,128)S(1)} copy-done((s32[2,6]{1,0:T(2,128)S(1)}, s32[2,6]{1,0:T(2,128)}, u32[]{:S(2)}) %copy-start.9) | copy-done | bytes 72
  7.7 0.9 %copy-done.14 = bf16[512,256]{1,0:T(8,128)(2,1)S(1)} copy-done((bf16[512,256]{1,0:T(8,128)(2,1)S(1)}, bf16[512,256]{1,0:T(8,128)(2,1)}, u32[]{:S(2)}) %copy-start.14) | copy-done | bytes 262168
  8.7 8.3 %shard_map.137 = (bf16[384,1024]{1,0:T(8,128)(2,1)S(1)}, bf16[384,1024]{1,0:T(8,128)(2,1)S(1)}, bf16[384,256]{1,0:T(8,128)(2,1)S(1)}, bf16[384,256]{1,0:T(8,128)(2,1)S(1)}) custom-call(s32[3]{0:T(128)S(1)} %pad_add_fusion.place_ref, s32[2,6]{1,0:T(2,128)S(1)} %copy-done.9, s32[1,2,6]{2,1,0:T(2,128)S(1)} %bitcast.27, bf16[2,6,96,512]{3,2,1,0:T(8,128)(2,1)S(1)} %copy-done.1, ...), custom_call_target="tpu_custom_call" | custom-call | flops 2617245696 | bytes 4980736 | tf_op jit(solution)/shard_map/pallas_call | solution.py:199
  17.0 0.1 collective-permute-start.3
  17.1 0.5 collective-permute-start.9
  17.6 2.1 %collective-permute-done.9 = bf16[384,256]{1,0:T(8,128)(2,1)S(1)} collective-permute-done((bf16[384,256]{1,0:T(8,128)(2,1)S(1)}, bf16[384,256]{1,0:T(8,128)(2,1)S(1)}, u32[]{:S(2)}, u32[]{:S(2)}) %collective-permute-start.9) | collective-permute-done | bytes 196640 | tf_op jit(solution)/shard_map/ppermute | solution.py:353
  19.7 0.1 add_convert_fusion.1
  19.7 1.9 %collective-permute-start.10 = (bf16[192,256]{1,0:T(8,128)(2,1)S(1)}, bf16[192,256]{1,0:T(8,128)(2,1)S(1)}, u32[]{:S(2)}, u32[]{:S(2)}) collective-permute-start(bf16[192,256]{1,0:T(8,128)(2,1)S(1)} %slice.31), channel_id=1, source_target_pairs={{0,2},{1,3},{2,0},{3,1},{4,6},{5,7},{6,4},{7,5},{8,10},{9,11},{10,... | collective-permute-start | bytes 294920 | tf_op jit(solution)/shard_map/ppermute | solution.py:353
  21.6 0.3 add_convert_fusion
  21.9 0.0 copy-start.4
  22.0 0.0 copy-start.11
  22.0 0.8 %fusion.2 = (bf16[192,1024]{1,0:T(8,128)(2,1)}, bf16[192,1024]{1,0:T(8,128)(2,1)S(1)}) fusion(bf16[384,1024]{1,0:T(8,128)(2,1)S(1)} %add_convert_fusion), kind=kLoop, calls=%fused_computation.10 | loop fusion | bytes 1572864 | tf_op jit(solution)/shard_map/slice | solution.py:359
  22.8 0.2 collective-permute-start.4
  23.0 1.7 %collective-permute-done.10 = bf16[192,256]{1,0:T(8,128)(2,1)S(1)} collective-permute-done((bf16[192,256]{1,0:T(8,128)(2,1)S(1)}, bf16[192,256]{1,0:T(8,128)(2,1)S(1)}, u32[]{:S(2)}, u32[]{:S(2)}) %collective-permute-start.10) | collective-permute-done | bytes 98336 | tf_op jit(solution)/shard_map/ppermute | solution.py:353
  24.7 0.7 %add_convert_fusion.2 = bf16[192,256]{1,0:T(8,128)(2,1)} fusion(bf16[192,256]{1,0:T(8,128)(2,1)S(1)} %collective-permute-done.10, bf16[384,256]{1,0:T(8,128)(2,1)S(1)} %add_convert_fusion.1), kind=kLoop, calls=%fused_computation.2 | loop fusion | flops 196608 | bytes 294912 | tf_op jit(solution)/shard_map/convert_element_type | solution.py:447
  25.4 2.8 %collective-permute-start.11 = (bf16[192,256]{1,0:T(8,128)(2,1)}, bf16[192,256]{1,0:T(8,128)(2,1)S(1)}, u32[]{:S(2)}, u32[]{:S(2)}) collective-permute-start(bf16[192,256]{1,0:T(8,128)(2,1)} %add_convert_fusion.2), channel_id=1, source_target_pairs={{0,8},{4,12},{8,0},{12,4},{1,9},{5,13},{9,1},{13,5},{2,10},{6,14},... | collective-permute-start | bytes 294920 | tf_op jit(solution)/shard_map/ppermute | solution.py:455
  28.2 0.4 shard_map.138
  28.6 0.0 collective-permute-start.5
  28.6 1.2 %collective-permute-done.5 = f32[8,256]{1,0:T(8,128)S(1)} collective-permute-done((f32[8,256]{1,0:T(8,128)S(1)}, f32[8,256]{1,0:T(8,128)S(1)}, u32[]{:S(2)}, u32[]{:S(2)}) %collective-permute-start.5) | collective-permute-done | bytes 8224 | tf_op jit(solution)/shard_map/ppermute | solution.py:353
  29.8 2.0 %collective-permute-start.6 = (f32[8,256]{1,0:T(8,128)S(1)}, f32[8,256]{1,0:T(8,128)S(1)}, u32[]{:S(2)}, u32[]{:S(2)}) collective-permute-start(f32[8,256]{1,0:T(8,128)S(1)} %add.27), channel_id=1, source_target_pairs={{0,2},{1,3},{2,0},{3,1},{4,6},{5,7},{6,4},{7,5},{8,10},{9,11},{10,... | collective-permute-start | bytes 24584 | tf_op jit(solution)/shard_map/ppermute | solution.py:353
  31.8 2.3 %collective-permute-done.6 = f32[8,256]{1,0:T(8,128)S(1)} collective-permute-done((f32[8,256]{1,0:T(8,128)S(1)}, f32[8,256]{1,0:T(8,128)S(1)}, u32[]{:S(2)}, u32[]{:S(2)}) %collective-permute-start.6) | collective-permute-done | bytes 8224 | tf_op jit(solution)/shard_map/ppermute | solution.py:353
  34.1 2.6 %collective-permute-start.7 = (f32[8,256]{1,0:T(8,128)S(1)}, f32[8,256]{1,0:T(8,128)S(1)}, u32[]{:S(2)}, u32[]{:S(2)}) collective-permute-start(f32[8,256]{1,0:T(8,128)S(1)} %add.28), channel_id=1, source_target_pairs={{0,8},{4,12},{8,0},{12,4},{1,9},{5,13},{9,1},{13,5},{2,10},{6,14},... | collective-permute-start | bytes 24584 | tf_op jit(solution)/shard_map/ppermute | solution.py:353
  36.7 2.0 %collective-permute-done.7 = f32[8,256]{1,0:T(8,128)S(1)} collective-permute-done((f32[8,256]{1,0:T(8,128)S(1)}, f32[8,256]{1,0:T(8,128)S(1)}, u32[]{:S(2)}, u32[]{:S(2)}) %collective-permute-start.7) | collective-permute-done | bytes 8224 | tf_op jit(solution)/shard_map/ppermute | solution.py:353
  38.6 0.6 add.29
  39.2 1.6 %collective-permute-start.8 = (f32[8,256]{1,0:T(8,128)}, f32[8,256]{1,0:T(8,128)}, u32[]{:S(2)}, u32[]{:S(2)}) collective-permute-start(f32[8,256]{1,0:T(8,128)} %add.29), channel_id=1, source_target_pairs={{0,4},{4,0},{8,12},{12,8},{1,5},{5,1},{9,13},{13,9},{2,6},{6,2},{1... | collective-permute-start | bytes 24584 | tf_op jit(solution)/shard_map/ppermute | solution.py:353
  40.8 2.4 %collective-permute-done.8 = f32[8,256]{1,0:T(8,128)} collective-permute-done((f32[8,256]{1,0:T(8,128)}, f32[8,256]{1,0:T(8,128)}, u32[]{:S(2)}, u32[]{:S(2)}) %collective-permute-start.8) | collective-permute-done | bytes 8224 | tf_op jit(solution)/shard_map/ppermute | solution.py:353
  43.2 0.7 %add.30.pool_ref = f32[8,256]{1,0:T(8,128)S(1)} add(f32[8,256]{1,0:T(8,128)} %add.29, f32[8,256]{1,0:T(8,128)} %collective-permute-done.8) | non-fusion elementwise | flops 2048 | bytes 24576 | tf_op jit(solution)/shard_map/add | solution.py:459
  44.0 1.5 %shard_map.139 = (bf16[192,256]{1,0:T(8,128)(2,1)S(1)}, bf16[96,256]{1,0:T(8,128)(2,1)}) custom-call(s32[3]{0:T(128)S(1)} %pad_add_fusion.place_ref, s32[2,6]{1,0:T(2,128)S(1)} %copy-done.10, bf16[192,1024]{1,0:T(8,128)(2,1)S(1)} %get-tuple-element.18.keep_ref, bf16[192,1024]{1,0:T(8,128)(2,1)S(1)} %collective-permute-done.4.moved_ref, ...), custom_call_target="tpu_custom_call" | custom-call | flops 100663296 | bytes 1441792 | tf_op jit(solution)/shard_map/pallas_call | solution.py:481
  45.5 0.7 %collective-permute-start.15 = (bf16[96,256]{1,0:T(8,128)(2,1)}, bf16[96,256]{1,0:T(8,128)(2,1)S(1)}, u32[]{:S(2)}, u32[]{:S(2)}) collective-permute-start(bf16[96,256]{1,0:T(8,128)(2,1)} %get-tuple-element.16), channel_id=1, source_target_pairs={{1,4},{4,1},{5,8},{8,5},{9,12},{12,9},{3,6},{6,3},{7,10},{10,7},{1... | collective-permute-start | bytes 147464 | tf_op jit(solution)/shard_map/ppermute | solution.py:371
  46.2 2.9 %collective-permute-start = (bf16[2,96,256]{2,1,0:T(8,128)(2,1)S(1)}, bf16[2,96,256]{2,1,0:T(8,128)(2,1)S(1)}, u32[]{:S(2)}, u32[]{:S(2)}) collective-permute-start(bf16[2,96,256]{2,1,0:T(8,128)(2,1)S(1)} %get-tuple-element.20), channel_id=1, source_target_pairs={{0,4},{4,0},{8,12},{12,8},{1,5},{5,1},{9,13},{13,9},{2,6},{6,2},{1... | collective-permute-start | bytes 294920 | tf_op jit(solution)/shard_map/ppermute | solution.py:381
  49.1 0.8 %collective-permute-start.1 = (bf16[2,96,256]{2,1,0:T(8,128)(2,1)S(1)}, bf16[2,96,256]{2,1,0:T(8,128)(2,1)S(1)}, u32[]{:S(2)}, u32[]{:S(2)}) collective-permute-start(bf16[2,96,256]{2,1,0:T(8,128)(2,1)S(1)} %get-tuple-element.19), channel_id=1, source_target_pairs={{4,8},{8,4},{5,9},{9,5},{6,10},{10,6},{7,11},{11,7},{20,24},{24,20... | collective-permute-start | bytes 294920 | tf_op jit(solution)/shard_map/ppermute | solution.py:382
  49.9 0.9 %copy.17 = bf16[256,48]{1,0:T(8,128)(2,1)S(1)} copy(bf16[256,48]{0,1:T(8,128)(2,1)} %param.24) | data formatting | bytes 49152 | tf_op args[10]
  50.7 1.5 %collective-permute-start.16 = (bf16[96,256]{1,0:T(8,128)(2,1)S(1)}, bf16[96,256]{1,0:T(8,128)(2,1)S(1)}, u32[]{:S(2)}, u32[]{:S(2)}) collective-permute-start(bf16[96,256]{1,0:T(8,128)(2,1)S(1)} %collective-permute-done.15.refs_4_), channel_id=1, source_target_pairs={{0,1},{1,0},{2,3},{3,2},{4,5},{5,4},{6,7},{7,6},{8,9},{9,8},{10,11... | collective-permute-start | bytes 147464 | tf_op jit(solution)/shard_map/ppermute | solution.py:353
  52.2 0.1 pad_maximum_fusion.reduce_ref
  52.3 0.1 collective-permute-start.12
  52.4 1.1 %collective-permute-start.13 = (bf16[192,256]{1,0:T(8,128)(2,1)}, bf16[192,256]{1,0:T(8,128)(2,1)S(1)}, u32[]{:S(2)}, u32[]{:S(2)}) collective-permute-start(bf16[192,256]{1,0:T(8,128)(2,1)} %copy-done.6), channel_id=1, source_target_pairs={{0,2},{1,3},{2,0},{3,1},{4,6},{5,7},{6,4},{7,5},{8,10},{9,11},{10,... | collective-permute-start | bytes 294920 | tf_op jit(solution)/shard_map/ppermute | solution.py:353
  53.5 0.8 %collective-permute-start.14 = (bf16[192,256]{1,0:T(8,128)(2,1)}, bf16[192,256]{1,0:T(8,128)(2,1)S(1)}, u32[]{:S(2)}, u32[]{:S(2)}) collective-permute-start(bf16[192,256]{1,0:T(8,128)(2,1)} %copy-done.6), channel_id=1, source_target_pairs={{0,3},{1,2},{2,1},{3,0},{4,7},{5,6},{6,5},{7,4},{8,11},{9,10},{10,... | collective-permute-start | bytes 294920 | tf_op jit(solution)/shard_map/ppermute | solution.py:353
  54.3 1.0 %collective-permute-start.17 = (bf16[96,256]{1,0:T(8,128)(2,1)S(1)}, bf16[96,256]{1,0:T(8,128)(2,1)S(1)}, u32[]{:S(2)}, u32[]{:S(2)}) collective-permute-start(bf16[96,256]{1,0:T(8,128)(2,1)S(1)} %collective-permute-done.15.refs_4_), channel_id=1, source_target_pairs={{0,2},{1,3},{2,0},{3,1},{4,6},{5,7},{6,4},{7,5},{8,10},{9,11},{10,... | collective-permute-start | bytes 147464 | tf_op jit(solution)/shard_map/ppermute | solution.py:353
  55.3 0.7 %collective-permute-start.18 = (bf16[96,256]{1,0:T(8,128)(2,1)S(1)}, bf16[96,256]{1,0:T(8,128)(2,1)S(1)}, u32[]{:S(2)}, u32[]{:S(2)}) collective-permute-start(bf16[96,256]{1,0:T(8,128)(2,1)S(1)} %collective-permute-done.15.refs_4_), channel_id=1, source_target_pairs={{0,3},{1,2},{2,1},{3,0},{4,7},{5,6},{6,5},{7,4},{8,11},{9,10},{10,... | collective-permute-start | bytes 147464 | tf_op jit(solution)/shard_map/ppermute | solution.py:353
  56.0 0.8 %pad_maximum_fusion.1 = f32[144]{0:T(256)S(1)} fusion(f32[48]{0:T(128)} %param.25), kind=kLoop, calls=%fused_computation.8 | loop fusion | flops 288 | bytes 768 | tf_op jit(solution)/shard_map/concatenate | solution.py:475
  56.9 2.0 %shard_map.136.low_ref = f32[2,6,96,256]{3,2,1,0:T(8,128)S(1)} custom-call(s32[3]{0:T(128)S(1)} %pad_add_fusion.place_ref, bf16[2,6,96,256]{3,2,1,0:T(8,128)(2,1)S(1)} %copy-done.3, bf16[2,96,256]{2,1,0:T(8,128)(2,1)S(1)} %collective-permute-done.first_ref, bf16[2,96,256]{2,1,0:T(8,128)(2,1)S(1)} %collective-permute-done.1.second_ref, ...), custom_call_target="tpu_custom_call" | custom-call | flops 452984832 | bytes 1179648 | tf_op jit(solution)/shard_map/pallas_call | solution.py:462
  58.9 2.6 %collective-permute-done.17.refs_6_ = bf16[96,256]{1,0:T(8,128)(2,1)S(1)} collective-permute-done((bf16[96,256]{1,0:T(8,128)(2,1)S(1)}, bf16[96,256]{1,0:T(8,128)(2,1)S(1)}, u32[]{:S(2)}, u32[]{:S(2)}) %collective-permute-start.17) | collective-permute-done | bytes 49184 | tf_op jit(solution)/shard_map/ppermute | solution.py:353
  61.4 0.1 collective-permute-done.18.refs_7_
  61.6 3.0 %shard_map.140 = bf16[2,6,96,256]{3,2,1,0:T(8,128)(2,1)} custom-call(s32[3]{0:T(128)S(1)} %pad_add_fusion.place_ref, s32[2,6]{1,0:T(2,128)S(1)} %copy-done.10, f32[2,6,96,256]{3,2,1,0:T(8,128)S(1)} %shard_map.136.low_ref, bf16[3,3,304,256]{3,2,1,0:T(8,128)(2,1)S(1)} %copy-done, bf16[192,256]{1,0:T(8,128)(2,1)S(1)} %copy-done.7, ...), custom_call_target="tpu_custom_call" | custom-call | flops 905969664 | bytes 3366912 | tf_op jit(solution)/shard_map/pallas_call | solution.py:504
  (40 shorter events, 0.1 us)
Async XLA Ops:
  0.0 5.8 %collective-permute-start.2 = (s32[2,6]{1,0:T(2,128)}, s32[2,6]{1,0:T(2,128)S(1)}, u32[]{:S(2)}, u32[]{:S(2)}) collective-permute-start(s32[2,6]{1,0:T(2,128)} %mask_ref.5), channel_id=1, source_target_pairs={{8,0},{12,4},{0,8},{4,12},{9,1},{13,5},{1,9},{5,13},{10,2},{14,6},... | collective-permute-start | bytes 152 | tf_op jit(solution)/shard_map/ppermute | solution.py:424
  5.8 1.3 %copy-start.1 = (bf16[2,6,96,512]{3,2,1,0:T(8,128)(2,1)S(1)}, bf16[2,6,96,512]{3,2,1,0:T(8,128)(2,1)}, u32[]{:S(2)}) copy-start(bf16[2,6,96,512]{3,2,1,0:T(8,128)(2,1)} %features_ref.3) | copy-start | bytes 3538948
  7.1 0.7 %copy-start.9 = (s32[2,6]{1,0:T(2,128)S(1)}, s32[2,6]{1,0:T(2,128)}, u32[]{:S(2)}) copy-start(s32[2,6]{1,0:T(2,128)} %mask_ref.5) | copy-start | bytes 148
  7.7 0.9 %copy-start.14 = (bf16[512,256]{1,0:T(8,128)(2,1)S(1)}, bf16[512,256]{1,0:T(8,128)(2,1)}, u32[]{:S(2)}) copy-start(bf16[512,256]{1,0:T(8,128)(2,1)} %one_ref.1) | copy-start | bytes 786436
  17.0 4.6 %collective-permute-start.3 = (bf16[384,1024]{1,0:T(8,128)(2,1)S(1)}, bf16[384,1024]{1,0:T(8,128)(2,1)S(1)}, u32[]{:S(2)}, u32[]{:S(2)}) collective-permute-start(bf16[384,1024]{1,0:T(8,128)(2,1)S(1)} %get-tuple-element.12), channel_id=1, source_target_pairs={{0,1},{1,0},{2,3},{3,2},{4,5},{5,4},{6,7},{7,6},{8,9},{9,8},{10,11... | collective-permute-start | bytes 2359304 | tf_op jit(solution)/shard_map/ppermute | solution.py:353
  17.1 2.6 %collective-permute-start.9 = (bf16[384,256]{1,0:T(8,128)(2,1)S(1)}, bf16[384,256]{1,0:T(8,128)(2,1)S(1)}, u32[]{:S(2)}, u32[]{:S(2)}) collective-permute-start(bf16[384,256]{1,0:T(8,128)(2,1)S(1)} %get-tuple-element.14), channel_id=1, source_target_pairs={{0,1},{1,0},{2,3},{3,2},{4,5},{5,4},{6,7},{7,6},{8,9},{9,8},{10,11... | collective-permute-start | bytes 589832 | tf_op jit(solution)/shard_map/ppermute | solution.py:353
  19.7 5.0 %collective-permute-start.10 = (bf16[192,256]{1,0:T(8,128)(2,1)S(1)}, bf16[192,256]{1,0:T(8,128)(2,1)S(1)}, u32[]{:S(2)}, u32[]{:S(2)}) collective-permute-start(bf16[192,256]{1,0:T(8,128)(2,1)S(1)} %slice.31), channel_id=1, source_target_pairs={{0,2},{1,3},{2,0},{3,1},{4,6},{5,7},{6,4},{7,5},{8,10},{9,11},{10,... | collective-permute-start | bytes 294920 | tf_op jit(solution)/shard_map/ppermute | solution.py:353
  21.6 6.6 %copy-start.2 = (bf16[2,6,96,512]{3,2,1,0:T(8,128)(2,1)S(1)}, bf16[2,6,96,512]{3,2,1,0:T(8,128)(2,1)}, u32[]{:S(2)}) copy-start(bf16[2,6,96,512]{3,2,1,0:T(8,128)(2,1)} %features_ref.3) | copy-start | bytes 3538948
  21.6 6.6 %copy-start.5 = (bf16[512,256]{1,0:T(8,128)(2,1)S(1)}, bf16[512,256]{1,0:T(8,128)(2,1)}, u32[]{:S(2)}) copy-start(bf16[512,256]{1,0:T(8,128)(2,1)} %weight_ref.3) | copy-start | bytes 786436
  21.9 22.0 %copy-start.4 = (bf16[1280,256]{1,0:T(8,128)(2,1)S(1)}, bf16[1280,256]{1,0:T(8,128)(2,1)}, u32[]{:S(2)}) copy-start(bf16[1280,256]{1,0:T(8,128)(2,1)} %weight_ref.4) | copy-start | bytes 1966084
  22.0 22.0 %copy-start.8 = (f32[4,256]{1,0:T(4,128)S(1)}, f32[4,256]{1,0:T(4,128)}, u32[]{:S(2)}) copy-start(f32[4,256]{1,0:T(4,128)} %bias_branch_ref.1) | copy-start | bytes 12292
  22.0 22.0 %copy-start.10 = (s32[2,6]{1,0:T(2,128)S(1)}, s32[2,6]{1,0:T(2,128)}, u32[]{:S(2)}) copy-start(s32[2,6]{1,0:T(2,128)} %mask_ref.5) | copy-start | bytes 148
  22.0 22.0 %copy-start.11 = (f32[256]{0:T(256)S(1)}, f32[256]{0:T(256)}, u32[]{:S(2)}) copy-start(f32[256]{0:T(256)} %param.21) | copy-start | bytes 3076
  22.0 22.0 %copy-start.12 = (f32[256]{0:T(256)S(1)}, f32[256]{0:T(256)}, u32[]{:S(2)}) copy-start(f32[256]{0:T(256)} %param.23) | copy-start | bytes 3076
  22.8 21.1 %collective-permute-start.4 = (bf16[192,1024]{1,0:T(8,128)(2,1)}, bf16[192,1024]{1,0:T(8,128)(2,1)S(1)}, u32[]{:S(2)}, u32[]{:S(2)}) collective-permute-start(bf16[192,1024]{1,0:T(8,128)(2,1)} %get-tuple-element.17), channel_id=1, source_target_pairs={{0,2},{1,3},{2,0},{3,1},{4,6},{5,7},{6,4},{7,5},{8,10},{9,11},{10,... | collective-permute-start | bytes 1179656 | tf_op jit(solution)/shard_map/ppermute | solution.py:353
  25.4 20.7 %copy-start.3 = (bf16[2,6,96,256]{3,2,1,0:T(8,128)(2,1)S(1)}, bf16[2,6,96,256]{3,2,1,0:T(8,128)(2,1)}, u32[]{:S(2)}) copy-start(bf16[2,6,96,256]{3,2,1,0:T(8,128)(2,1)} %low_ref.1) | copy-start | bytes 1769476
  25.4 31.4 %copy-start = (bf16[3,3,304,256]{3,2,1,0:T(8,128)(2,1)S(1)}, bf16[3,3,304,256]{3,2,1,0:T(8,128)(2,1)}, u32[]{:S(2)}) copy-start(bf16[3,3,304,256]{3,2,1,0:T(8,128)(2,1)} %weight_ref.5) | copy-start | bytes 4202500
  25.4 18.5 %collective-permute-start.11 = (bf16[192,256]{1,0:T(8,128)(2,1)}, bf16[192,256]{1,0:T(8,128)(2,1)S(1)}, u32[]{:S(2)}, u32[]{:S(2)}) collective-permute-start(bf16[192,256]{1,0:T(8,128)(2,1)} %add_convert_fusion.2), channel_id=1, source_target_pairs={{0,8},{4,12},{8,0},{12,4},{1,9},{5,13},{9,1},{13,5},{2,10},{6,14},... | collective-permute-start | bytes 294920 | tf_op jit(solution)/shard_map/ppermute | solution.py:455
  28.6 28.3 %copy-start.13 = (f32[256]{0:T(256)S(1)}, f32[256]{0:T(256)}, u32[]{:S(2)}) copy-start(f32[256]{0:T(256)} %param.27) | copy-start | bytes 3076
  28.6 1.2 %collective-permute-start.5 = (f32[8,256]{1,0:T(8,128)S(1)}, f32[8,256]{1,0:T(8,128)S(1)}, u32[]{:S(2)}, u32[]{:S(2)}) collective-permute-start(f32[8,256]{1,0:T(8,128)S(1)} %shard_map.138), channel_id=1, source_target_pairs={{0,1},{1,0},{2,3},{3,2},{4,5},{5,4},{6,7},{7,6},{8,9},{9,8},{10,11... | collective-permute-start | bytes 24584 | tf_op jit(solution)/shard_map/ppermute | solution.py:353
  29.8 4.3 %collective-permute-start.6 = (f32[8,256]{1,0:T(8,128)S(1)}, f32[8,256]{1,0:T(8,128)S(1)}, u32[]{:S(2)}, u32[]{:S(2)}) collective-permute-start(f32[8,256]{1,0:T(8,128)S(1)} %add.27), channel_id=1, source_target_pairs={{0,2},{1,3},{2,0},{3,1},{4,6},{5,7},{6,4},{7,5},{8,10},{9,11},{10,... | collective-permute-start | bytes 24584 | tf_op jit(solution)/shard_map/ppermute | solution.py:353
  34.1 4.5 %collective-permute-start.7 = (f32[8,256]{1,0:T(8,128)S(1)}, f32[8,256]{1,0:T(8,128)S(1)}, u32[]{:S(2)}, u32[]{:S(2)}) collective-permute-start(f32[8,256]{1,0:T(8,128)S(1)} %add.28), channel_id=1, source_target_pairs={{0,8},{4,12},{8,0},{12,4},{1,9},{5,13},{9,1},{13,5},{2,10},{6,14},... | collective-permute-start | bytes 24584 | tf_op jit(solution)/shard_map/ppermute | solution.py:353
  39.2 4.0 %collective-permute-start.8 = (f32[8,256]{1,0:T(8,128)}, f32[8,256]{1,0:T(8,128)}, u32[]{:S(2)}, u32[]{:S(2)}) collective-permute-start(f32[8,256]{1,0:T(8,128)} %add.29), channel_id=1, source_target_pairs={{0,4},{4,0},{8,12},{12,8},{1,5},{5,1},{9,13},{13,9},{2,6},{6,2},{1... | collective-permute-start | bytes 24584 | tf_op jit(solution)/shard_map/ppermute | solution.py:353
  45.5 3.6 %copy-start.6 = (bf16[192,256]{1,0:T(8,128)(2,1)}, bf16[192,256]{1,0:T(8,128)(2,1)S(1)}, u32[]{:S(2)}) copy-start(bf16[192,256]{1,0:T(8,128)(2,1)S(1)} %get-tuple-element.15.refs_0_) | copy-start | bytes 294916
  45.5 5.3 %collective-permute-start.15 = (bf16[96,256]{1,0:T(8,128)(2,1)}, bf16[96,256]{1,0:T(8,128)(2,1)S(1)}, u32[]{:S(2)}, u32[]{:S(2)}) collective-permute-start(bf16[96,256]{1,0:T(8,128)(2,1)} %get-tuple-element.16), channel_id=1, source_target_pairs={{1,4},{4,1},{5,8},{8,5},{9,12},{12,9},{3,6},{6,3},{7,10},{10,7},{1... | collective-permute-start | bytes 147464 | tf_op jit(solution)/shard_map/ppermute | solution.py:371
  46.2 7.3 %collective-permute-start = (bf16[2,96,256]{2,1,0:T(8,128)(2,1)S(1)}, bf16[2,96,256]{2,1,0:T(8,128)(2,1)S(1)}, u32[]{:S(2)}, u32[]{:S(2)}) collective-permute-start(bf16[2,96,256]{2,1,0:T(8,128)(2,1)S(1)} %get-tuple-element.20), channel_id=1, source_target_pairs={{0,4},{4,0},{8,12},{12,8},{1,5},{5,1},{9,13},{13,9},{2,6},{6,2},{1... | collective-permute-start | bytes 294920 | tf_op jit(solution)/shard_map/ppermute | solution.py:381
  49.1 12.5 %copy-start.7 = (bf16[192,256]{1,0:T(8,128)(2,1)S(1)}, bf16[192,256]{1,0:T(8,128)(2,1)}, u32[]{:S(2)}) copy-start(bf16[192,256]{1,0:T(8,128)(2,1)} %copy-done.6) | copy-start | bytes 294916
  49.1 5.2 %collective-permute-start.1 = (bf16[2,96,256]{2,1,0:T(8,128)(2,1)S(1)}, bf16[2,96,256]{2,1,0:T(8,128)(2,1)S(1)}, u32[]{:S(2)}, u32[]{:S(2)}) collective-permute-start(bf16[2,96,256]{2,1,0:T(8,128)(2,1)S(1)} %get-tuple-element.19), channel_id=1, source_target_pairs={{4,8},{8,4},{5,9},{9,5},{6,10},{10,6},{7,11},{11,7},{20,24},{24,20... | collective-permute-start | bytes 294920 | tf_op jit(solution)/shard_map/ppermute | solution.py:382
  50.7 4.6 %collective-permute-start.16 = (bf16[96,256]{1,0:T(8,128)(2,1)S(1)}, bf16[96,256]{1,0:T(8,128)(2,1)S(1)}, u32[]{:S(2)}, u32[]{:S(2)}) collective-permute-start(bf16[96,256]{1,0:T(8,128)(2,1)S(1)} %collective-permute-done.15.refs_4_), channel_id=1, source_target_pairs={{0,1},{1,0},{2,3},{3,2},{4,5},{5,4},{6,7},{7,6},{8,9},{9,8},{10,11... | collective-permute-start | bytes 147464 | tf_op jit(solution)/shard_map/ppermute | solution.py:353
  52.3 9.3 %collective-permute-start.12 = (bf16[192,256]{1,0:T(8,128)(2,1)}, bf16[192,256]{1,0:T(8,128)(2,1)S(1)}, u32[]{:S(2)}, u32[]{:S(2)}) collective-permute-start(bf16[192,256]{1,0:T(8,128)(2,1)} %copy-done.6), channel_id=1, source_target_pairs={{0,1},{1,0},{2,3},{3,2},{4,5},{5,4},{6,7},{7,6},{8,9},{9,8},{10,11... | collective-permute-start | bytes 294920 | tf_op jit(solution)/shard_map/ppermute | solution.py:353
  52.4 9.2 %collective-permute-start.13 = (bf16[192,256]{1,0:T(8,128)(2,1)}, bf16[192,256]{1,0:T(8,128)(2,1)S(1)}, u32[]{:S(2)}, u32[]{:S(2)}) collective-permute-start(bf16[192,256]{1,0:T(8,128)(2,1)} %copy-done.6), channel_id=1, source_target_pairs={{0,2},{1,3},{2,0},{3,1},{4,6},{5,7},{6,4},{7,5},{8,10},{9,11},{10,... | collective-permute-start | bytes 294920 | tf_op jit(solution)/shard_map/ppermute | solution.py:353
  53.5 8.1 %collective-permute-start.14 = (bf16[192,256]{1,0:T(8,128)(2,1)}, bf16[192,256]{1,0:T(8,128)(2,1)S(1)}, u32[]{:S(2)}, u32[]{:S(2)}) collective-permute-start(bf16[192,256]{1,0:T(8,128)(2,1)} %copy-done.6), channel_id=1, source_target_pairs={{0,3},{1,2},{2,1},{3,0},{4,7},{5,6},{6,5},{7,4},{8,11},{9,10},{10,... | collective-permute-start | bytes 294920 | tf_op jit(solution)/shard_map/ppermute | solution.py:353
  54.3 7.2 %collective-permute-start.17 = (bf16[96,256]{1,0:T(8,128)(2,1)S(1)}, bf16[96,256]{1,0:T(8,128)(2,1)S(1)}, u32[]{:S(2)}, u32[]{:S(2)}) collective-permute-start(bf16[96,256]{1,0:T(8,128)(2,1)S(1)} %collective-permute-done.15.refs_4_), channel_id=1, source_target_pairs={{0,2},{1,3},{2,0},{3,1},{4,6},{5,7},{6,4},{7,5},{8,10},{9,11},{10,... | collective-permute-start | bytes 147464 | tf_op jit(solution)/shard_map/ppermute | solution.py:353
  55.3 6.3 %collective-permute-start.18 = (bf16[96,256]{1,0:T(8,128)(2,1)S(1)}, bf16[96,256]{1,0:T(8,128)(2,1)S(1)}, u32[]{:S(2)}, u32[]{:S(2)}) collective-permute-start(bf16[96,256]{1,0:T(8,128)(2,1)S(1)} %collective-permute-done.15.refs_4_), channel_id=1, source_target_pairs={{0,3},{1,2},{2,1},{3,0},{4,7},{5,6},{6,5},{7,4},{8,11},{9,10},{10,... | collective-permute-start | bytes 147464 | tf_op jit(solution)/shard_map/ppermute | solution.py:353

commit v2 on v1

--- a/solution.py
+++ b/solution.py
@@ -12,22 +12,23 @@
 PRECISE = lax.Precision.HIGHEST
 ROW_BLOCK = 6
 MOST_LAND = 4
-VMEM_LIMIT = 50 * 2 ** 20
+VMEM_LIMIT = 32 * 2 ** 20
+WHOLE_VMEM = 60 * 2 ** 20
+EARLY = 2
 F32 = jnp.float32
 BF16 = jnp.bfloat16
 VMEM = pl.BlockSpec(memory_space=pltpu.VMEM)
-SMEM = pl.BlockSpec(memory_space=pltpu.SMEM)
-ANY = pl.BlockSpec(memory_space=pl.ANY)
-
-
-def call(body, outs, in_specs, scratch, flops, bytes_accessed):
+HBM = pl.BlockSpec(memory_space=pltpu.HBM)
+
+
+def call(body, outs, in_specs, scratch, flops, bytes_accessed, limit=VMEM_LIMIT):
     return pl.pallas_call(
         body,
         out_shape=outs,
         in_specs=in_specs,
         out_specs=jax.tree.map(lambda _: VMEM, outs),
         scratch_shapes=scratch,
-        compiler_params=pltpu.CompilerParams(vmem_limit_bytes=VMEM_LIMIT),
+        compiler_params=pltpu.CompilerParams(vmem_limit_bytes=limit),
         cost_estimate=pl.CostEstimate(
             flops=flops, bytes_accessed=bytes_accessed, transcendentals=0
         ),
@@ -55,10 +56,12 @@
             land_before = land_before + live
             sea_before = sea_before + (1 - live)
         base = image * MOST_LAND
-        slots_ref[base] = jnp.int32(0)
-        for slot, value in enumerate(chosen):
-            slots_ref[base + 1 + slot] = value
-        slots_ref[base + MOST_LAND - 1] = jnp.int32(row_count - 1)
+        rows = [jnp.int32(0), *chosen, jnp.int32(row_count - 1)]
+        flags = [(land_total > slot).astype(jnp.int32) for slot in range(MOST_LAND - 2)]
+        flags = [mask_ref[image, 0], *flags, mask_ref[image, row_count - 1]]
+        for slot in range(MOST_LAND):
+            slots_ref[0, base + slot] = rows[slot]
+            slots_ref[1, base + slot] = flags[slot]
 
 
 def split_three(value):
@@ -74,10 +77,13 @@
 
 
 def shifted(value, by, columns):
-    column = lax.broadcasted_iota(jnp.int32, value.shape, 0) % columns
-    moved = pltpu.roll(value, by % value.shape[0], 0)
-    inside = column >= by if by > 0 else column < columns + by
-    return jnp.where(inside, moved, 0.0)
+    blocks = value.reshape(-1, columns, value.shape[1])
+    empty = jnp.zeros((blocks.shape[0], abs(by), value.shape[1]), value.dtype)
+    if by > 0:
+        moved = jnp.concatenate([empty, blocks[:, : columns - by]], axis=1)
+    else:
+        moved = jnp.concatenate([blocks[:, -by:], empty], axis=1)
+    return moved.reshape(value.shape)
 
 
 class Plan:
@@ -100,110 +106,151 @@
                 self.terms.append((branch, hop, 0, up))
                 self.terms.append((branch, hop, 2, down))
 
-    def tap_columns(self, dilation):
-        return [1] + ([0, 2] if dilation < self.columns else [])
-
-
-def branch_kernel(plan, place_ref, mask_ref, far_mask_ref, features_ref, one_ref, dilated_ref, *refs):
+    def rows_of(self, position, sect, slots_ref):
+        owner = sect ^ reversed_bits(position, self.bits)
+        for row in range(self.share_rows):
+            place = owner * self.share_rows + row
+            start = (position * self.share_rows + row) * self.columns
+            yield lax.div(place, MOST_LAND), slots_ref[0, place], start
+
+
+def tap_sum(rows, taps, dilation, columns):
+    width = taps.shape[1] // 3
+    if dilation >= columns:
+        return jnp.dot(rows, taps[:, width : 2 * width], preferred_element_type=F32)
+    result = jnp.dot(rows, taps, preferred_element_type=F32)
+    return (
+        result[:, width : 2 * width]
+        + shifted(result[:, :width], dilation, columns)
+        + shifted(result[:, 2 * width :], -dilation, columns)
+    )
+
+
+def store_halves(keep, send, index, value):
+    half, width = keep.shape[0], value.shape[1]
+    value = value.astype(BF16)
+    keep[:, pl.ds(index * width, width)] = value[:half]
+    send[:, pl.ds(index * width, width)] = value[half:]
+
+
+def early_kernel(plan, mask_ref, features_ref, dilated_ref, keep, send, slots_ref, land_ref, rows_ref, taps_ref, mask_sem, row_sems, tap_sems):
+    columns, width = plan.columns, dilated_ref.shape[4]
+    mask_copy = pltpu.make_async_copy(mask_ref, land_ref, mask_sem)
+    mask_copy.start()
+    branches = range(EARLY - 1, len(DILATIONS))
+    tap_copies = []
+    for index, branch in enumerate(branches):
+        tap_copies.append([])
+        for tap in range(3):
+            copy = pltpu.make_async_copy(
+                dilated_ref.at[branch, 1, tap],
+                taps_ref.at[index, :, pl.ds(tap * width, width)],
+                tap_sems.at[index, tap],
+            )
+            copy.start()
+            tap_copies[-1].append(copy)
+    mask_copy.wait()
+    fill_slots(land_ref, slots_ref, plan.batches, plan.row_count)
+    row_copies = []
+    sect = lax.axis_index("sect")
+    for position in range(plan.sects):
+        for image, row, start in plan.rows_of(position, sect, slots_ref):
+            copy = pltpu.make_async_copy(
+                features_ref.at[image, row],
+                rows_ref.at[pl.ds(start, columns)],
+                row_sems.at[start // columns],
+            )
+            copy.start()
+            row_copies.append(copy)
+    for copy in row_copies:
+        copy.wait()
+    for index, branch in enumerate(branches):
+        for copy in tap_copies[index]:
+            copy.wait()
+        value = tap_sum(rows_ref[...], taps_ref[index], DILATIONS[branch], columns)
+        store_halves(keep, send, index, value)
+
+
+def early_partials(plan, mask, features, weight_dilated):
+    channels, width = weight_dilated.shape[3:]
+    half = plan.sects // 2 * plan.share
+    branches = len(DILATIONS) + 1 - EARLY
+    out = jax.ShapeDtypeStruct((half, branches * width), BF16)
+    slots = plan.batches * MOST_LAND
+    scratch = [
+        pltpu.SMEM((2, slots), jnp.int32),
+        pltpu.SMEM(mask.shape, jnp.int32),
+        pltpu.VMEM((2 * half, channels), BF16),
+        pltpu.VMEM((branches, channels, 3 * width), BF16),
+        pltpu.SemaphoreType.DMA,
+        pltpu.SemaphoreType.DMA((slots,)),
+        pltpu.SemaphoreType.DMA((branches, 3)),
+    ]
+    return call(
+        functools.partial(early_kernel, plan),
+        (out, out),
+        [HBM, HBM, HBM],
+        scratch,
+        2 * 3 * branches * 2 * half * channels * width,
+        2 * (3 * branches * channels * width + 2 * half * channels),
+        WHOLE_VMEM,
+    )(mask, features, weight_dilated)
+
+
+def late_kernel(plan, needed, mask_ref, far_mask_ref, features_ref, one_ref, *refs):
     terms = len(plan.terms)
+    dilated = dict(zip(needed, refs[: len(needed)]))
+    refs = refs[len(needed) :]
     outs = refs[: 2 + (2 if terms else 0)]
-    slots_ref, rows_ref, weights_ref, row_sems, weight_sems = refs[len(outs) :]
-    columns, width = plan.columns, one_ref.shape[1]
-    half = plan.sects // 2 * plan.share
-    sect, band = place_ref[0], place_ref[1]
-
-    def fetch_rows(group, mask):
+    slots_ref, rows_ref = refs[len(outs) :]
+    sect, band = lax.axis_index("sect"), lax.axis_index("band")
+
+    def gather(mask):
         fill_slots(mask, slots_ref, plan.batches, plan.row_count)
-        copies = []
         for position in range(plan.sects):
-            owner = sect ^ reversed_bits(position, plan.bits)
-            for row in range(plan.share_rows):
-                place = owner * plan.share_rows + row
-                image = lax.div(place, MOST_LAND)
-                index = position * plan.share_rows + row
-                copies.append(
-                    pltpu.make_async_copy(
-                        features_ref.at[image, slots_ref[place]],
-                        rows_ref.at[group, pl.ds(index * columns, columns)],
-                        row_sems.at[group, index],
-                    )
-                )
-                copies[-1].start()
-        return copies
-
-    weight_copies = []
-
-    def fetch_weight(source):
-        index = len(weight_copies)
-        copy = pltpu.make_async_copy(source, weights_ref.at[index], weight_sems.at[index])
-        copy.start()
-        weight_copies.append(copy)
-
-    def product(group, index):
-        weight_copies[index].wait()
-        return jnp.dot(rows_ref[group], weights_ref[index], preferred_element_type=F32)
-
-    own_rows = fetch_rows(0, mask_ref)
-    fetch_weight(one_ref)
-    work = [(0, 0, None, [(0, 0)])]
-    for branch, dilation in enumerate(DILATIONS):
-        taps = []
-        for tap in plan.tap_columns(dilation):
-            taps.append((len(weight_copies), (1 - tap) * dilation))
-            fetch_weight(dilated_ref.at[branch, 1, tap])
-        work.append((0, branch + 1, None, taps))
-    term_rows = []
+            for image, row, start in plan.rows_of(position, sect, slots_ref):
+                rows_ref[pl.ds(start, plan.columns)] = features_ref[image, row]
+
+    def taps_of(branch, row_tap):
+        return jnp.concatenate([dilated[branch][row_tap, tap] for tap in range(3)], axis=1)
+
     for term, (branch, hop, row_tap, _) in enumerate(plan.terms):
-        term_rows.append(fetch_rows(term + 1, far_mask_ref.at[term]))
+        gather(far_mask_ref.at[term])
         if row_tap is None:
             row_tap = jnp.where(band + hop < plan.bands, 0, 2)
-        taps = []
-        for tap in plan.tap_columns(DILATIONS[branch]):
-            taps.append((len(weight_copies), (1 - tap) * DILATIONS[branch]))
-            fetch_weight(dilated_ref.at[branch, row_tap, tap])
-        work.append((term + 1, None, term, taps))
-    for copy in own_rows:
-        copy.wait()
-    for group, branch, term, taps in work:
-        if term is not None:
-            for copy in term_rows[term]:
-                copy.wait()
-        total = product(group, taps[0][0])
-        for index, by in taps[1:]:
-            total = total + shifted(product(group, index), by, columns)
-        total = total.astype(BF16)
-        keep, send = outs[:2] if term is None else outs[2:]
-        place = branch if term is None else term
-        keep[:, pl.ds(place * width, width)] = total[:half]
-        send[:, pl.ds(place * width, width)] = total[half:]
-
-
-def branch_partials(plan, place, mask, far_mask, features, weight_one, weight_dilated):
+        taps = taps_of(branch, row_tap)
+        value = tap_sum(rows_ref[...], taps, DILATIONS[branch], plan.columns)
+        store_halves(outs[2], outs[3], term, value)
+    gather(mask_ref)
+    value = jnp.dot(rows_ref[...], one_ref[...], preferred_element_type=F32)
+    store_halves(outs[0], outs[1], 0, value)
+    for branch in range(EARLY - 1):
+        value = tap_sum(rows_ref[...], taps_of(branch, 1), DILATIONS[branch], plan.columns)
+        store_halves(outs[0], outs[1], branch + 1, value)
+
+
+def late_partials(plan, mask, far_mask, features, weight_one, weight_dilated):
     terms = len(plan.terms)
     channels, width = weight_one.shape
     half = plan.sects // 2 * plan.share
-    own = jax.ShapeDtypeStruct((half, 4 * width), BF16)
+    own = jax.ShapeDtypeStruct((half, EARLY * width), BF16)
     outs = [own, own]
     if terms:
         far = jax.ShapeDtypeStruct((half, terms * width), BF16)
         outs += [far, far]
-    weights = 1 + 9 + 3 * terms
-    scratch = [
-        pltpu.SMEM((plan.batches * MOST_LAND,), jnp.int32),
-        pltpu.VMEM((1 + terms, 2 * half, channels), BF16),
-        pltpu.VMEM((weights, channels, width), BF16),
-        pltpu.SemaphoreType.DMA((1 + terms, plan.batches * MOST_LAND)),
-        pltpu.SemaphoreType.DMA((weights,)),
-    ]
-    flops = 2 * weights * 2 * half * channels * width
+    needed = sorted({term[0] for term in plan.terms} | set(range(EARLY - 1)))
+    products = 1 + 3 * (EARLY - 1 + terms)
     return call(
-        functools.partial(branch_kernel, plan),
+        functools.partial(late_kernel, plan, needed),
         tuple(outs),
-        [SMEM, SMEM, SMEM, ANY, ANY, ANY],
-        scratch,
-        flops,
-        2 * (weights * channels * width + (1 + terms) * 2 * half * channels),
-    )(place, mask, far_mask, features, weight_one, weight_dilated)
+        [VMEM] * (4 + len(needed)),
+        [
+            pltpu.SMEM((2, plan.batches * MOST_LAND), jnp.int32),
+            pltpu.VMEM((2 * half, channels), BF16),
+        ],
+        2 * products * 2 * half * channels * width,
+        2 * (9 * len(needed) * channels * width + features.size),
+    )(mask, far_mask, features, weight_one, *[weight_dilated[branch] for branch in needed])
 
 
 def pool_kernel(features_ref, weight_ref, out_ref):
@@ -223,12 +270,12 @@
     out_ref[...] = precise_dot(stacked, weight_ref[...])
 
 
-def low_kernel(place_ref, low_ref, first_ref, second_ref, reduce_ref, bias_reduce_ref, merging_ref, bias_ref, out_ref, framed_ref):
+def low_kernel(plan, low_ref, first_ref, second_ref, reduce_ref, bias_reduce_ref, merging_ref, bias_ref, out_ref, framed_ref):
     batches, row_count, columns, depth = low_ref.shape
-    band, bands = place_ref[1], place_ref[2]
+    band, bands = lax.axis_index("band"), plan.bands
     wide = reduce_ref.shape[1]
     reduced = wide // 3
-    even = band % 2 == 0
+    even = lax.rem(band, 2) == 0
 
     def reduce(rows):
         value = jnp.dot(rows, reduce_ref[...], preferred_element_type=F32) + bias_reduce_ref[...]
@@ -257,19 +304,21 @@
         out_ref[image] = total.reshape(row_count, columns, -1)
 
 
-def project_kernel(plan, place_ref, mask_ref, keep_ref, moved_ref, bias_branch_ref, pool_ref, bias_pool_ref, weight_ref, bias_ref, *refs):
+def project_kernel(plan, mask_ref, keep_ref, moved_ref, early_keep_ref, early_moved_ref, bias_branch_ref, pool_ref, bias_pool_ref, weight_ref, bias_ref, *refs):
     far_refs = refs[: len(plan.terms)]
     out_ref, edge_ref, slots_ref, context_ref = refs[len(plan.terms) :]
     columns, width = plan.columns, weight_ref.shape[1]
-    sect = place_ref[0]
+    sect = lax.axis_index("sect")
     fill_slots(mask_ref, slots_ref, plan.batches, plan.row_count)
     cells = plan.row_count * plan.bands * columns
     pooled = jnp.maximum(pool_ref[...] / cells + bias_pool_ref[...], 0.0)
     context_ref[...] = precise_dot(pooled, weight_ref[4 * width :]) + bias_ref[...]
     total = jnp.zeros((plan.share, width), F32)
     for branch in range(4):
-        lanes = pl.ds(branch * width, width)
-        value = keep_ref[:, lanes].astype(F32) + moved_ref[:, lanes].astype(F32)
+        early = branch >= EARLY
+        kept, added = (early_keep_ref, early_moved_ref) if early else (keep_ref, moved_ref)
+        lanes = pl.ds((branch - EARLY if early else branch) * width, width)
+        value = kept[:, lanes].astype(F32) + added[:, lanes].astype(F32)
         for term, far in zip(plan.terms, far_refs):
             if term[0] + 1 == branch:
                 value = value + far[...].astype(F32)
@@ -280,7 +329,7 @@
     for row in range(plan.share_rows):
         place = sect * plan.share_rows + row
         image = lax.div(place, MOST_LAND)
-        keep = mask_ref[image, slots_ref[place]].astype(F32)
+        keep = slots_ref[1, place].astype(F32)
         value = total[row * columns : (row + 1) * columns] + context_ref[pl.ds(image, 1)]
         out_ref[pl.ds(row * columns, columns)] = (jnp.maximum(value, 0.0) * keep).astype(BF16)
     at_top = lax.rem(sect * plan.share_rows, MOST_LAND) == 0
@@ -294,12 +343,12 @@
         edge_ref[...] = out_ref[pl.ds(plan.share - columns, columns)]
 
 
-def merge_kernel(plan, place_ref, mask_ref, low_ref, weight_ref, *refs):
+def merge_kernel(plan, mask_ref, low_ref, weight_ref, *refs):
     sects, columns = plan.sects, plan.columns
     share_refs, edge_refs = refs[:sects], refs[sects : 2 * sects]
     out_ref, slots_ref, rows_ref, halo_ref, total_ref = refs[2 * sects :]
     width = weight_ref.shape[3]
-    sect = place_ref[0]
+    sect = lax.axis_index("sect")
     fill_slots(mask_ref, slots_ref, plan.batches, plan.row_count)
 
     def spread(value):
@@ -330,7 +379,7 @@
             for row in range(plan.share_rows):
                 place = owner * plan.share_rows + row
                 image = lax.div(place, MOST_LAND)
-                at = slots_ref[place] + 2 - tap
+                at = slots_ref[0, place] + 2 - tap
                 start = (offset * plan.share_rows + row) * columns
                 total_ref[image, at] = total_ref[image, at] + result[start : start + columns]
             first = owner * plan.share_rows
@@ -418,18 +467,11 @@
     bands, sects = lax.axis_size("band"), lax.axis_size("sect")
     plan = Plan(batches, row_count, columns, bands, sects)
     width = weight_one.shape[1]
-    band, sect = lax.axis_index("band"), lax.axis_index("sect")
-    place = jnp.stack([sect, band, jnp.int32(bands)]).astype(jnp.int32)
-    far_masks = [
-        lax.ppermute(land_mask, "band", [(target, source) for source, target in pairs])
-        for _, _, _, pairs in plan.terms
-    ]
-    far_mask = jnp.stack(far_masks or [land_mask])
-    pieces = branch_partials(
-        plan, place, land_mask, far_mask, features, weight_one, weight_dilated
-    )
-    keep, send = pieces[:2]
-    far_keep, far_send = pieces[2:] if plan.terms else (None, None)
+    band = lax.axis_index("band")
+    early_keep, early_send = early_partials(plan, land_mask, features, weight_dilated)
+    early_keep, early_send, later_mask, later_features, later_low = lax.optimization_barrier(
+        (early_keep, early_send, land_mask, features, low_level)
+    )
     pool = call(
         pool_kernel,
         jax.ShapeDtypeStruct((8, width), F32),
@@ -437,7 +479,27 @@
         [],
         3 * 16 * channels * width,
         2 * features.size,
-    )(features, weight_pool)
+    )(later_features, weight_pool)
+    early_moved = swap(early_send, "sect", 1)
+    far_masks = [
+        lax.ppermute(later_mask, "band", [(target, source) for source, target in pairs])
+        for _, _, _, pairs in plan.terms
+    ]
+    pool_bits = list(range(bands.bit_length() - 1))
+    if pool_bits:
+        pool = pool + swap(pool, "band", 1 << pool_bits.pop())
+    far_mask = jnp.stack(far_masks or [land_mask])
+    for bit in range(1, plan.bits):
+        early_keep, early_send = add_halves(early_keep, early_moved)
+        early_moved = swap(early_send, "sect", 1 << bit)
+    for bit in range(1, plan.bits):
+        pool = pool + swap(pool, "sect", 1 << bit)
+    pieces = late_partials(
+        plan, later_mask, far_mask, later_features, weight_one, weight_dilated
+    )
+    keep, send = pieces[:2]
+    far_keep, far_send = pieces[2:] if plan.terms else (None, None)
+    pool = pool + swap(pool, "sect", 1)
     for bit in range(plan.bits):
         pattern = 1 << bit
         last = bit == plan.bits - 1
@@ -450,25 +512,23 @@
         moved = swap(send, "sect", pattern)
         if not last:
             keep, send = add_halves(keep, moved)
-        pool = pool + swap(pool, "sect", pattern)
     far_terms = [
         lax.ppermute(far[:, term * width : (term + 1) * width], "band", pairs)
         for term, (_, _, _, pairs) in enumerate(plan.terms)
     ]
-    for bit in reversed(range(bands.bit_length() - 1)):
+    first, second = swap_low_edges(later_low, band, bands)
+    for bit in reversed(pool_bits):
         pool = pool + swap(pool, "band", 1 << bit)
-    first, second = swap_low_edges(low_level, band, bands)
     reduced = weight_reduce.shape[1]
     low_part = call(
-        low_kernel,
+        functools.partial(low_kernel, plan),
         jax.ShapeDtypeStruct((batches, row_count, columns, weight_merging.shape[3]), F32),
-        [SMEM] + [VMEM] * 7,
+        [VMEM] * 7,
         [pltpu.VMEM((batches, row_count + 2, columns, 3 * reduced), BF16)],
         2 * 3 * batches * row_count * columns * 256 * 256,
         4 * low_level.size,
     )(
-        place,
-        low_level,
+        later_low,
         first,
         second,
         jnp.concatenate([weight_reduce] * 3, axis=1),
@@ -481,15 +541,16 @@
     out, edge = call(
         functools.partial(project_kernel, plan),
         (share, row),
-        [SMEM, SMEM] + [VMEM] * (7 + len(plan.terms)),
-        [pltpu.SMEM((batches * MOST_LAND,), jnp.int32), pltpu.VMEM((8, width), F32)],
+        [VMEM] * (10 + len(plan.terms)),
+        [pltpu.SMEM((2, batches * MOST_LAND), jnp.int32), pltpu.VMEM((8, width), F32)],
         2 * plan.share * 4 * width * width,
         4 * plan.share * 4 * width + 2 * weight_project.size,
     )(
-        place,
         land_mask,
         keep,
         moved,
+        early_keep,
+        early_moved,
         bias_branch,
         pool,
         bias_pool[None],
@@ -504,16 +565,16 @@
     return call(
         functools.partial(merge_kernel, plan),
         jax.ShapeDtypeStruct(low_part.shape, BF16),
-        [SMEM, SMEM] + [VMEM] * (2 + 2 * sects),
+        [VMEM] * (3 + 2 * sects),
         [
-            pltpu.SMEM((batches * MOST_LAND,), jnp.int32),
+            pltpu.SMEM((2, batches * MOST_LAND), jnp.int32),
             pltpu.VMEM((live, 3 * width), BF16),
             pltpu.VMEM((sects * columns, 3 * width), BF16),
             pltpu.VMEM((batches, row_count + 2, columns, width), F32),
         ],
         2 * 9 * live * width * width,
         4 * low_part.size + 2 * weight_merging.size + 4 * live * width,
-    )(place, land_mask, low_part, weight_merging, *shares, *halos)
+    )(land_mask, low_part, weight_merging, *shares, *halos)
 
 
 def from_behind(value, axis, by):

time: 65.4 us -> 59.8 us (0.914)
  Pallas kernels: 15.2 us -> 12.7 us
  waiting for transfers between devices: 16 us -> 14.2 us
  starting transfers between devices: 25.1 us -> 23.4 us
  other arithmetic: 3.41 us -> 4.11 us
    ppermute x1, starting transfers between devices: 2.9 us -> 0.45 us  [swap_low_edges(): first = lax.ppermute(jnp.where(even, bottom, top), 'band', first_pairs)]
    unnamed x31 -> x29, local copies, waits for them, and re-layouts: 3.81 us -> 1.54 us
    pallas_call x3 -> x4, Pallas kernels: 11.8 us -> 9.89 us  [the longest x1 4.98 us: early_partials(): call(functools.partial(early_kernel, plan), (out, out), [HBM, HBM, HBM],...]
    squeeze x0 -> x1, local copies, waits for them, and re-layouts: none -> 1.82 us  [late_partials(): weight_dilated[branch]]
    ppermute x1, waiting for transfers between devices: 1.68 us -> 0.01 us  [shards(): lax.ppermute(later_mask, 'band', [(target, source) for source, target in...]
    ppermute x14 -> x16, starting transfers between devices: 13.9 us -> 14.9 us  [swap(): return lax.ppermute(value, axis, [(i, i ^ pattern) for i in range(count)])]
    concatenate x1, other arithmetic: 0.15 us -> 1.1 us  [shards(): jnp.concatenate([weight_reduce] * 3, axis=1)]
    concatenate x1, other arithmetic: 0.84 us -> 0.08 us  [shards(): jnp.concatenate([bias_reduce] * 3)[None]]
  transfers between devices with their start and end apart: 19 -> 21, of which waited for: 9 -> 9; matrix products, arithmetic and copies ran while one was open for 8% -> 15% of each run, Pallas kernels for 4% -> 5%
where the time goes in v2:
time: 59.8 us; the launch traced here: 59.4 us
  starting transfers between devices  23.4 us (39%)
  waiting for transfers between devices  14.2 us (24%)
  Pallas kernels  12.7 us (21%)
  local copies, waits for them, and re-layouts  4.79 us (8%)
  other arithmetic  4.11 us (7%)
    ppermute x16, starting transfers between devices, swap(): return lax.ppermute(value, axis, [(i, i ^ pattern) for i in range(count)])  14.9 us
    ppermute x16, waiting for transfers between devices, swap(): return lax.ppermute(value, axis, [(i, i ^ pattern) for i in range(count)])  14.2 us
    pallas_call x1, Pallas kernels, early_partials(): call(functools.partial(early_kernel, plan), (out, out), [HBM, HBM, HBM],...  4.98 us
    ppermute x1, starting transfers between devices, shards(): lax.ppermute(later_mask, 'band', [(target, source) for source, target in...  4.1 us
    ppermute x1, starting transfers between devices, shards(): lax.ppermute(far[:, term * width:(term + 1) * width], 'band', pairs)  2.59 us
    pallas_call x1, Pallas kernels, late_partials(): call(functools.partial(late_kernel, plan, needed), tuple(outs), [VMEM] *...  2.49 us
    pallas_call x1, Pallas kernels, shards(): call(functools.partial(merge_kernel, plan), jax.ShapeDtypeStruct(low_part...  2.4 us
    squeeze x1, local copies, waits for them, and re-layouts, late_partials(): weight_dilated[branch]  1.82 us
  transfers between devices with their start and end apart: 21, of which 9 were waited for; matrix products, arithmetic and copies ran while one was open for 15% of the time, Pallas kernels for 5%

profile of v2, /device:TPU:0, one launch (start us, length us, event | category | flops | bytes accessed | tf_op | source)
XLA Modules:
  0.0 59.4 jit_solution(712011712624798838)
XLA Ops:
  0.0 5.0 %shard_map.136 = (bf16[384,512]{1,0:T(8,128)(2,1)}, bf16[384,512]{1,0:T(8,128)(2,1)}) custom-call(s32[2,6]{1,0:T(2,128)} %mask_ref.6, bf16[2,6,96,512]{3,2,1,0:T(8,128)(2,1)} %features_ref.3, bf16[3,3,3,512,256]{4,3,2,1,0:T(8,128)(2,1)} %dilated_ref.1), custom_call_target="tpu_custom_call" | custom-call | flops 1207959552 | bytes 2359296 | tf_op jit(solution)/shard_map/pallas_call | solution.py:189
  5.0 0.0 copy-start
  5.0 0.0 copy-start.10
  5.0 4.1 %collective-permute-start.2 = (s32[2,6]{1,0:T(2,128)S(1)}, s32[2,6]{1,0:T(2,128)S(1)}, u32[]{:S(2)}, u32[]{:S(2)}) collective-permute-start(s32[2,6]{1,0:T(2,128)S(1)} %copy-done.5), channel_id=1, source_target_pairs={{8,0},{12,4},{0,8},{4,12},{9,1},{13,5},{1,9},{5,13},{10,2},{14,6},... | collective-permute-start | bytes 152 | tf_op jit(solution)/shard_map/ppermute | solution.py:485
  9.1 1.8 %slice_bitcast_fusion.refs_0_ = bf16[3,3,512,256]{3,2,1,0:T(8,128)(2,1)S(1)} fusion(bf16[3,3,3,512,256]{4,3,2,1,0:T(8,128)(2,1)} %dilated_ref.1), kind=kLoop, calls=%fused_computation | loop fusion | bytes 4718592 | tf_op jit(solution)/shard_map/squeeze | solution.py:253
  11.0 2.5 %shard_map.138 = (bf16[384,512]{1,0:T(8,128)(2,1)S(1)}, bf16[384,512]{1,0:T(8,128)(2,1)}, bf16[384,256]{1,0:T(8,128)(2,1)S(1)}, bf16[384,256]{1,0:T(8,128)(2,1)S(1)}) custom-call(s32[2,6]{1,0:T(2,128)S(1)} %copy-done.5, s32[1,2,6]{2,1,0:T(2,128)S(1)} %bitcast.17, bf16[2,6,96,512]{3,2,1,0:T(8,128)(2,1)S(1)} %copy-done, bf16[512,256]{1,0:T(8,128)(2,1)S(1)} %copy-done.10, ...), custom_call_target="tpu_custom_call" | custom-call | flops 1409286144 | bytes 3538944 | tf_op jit(solution)/shard_map/pallas_call | solution.py:243
  13.5 0.5 collective-permute-start.5
  14.0 0.9 %collective-permute-done.11 = bf16[384,256]{1,0:T(8,128)(2,1)S(1)} collective-permute-done((bf16[384,256]{1,0:T(8,128)(2,1)S(1)}, bf16[384,256]{1,0:T(8,128)(2,1)S(1)}, u32[]{:S(2)}, u32[]{:S(2)}) %collective-permute-start.11) | collective-permute-done | bytes 196640 | tf_op jit(solution)/shard_map/ppermute | solution.py:402
  15.0 1.6 %collective-permute-start.12 = (bf16[192,256]{1,0:T(8,128)(2,1)S(1)}, bf16[192,256]{1,0:T(8,128)(2,1)S(1)}, u32[]{:S(2)}, u32[]{:S(2)}) collective-permute-start(bf16[192,256]{1,0:T(8,128)(2,1)S(1)} %slice.47), channel_id=1, source_target_pairs={{0,2},{1,3},{2,0},{3,1},{4,6},{5,7},{6,4},{7,5},{8,10},{9,11},{10,... | collective-permute-start | bytes 294920 | tf_op jit(solution)/shard_map/ppermute | solution.py:402
  16.6 0.4 shard_map.139
  17.0 2.6 %collective-permute-start.7 = (f32[8,256]{1,0:T(8,128)S(1)}, f32[8,256]{1,0:T(8,128)S(1)}, u32[]{:S(2)}, u32[]{:S(2)}) collective-permute-start(f32[8,256]{1,0:T(8,128)S(1)} %shard_map.139), channel_id=1, source_target_pairs={{0,8},{4,12},{8,0},{12,4},{1,9},{5,13},{9,1},{13,5},{2,10},{6,14},... | collective-permute-start | bytes 24584 | tf_op jit(solution)/shard_map/ppermute | solution.py:402
  19.6 2.0 %collective-permute-done.7 = f32[8,256]{1,0:T(8,128)S(1)} collective-permute-done((f32[8,256]{1,0:T(8,128)S(1)}, f32[8,256]{1,0:T(8,128)S(1)}, u32[]{:S(2)}, u32[]{:S(2)}) %collective-permute-start.7) | collective-permute-done | bytes 8224 | tf_op jit(solution)/shard_map/ppermute | solution.py:402
  21.6 0.5 collective-permute-start.8
  22.1 3.1 %collective-permute-done.8 = f32[8,256]{1,0:T(8,128)S(1)} collective-permute-done((f32[8,256]{1,0:T(8,128)S(1)}, f32[8,256]{1,0:T(8,128)S(1)}, u32[]{:S(2)}, u32[]{:S(2)}) %collective-permute-start.8) | collective-permute-done | bytes 8224 | tf_op jit(solution)/shard_map/ppermute | solution.py:402
  25.2 0.5 collective-permute-start.3
  25.7 0.7 %collective-permute-done.9 = f32[8,256]{1,0:T(8,128)S(1)} collective-permute-done((f32[8,256]{1,0:T(8,128)S(1)}, f32[8,256]{1,0:T(8,128)S(1)}, u32[]{:S(2)}, u32[]{:S(2)}) %collective-permute-start.9) | collective-permute-done | bytes 8224 | tf_op jit(solution)/shard_map/ppermute | solution.py:402
  26.4 0.6 add.33
  27.0 1.6 %collective-permute-start.10 = (f32[8,256]{1,0:T(8,128)}, f32[8,256]{1,0:T(8,128)}, u32[]{:S(2)}, u32[]{:S(2)}) collective-permute-start(f32[8,256]{1,0:T(8,128)} %add.33), channel_id=1, source_target_pairs={{0,4},{4,0},{8,12},{12,8},{1,5},{5,1},{9,13},{13,9},{2,6},{6,2},{1... | collective-permute-start | bytes 24584 | tf_op jit(solution)/shard_map/ppermute | solution.py:402
  28.6 0.7 %add_convert_fusion.3 = bf16[192,256]{1,0:T(8,128)(2,1)} fusion(bf16[192,256]{1,0:T(8,128)(2,1)S(1)} %collective-permute-done.12, bf16[384,256]{1,0:T(8,128)(2,1)S(1)} %add_convert_fusion.2), kind=kLoop, calls=%fused_computation.4 | loop fusion | flops 196608 | bytes 294912 | tf_op jit(solution)/shard_map/convert_element_type | solution.py:509
  29.3 2.6 %collective-permute-start.13 = (bf16[192,256]{1,0:T(8,128)(2,1)}, bf16[192,256]{1,0:T(8,128)(2,1)S(1)}, u32[]{:S(2)}, u32[]{:S(2)}) collective-permute-start(bf16[192,256]{1,0:T(8,128)(2,1)} %add_convert_fusion.3), channel_id=1, source_target_pairs={{0,8},{4,12},{8,0},{12,4},{1,9},{5,13},{9,1},{13,5},{2,10},{6,14},... | collective-permute-start | bytes 294920 | tf_op jit(solution)/shard_map/ppermute | solution.py:516
  31.9 0.1 add_convert_fusion
  32.0 0.7 %fusion = (bf16[192,512]{1,0:T(8,128)(2,1)}, bf16[192,512]{1,0:T(8,128)(2,1)S(1)}) fusion(bf16[384,512]{1,0:T(8,128)(2,1)S(1)} %add_convert_fusion), kind=kLoop, calls=%fused_computation.9 | loop fusion | bytes 786432 | tf_op jit(solution)/shard_map/slice | solution.py:408
  32.7 0.5 collective-permute-start.6
  33.3 0.1 add_convert_fusion.1
  33.4 0.7 %fusion.1 = (bf16[192,512]{1,0:T(8,128)(2,1)}, bf16[192,512]{1,0:T(8,128)(2,1)S(1)}) fusion(bf16[384,512]{1,0:T(8,128)(2,1)S(1)} %add_convert_fusion.1), kind=kLoop, calls=%fused_computation.10 | loop fusion | bytes 786432 | tf_op jit(solution)/shard_map/slice | solution.py:408
  34.1 1.5 %collective-permute-start.4 = (bf16[192,512]{1,0:T(8,128)(2,1)}, bf16[192,512]{1,0:T(8,128)(2,1)S(1)}, u32[]{:S(2)}, u32[]{:S(2)}) collective-permute-start(bf16[192,512]{1,0:T(8,128)(2,1)} %get-tuple-element.35), channel_id=1, source_target_pairs={{0,2},{1,3},{2,0},{3,1},{4,6},{5,7},{6,4},{7,5},{8,10},{9,11},{10,... | collective-permute-start | bytes 589832 | tf_op jit(solution)/shard_map/ppermute | solution.py:402
  35.6 0.7 %select_bitcast_fusion = (bf16[2,96,256]{2,1,0:T(8,128)(2,1)}, bf16[2,96,256]{2,1,0:T(8,128)(2,1)}) fusion(pred[]{:T(512)S(6)} %eq.5, bf16[2,6,96,256]{3,2,1,0:T(8,128)(2,1)S(1)} %copy-done.2), kind=kLoop, calls=%fused_computation.6 | loop fusion | flops 98304 | bytes 393217 | tf_op jit(solution)/shard_map/jit(_where)/select_n | solution.py:431
  36.3 0.4 collective-permute-start
  36.7 1.5 %copy.17 = bf16[256,48]{1,0:T(8,128)(2,1)} copy(bf16[256,48]{0,1:T(8,128)(2,1)} %param.24) | data formatting | bytes 49152 | tf_op args[10]
  38.2 0.7 %collective-permute-start.1 = (bf16[2,96,256]{2,1,0:T(8,128)(2,1)}, bf16[2,96,256]{2,1,0:T(8,128)(2,1)S(1)}, u32[]{:S(2)}, u32[]{:S(2)}) collective-permute-start(bf16[2,96,256]{2,1,0:T(8,128)(2,1)} %get-tuple-element.31), channel_id=1, source_target_pairs={{4,8},{8,4},{5,9},{9,5},{6,10},{10,6},{7,11},{11,7},{20,24},{24,20... | collective-permute-start | bytes 294920 | tf_op jit(solution)/shard_map/ppermute | solution.py:431
  38.9 0.7 %add.34.pool_ref = f32[8,256]{1,0:T(8,128)S(1)} add(f32[8,256]{1,0:T(8,128)} %add.33, f32[8,256]{1,0:T(8,128)} %collective-permute-done.10) | non-fusion elementwise | flops 2048 | bytes 24576 | tf_op jit(solution)/shard_map/add | solution.py:521
  39.6 1.3 %collective-permute-done.6.early_moved_ref = bf16[192,512]{1,0:T(8,128)(2,1)} collective-permute-done((bf16[192,512]{1,0:T(8,128)(2,1)}, bf16[192,512]{1,0:T(8,128)(2,1)}, u32[]{:S(2)}, u32[]{:S(2)}) %collective-permute-start.6) | collective-permute-done | bytes 196640 | tf_op jit(solution)/shard_map/ppermute | solution.py:402
  40.9 2.7 %collective-permute-done.4.moved_ref = bf16[192,512]{1,0:T(8,128)(2,1)S(1)} collective-permute-done((bf16[192,512]{1,0:T(8,128)(2,1)}, bf16[192,512]{1,0:T(8,128)(2,1)S(1)}, u32[]{:S(2)}, u32[]{:S(2)}) %collective-permute-start.4) | collective-permute-done | bytes 196640 | tf_op jit(solution)/shard_map/ppermute | solution.py:402
  43.6 1.3 %shard_map.140 = (bf16[192,256]{1,0:T(8,128)(2,1)S(1)}, bf16[96,256]{1,0:T(8,128)(2,1)S(1)}) custom-call(s32[2,6]{1,0:T(2,128)S(1)} %copy-done.5, bf16[192,512]{1,0:T(8,128)(2,1)S(1)} %get-tuple-element.36.keep_ref, bf16[192,512]{1,0:T(8,128)(2,1)S(1)} %collective-permute-done.4.moved_ref, bf16[192,512]{1,0:T(8,128)(2,1)S(1)} %get-tuple-element.34.early_keep_ref, ...), custom_call_target="tpu_custom_call" | custom-call | flops 100663296 | bytes 1441792 | tf_op jit(solution)/shard_map/pallas_call | solution.py:541
  44.8 0.7 %collective-permute-start.17 = (bf16[96,256]{1,0:T(8,128)(2,1)S(1)}, bf16[96,256]{1,0:T(8,128)(2,1)S(1)}, u32[]{:S(2)}, u32[]{:S(2)}) collective-permute-start(bf16[96,256]{1,0:T(8,128)(2,1)S(1)} %get-tuple-element.30), channel_id=1, source_target_pairs={{1,4},{4,1},{5,8},{8,5},{9,12},{12,9},{3,6},{6,3},{7,10},{10,7},{1... | collective-permute-start | bytes 147464 | tf_op jit(solution)/shard_map/ppermute | solution.py:420
  45.5 1.9 %collective-permute-start.14 = (bf16[192,256]{1,0:T(8,128)(2,1)S(1)}, bf16[192,256]{1,0:T(8,128)(2,1)S(1)}, u32[]{:S(2)}, u32[]{:S(2)}) collective-permute-start(bf16[192,256]{1,0:T(8,128)(2,1)S(1)} %get-tuple-element.29.refs_0_), channel_id=1, source_target_pairs={{0,1},{1,0},{2,3},{3,2},{4,5},{5,4},{6,7},{7,6},{8,9},{9,8},{10,11... | collective-permute-start | bytes 294920 | tf_op jit(solution)/shard_map/ppermute | solution.py:402
  47.4 1.1 %pad_maximum_fusion.reduce_ref = bf16[256,144]{1,0:T(8,128)(2,1)S(1)} fusion(bf16[256,48]{1,0:T(8,128)(2,1)} %copy.17), kind=kLoop, calls=%fused_computation.5 | loop fusion | flops 221184 | bytes 98304 | tf_op jit(solution)/shard_map/concatenate | solution.py:534
  48.5 0.6 %collective-permute-start.15 = (bf16[192,256]{1,0:T(8,128)(2,1)S(1)}, bf16[192,256]{1,0:T(8,128)(2,1)S(1)}, u32[]{:S(2)}, u32[]{:S(2)}) collective-permute-start(bf16[192,256]{1,0:T(8,128)(2,1)S(1)} %get-tuple-element.29.refs_0_), channel_id=1, source_target_pairs={{0,2},{1,3},{2,0},{3,1},{4,6},{5,7},{6,4},{7,5},{8,10},{9,11},{10,... | collective-permute-start | bytes 294920 | tf_op jit(solution)/shard_map/ppermute | solution.py:402
  49.1 0.8 %collective-permute-start.16 = (bf16[192,256]{1,0:T(8,128)(2,1)S(1)}, bf16[192,256]{1,0:T(8,128)(2,1)S(1)}, u32[]{:S(2)}, u32[]{:S(2)}) collective-permute-start(bf16[192,256]{1,0:T(8,128)(2,1)S(1)} %get-tuple-element.29.refs_0_), channel_id=1, source_target_pairs={{0,3},{1,2},{2,1},{3,0},{4,7},{5,6},{6,5},{7,4},{8,11},{9,10},{10,... | collective-permute-start | bytes 294920 | tf_op jit(solution)/shard_map/ppermute | solution.py:402
  49.9 0.8 %collective-permute-start.18 = (bf16[96,256]{1,0:T(8,128)(2,1)S(1)}, bf16[96,256]{1,0:T(8,128)(2,1)S(1)}, u32[]{:S(2)}, u32[]{:S(2)}) collective-permute-start(bf16[96,256]{1,0:T(8,128)(2,1)S(1)} %collective-permute-done.17.refs_4_), channel_id=1, source_target_pairs={{0,1},{1,0},{2,3},{3,2},{4,5},{5,4},{6,7},{7,6},{8,9},{9,8},{10,11... | collective-permute-start | bytes 147464 | tf_op jit(solution)/shard_map/ppermute | solution.py:402
  50.7 0.5 collective-permute-start.19
  51.3 0.9 %collective-permute-start.20 = (bf16[96,256]{1,0:T(8,128)(2,1)S(1)}, bf16[96,256]{1,0:T(8,128)(2,1)S(1)}, u32[]{:S(2)}, u32[]{:S(2)}) collective-permute-start(bf16[96,256]{1,0:T(8,128)(2,1)S(1)} %collective-permute-done.17.refs_4_), channel_id=1, source_target_pairs={{0,3},{1,2},{2,1},{3,0},{4,7},{5,6},{6,5},{7,4},{8,11},{9,10},{10,... | collective-permute-start | bytes 147464 | tf_op jit(solution)/shard_map/ppermute | solution.py:402
  52.1 0.1 pad_maximum_fusion.1
  52.3 1.2 %shard_map.137.low_ref = f32[2,6,96,256]{3,2,1,0:T(8,128)S(1)} custom-call(bf16[2,6,96,256]{3,2,1,0:T(8,128)(2,1)S(1)} %copy-done.2, bf16[2,96,256]{2,1,0:T(8,128)(2,1)S(1)} %collective-permute-done.first_ref, bf16[2,96,256]{2,1,0:T(8,128)(2,1)S(1)} %collective-permute-done.1.second_ref, bf16[256,144]{1,0:T(8,128)(2,1)S(1)} %pad_maximum_fusion.reduce_ref, ...), custom_call_target="tpu_custom_call" | custom-call | flops 452984832 | bytes 1179648 | tf_op jit(solution)/shard_map/pallas_call | solution.py:523
  53.4 0.8 %collective-permute-done.15.refs_2_ = bf16[192,256]{1,0:T(8,128)(2,1)S(1)} collective-permute-done((bf16[192,256]{1,0:T(8,128)(2,1)S(1)}, bf16[192,256]{1,0:T(8,128)(2,1)S(1)}, u32[]{:S(2)}, u32[]{:S(2)}) %collective-permute-start.15) | collective-permute-done | bytes 98336 | tf_op jit(solution)/shard_map/ppermute | solution.py:402
  54.2 0.2 collective-permute-done.16.refs_3_
  54.4 2.5 %collective-permute-done.19.refs_6_ = bf16[96,256]{1,0:T(8,128)(2,1)S(1)} collective-permute-done((bf16[96,256]{1,0:T(8,128)(2,1)S(1)}, bf16[96,256]{1,0:T(8,128)(2,1)S(1)}, u32[]{:S(2)}, u32[]{:S(2)}) %collective-permute-start.19) | collective-permute-done | bytes 49184 | tf_op jit(solution)/shard_map/ppermute | solution.py:402
  57.0 2.4 %shard_map.141 = bf16[2,6,96,256]{3,2,1,0:T(8,128)(2,1)} custom-call(s32[2,6]{1,0:T(2,128)S(1)} %copy-done.5, f32[2,6,96,256]{3,2,1,0:T(8,128)S(1)} %shard_map.137.low_ref, bf16[3,3,304,256]{3,2,1,0:T(8,128)(2,1)S(1)} %copy-done.1, bf16[192,256]{1,0:T(8,128)(2,1)S(1)} %get-tuple-element.29.refs_0_, bf16[192,256]{1,0:T(8,128)(2,1)S(1)} %collective-permute-done.14.refs_1_, ...), custom_call_target="tpu_custom_call" | custom-call | flops 905969664 | bytes 3366912 | tf_op jit(solution)/shard_map/pallas_call | solution.py:565
  (45 shorter events, 0.2 us)
Async XLA Ops:
  0.0 5.0 %copy-start.5 = (s32[2,6]{1,0:T(2,128)S(1)}, s32[2,6]{1,0:T(2,128)}, u32[]{:S(2)}) copy-start(s32[2,6]{1,0:T(2,128)} %mask_ref.6) | copy-start | bytes 148
  5.0 6.0 %copy-start = (bf16[2,6,96,512]{3,2,1,0:T(8,128)(2,1)S(1)}, bf16[2,6,96,512]{3,2,1,0:T(8,128)(2,1)}, u32[]{:S(2)}) copy-start(bf16[2,6,96,512]{3,2,1,0:T(8,128)(2,1)} %features_ref.3) | copy-start | bytes 3538948
  5.0 6.0 %copy-start.10 = (bf16[512,256]{1,0:T(8,128)(2,1)S(1)}, bf16[512,256]{1,0:T(8,128)(2,1)}, u32[]{:S(2)}) copy-start(bf16[512,256]{1,0:T(8,128)(2,1)} %one_ref.1) | copy-start | bytes 786436
  5.0 5.9 %collective-permute-start.2 = (s32[2,6]{1,0:T(2,128)S(1)}, s32[2,6]{1,0:T(2,128)S(1)}, u32[]{:S(2)}, u32[]{:S(2)}) collective-permute-start(s32[2,6]{1,0:T(2,128)S(1)} %copy-done.5), channel_id=1, source_target_pairs={{8,0},{12,4},{0,8},{4,12},{9,1},{13,5},{1,9},{5,13},{10,2},{14,6},... | collective-permute-start | bytes 152 | tf_op jit(solution)/shard_map/ppermute | solution.py:485
  11.0 2.5 %copy-start.12 = (bf16[384,512]{1,0:T(8,128)(2,1)S(1)}, bf16[384,512]{1,0:T(8,128)(2,1)}, u32[]{:S(2)}) copy-start(bf16[384,512]{1,0:T(8,128)(2,1)} %get-tuple-element.26) | copy-start | bytes 1179652
  11.0 5.6 %copy-start.4 = (bf16[512,256]{1,0:T(8,128)(2,1)S(1)}, bf16[512,256]{1,0:T(8,128)(2,1)}, u32[]{:S(2)}) copy-start(bf16[512,256]{1,0:T(8,128)(2,1)} %weight_ref.3) | copy-start | bytes 786436
  13.5 18.4 %copy-start.11 = (bf16[384,512]{1,0:T(8,128)(2,1)S(1)}, bf16[384,512]{1,0:T(8,128)(2,1)}, u32[]{:S(2)}) copy-start(bf16[384,512]{1,0:T(8,128)(2,1)} %get-tuple-element.25) | copy-start | bytes 1179652
  13.5 1.4 %collective-permute-start.11 = (bf16[384,256]{1,0:T(8,128)(2,1)S(1)}, bf16[384,256]{1,0:T(8,128)(2,1)S(1)}, u32[]{:S(2)}, u32[]{:S(2)}) collective-permute-start(bf16[384,256]{1,0:T(8,128)(2,1)S(1)} %get-tuple-element.28), channel_id=1, source_target_pairs={{0,1},{1,0},{2,3},{3,2},{4,5},{5,4},{6,7},{7,6},{8,9},{9,8},{10,11... | collective-permute-start | bytes 589832 | tf_op jit(solution)/shard_map/ppermute | solution.py:402
  13.5 18.4 %collective-permute-start.5 = (bf16[384,512]{1,0:T(8,128)(2,1)S(1)}, bf16[384,512]{1,0:T(8,128)(2,1)S(1)}, u32[]{:S(2)}, u32[]{:S(2)}) collective-permute-start(bf16[384,512]{1,0:T(8,128)(2,1)S(1)} %copy-done.12), channel_id=1, source_target_pairs={{0,1},{1,0},{2,3},{3,2},{4,5},{5,4},{6,7},{7,6},{8,9},{9,8},{10,11... | collective-permute-start | bytes 1179656 | tf_op jit(solution)/shard_map/ppermute | solution.py:402
  15.0 13.6 %collective-permute-start.12 = (bf16[192,256]{1,0:T(8,128)(2,1)S(1)}, bf16[192,256]{1,0:T(8,128)(2,1)S(1)}, u32[]{:S(2)}, u32[]{:S(2)}) collective-permute-start(bf16[192,256]{1,0:T(8,128)(2,1)S(1)} %slice.47), channel_id=1, source_target_pairs={{0,2},{1,3},{2,0},{3,1},{4,6},{5,7},{6,4},{7,5},{8,10},{9,11},{10,... | collective-permute-start | bytes 294920 | tf_op jit(solution)/shard_map/ppermute | solution.py:402
  17.0 18.6 %copy-start.2 = (bf16[2,6,96,256]{3,2,1,0:T(8,128)(2,1)S(1)}, bf16[2,6,96,256]{3,2,1,0:T(8,128)(2,1)}, u32[]{:S(2)}) copy-start(bf16[2,6,96,256]{3,2,1,0:T(8,128)(2,1)} %low_ref) | copy-start | bytes 1769476
  17.0 4.6 %collective-permute-start.7 = (f32[8,256]{1,0:T(8,128)S(1)}, f32[8,256]{1,0:T(8,128)S(1)}, u32[]{:S(2)}, u32[]{:S(2)}) collective-permute-start(f32[8,256]{1,0:T(8,128)S(1)} %shard_map.139), channel_id=1, source_target_pairs={{0,8},{4,12},{8,0},{12,4},{1,9},{5,13},{9,1},{13,5},{2,10},{6,14},... | collective-permute-start | bytes 24584 | tf_op jit(solution)/shard_map/ppermute | solution.py:402
  21.6 3.7 %collective-permute-start.8 = (f32[8,256]{1,0:T(8,128)S(1)}, f32[8,256]{1,0:T(8,128)S(1)}, u32[]{:S(2)}, u32[]{:S(2)}) collective-permute-start(f32[8,256]{1,0:T(8,128)S(1)} %add.31), channel_id=1, source_target_pairs={{0,2},{1,3},{2,0},{3,1},{4,6},{5,7},{6,4},{7,5},{8,10},{9,11},{10,... | collective-permute-start | bytes 24584 | tf_op jit(solution)/shard_map/ppermute | solution.py:402
  25.2 1.2 %collective-permute-start.9 = (f32[8,256]{1,0:T(8,128)S(1)}, f32[8,256]{1,0:T(8,128)S(1)}, u32[]{:S(2)}, u32[]{:S(2)}) collective-permute-start(f32[8,256]{1,0:T(8,128)S(1)} %add.32), channel_id=1, source_target_pairs={{0,1},{1,0},{2,3},{3,2},{4,5},{5,4},{6,7},{7,6},{8,9},{9,8},{10,11... | collective-permute-start | bytes 24584 | tf_op jit(solution)/shard_map/ppermute | solution.py:402
  25.2 8.0 %collective-permute-start.3 = (bf16[384,512]{1,0:T(8,128)(2,1)}, bf16[384,512]{1,0:T(8,128)(2,1)S(1)}, u32[]{:S(2)}, u32[]{:S(2)}) collective-permute-start(bf16[384,512]{1,0:T(8,128)(2,1)} %get-tuple-element.24), channel_id=1, source_target_pairs={{0,1},{1,0},{2,3},{3,2},{4,5},{5,4},{6,7},{7,6},{8,9},{9,8},{10,11... | collective-permute-start | bytes 1179656 | tf_op jit(solution)/shard_map/ppermute | solution.py:402
  27.0 16.6 %copy-start.3 = (bf16[1280,256]{1,0:T(8,128)(2,1)S(1)}, bf16[1280,256]{1,0:T(8,128)(2,1)}, u32[]{:S(2)}) copy-start(bf16[1280,256]{1,0:T(8,128)(2,1)} %weight_ref.4) | copy-start | bytes 1966084
  27.0 16.6 %copy-start.6 = (f32[4,256]{1,0:T(4,128)S(1)}, f32[4,256]{1,0:T(4,128)}, u32[]{:S(2)}) copy-start(f32[4,256]{1,0:T(4,128)} %bias_branch_ref.1) | copy-start | bytes 12292
  27.0 16.6 %copy-start.8 = (f32[256]{0:T(256)S(1)}, f32[256]{0:T(256)}, u32[]{:S(2)}) copy-start(f32[256]{0:T(256)} %param.21) | copy-start | bytes 3076
  27.0 16.6 %copy-start.9 = (f32[256]{0:T(256)S(1)}, f32[256]{0:T(256)}, u32[]{:S(2)}) copy-start(f32[256]{0:T(256)} %param.23) | copy-start | bytes 3076
  27.0 11.2 %collective-permute-start.10 = (f32[8,256]{1,0:T(8,128)}, f32[8,256]{1,0:T(8,128)}, u32[]{:S(2)}, u32[]{:S(2)}) collective-permute-start(f32[8,256]{1,0:T(8,128)} %add.33), channel_id=1, source_target_pairs={{0,4},{4,0},{8,12},{12,8},{1,5},{5,1},{9,13},{13,9},{2,6},{6,2},{1... | collective-permute-start | bytes 24584 | tf_op jit(solution)/shard_map/ppermute | solution.py:402
  29.3 10.3 %collective-permute-start.13 = (bf16[192,256]{1,0:T(8,128)(2,1)}, bf16[192,256]{1,0:T(8,128)(2,1)S(1)}, u32[]{:S(2)}, u32[]{:S(2)}) collective-permute-start(bf16[192,256]{1,0:T(8,128)(2,1)} %add_convert_fusion.3), channel_id=1, source_target_pairs={{0,8},{4,12},{8,0},{12,4},{1,9},{5,13},{9,1},{13,5},{2,10},{6,14},... | collective-permute-start | bytes 294920 | tf_op jit(solution)/shard_map/ppermute | solution.py:516
  32.0 20.2 %copy-start.13 = (f32[48]{0:T(128)S(1)}, f32[48]{0:T(128)}, u32[]{:S(2)}) copy-start(f32[48]{0:T(128)} %param.25) | copy-start | bytes 580
  32.0 20.2 %copy-start.1 = (bf16[3,3,304,256]{3,2,1,0:T(8,128)(2,1)S(1)}, bf16[3,3,304,256]{3,2,1,0:T(8,128)(2,1)}, u32[]{:S(2)}) copy-start(bf16[3,3,304,256]{3,2,1,0:T(8,128)(2,1)} %weight_ref.5) | copy-start | bytes 4202500
  32.7 19.5 %copy-start.7 = (f32[256]{0:T(256)S(1)}, f32[256]{0:T(256)}, u32[]{:S(2)}) copy-start(f32[256]{0:T(256)} %param.27) | copy-start | bytes 3076
  32.7 8.1 %collective-permute-start.6 = (bf16[192,512]{1,0:T(8,128)(2,1)}, bf16[192,512]{1,0:T(8,128)(2,1)}, u32[]{:S(2)}, u32[]{:S(2)}) collective-permute-start(bf16[192,512]{1,0:T(8,128)(2,1)} %get-tuple-element.33), channel_id=1, source_target_pairs={{0,2},{1,3},{2,0},{3,1},{4,6},{5,7},{6,4},{7,5},{8,10},{9,11},{10,... | collective-permute-start | bytes 589832 | tf_op jit(solution)/shard_map/ppermute | solution.py:402
  34.1 9.5 %collective-permute-start.4 = (bf16[192,512]{1,0:T(8,128)(2,1)}, bf16[192,512]{1,0:T(8,128)(2,1)S(1)}, u32[]{:S(2)}, u32[]{:S(2)}) collective-permute-start(bf16[192,512]{1,0:T(8,128)(2,1)} %get-tuple-element.35), channel_id=1, source_target_pairs={{0,2},{1,3},{2,0},{3,1},{4,6},{5,7},{6,4},{7,5},{8,10},{9,11},{10,... | collective-permute-start | bytes 589832 | tf_op jit(solution)/shard_map/ppermute | solution.py:402
  36.3 12.8 %collective-permute-start = (bf16[2,96,256]{2,1,0:T(8,128)(2,1)}, bf16[2,96,256]{2,1,0:T(8,128)(2,1)S(1)}, u32[]{:S(2)}, u32[]{:S(2)}) collective-permute-start(bf16[2,96,256]{2,1,0:T(8,128)(2,1)} %get-tuple-element.32), channel_id=1, source_target_pairs={{0,4},{4,0},{8,12},{12,8},{1,5},{5,1},{9,13},{13,9},{2,6},{6,2},{1... | collective-permute-start | bytes 294920 | tf_op jit(solution)/shard_map/ppermute | solution.py:430
  38.2 12.5 %collective-permute-start.1 = (bf16[2,96,256]{2,1,0:T(8,128)(2,1)}, bf16[2,96,256]{2,1,0:T(8,128)(2,1)S(1)}, u32[]{:S(2)}, u32[]{:S(2)}) collective-permute-start(bf16[2,96,256]{2,1,0:T(8,128)(2,1)} %get-tuple-element.31), channel_id=1, source_target_pairs={{4,8},{8,4},{5,9},{9,5},{6,10},{10,6},{7,11},{11,7},{20,24},{24,20... | collective-permute-start | bytes 294920 | tf_op jit(solution)/shard_map/ppermute | solution.py:431
  44.8 5.1 %collective-permute-start.17 = (bf16[96,256]{1,0:T(8,128)(2,1)S(1)}, bf16[96,256]{1,0:T(8,128)(2,1)S(1)}, u32[]{:S(2)}, u32[]{:S(2)}) collective-permute-start(bf16[96,256]{1,0:T(8,128)(2,1)S(1)} %get-tuple-element.30), channel_id=1, source_target_pairs={{1,4},{4,1},{5,8},{8,5},{9,12},{12,9},{3,6},{6,3},{7,10},{10,7},{1... | collective-permute-start | bytes 147464 | tf_op jit(solution)/shard_map/ppermute | solution.py:420
  45.5 5.7 %collective-permute-start.14 = (bf16[192,256]{1,0:T(8,128)(2,1)S(1)}, bf16[192,256]{1,0:T(8,128)(2,1)S(1)}, u32[]{:S(2)}, u32[]{:S(2)}) collective-permute-start(bf16[192,256]{1,0:T(8,128)(2,1)S(1)} %get-tuple-element.29.refs_0_), channel_id=1, source_target_pairs={{0,1},{1,0},{2,3},{3,2},{4,5},{5,4},{6,7},{7,6},{8,9},{9,8},{10,11... | collective-permute-start | bytes 294920 | tf_op jit(solution)/shard_map/ppermute | solution.py:402
  48.5 5.7 %collective-permute-start.15 = (bf16[192,256]{1,0:T(8,128)(2,1)S(1)}, bf16[192,256]{1,0:T(8,128)(2,1)S(1)}, u32[]{:S(2)}, u32[]{:S(2)}) collective-permute-start(bf16[192,256]{1,0:T(8,128)(2,1)S(1)} %get-tuple-element.29.refs_0_), channel_id=1, source_target_pairs={{0,2},{1,3},{2,0},{3,1},{4,6},{5,7},{6,4},{7,5},{8,10},{9,11},{10,... | collective-permute-start | bytes 294920 | tf_op jit(solution)/shard_map/ppermute | solution.py:402
  49.1 5.3 %collective-permute-start.16 = (bf16[192,256]{1,0:T(8,128)(2,1)S(1)}, bf16[192,256]{1,0:T(8,128)(2,1)S(1)}, u32[]{:S(2)}, u32[]{:S(2)}) collective-permute-start(bf16[192,256]{1,0:T(8,128)(2,1)S(1)} %get-tuple-element.29.refs_0_), channel_id=1, source_target_pairs={{0,3},{1,2},{2,1},{3,0},{4,7},{5,6},{6,5},{7,4},{8,11},{9,10},{10,... | collective-permute-start | bytes 294920 | tf_op jit(solution)/shard_map/ppermute | solution.py:402
  49.9 4.5 %collective-permute-start.18 = (bf16[96,256]{1,0:T(8,128)(2,1)S(1)}, bf16[96,256]{1,0:T(8,128)(2,1)S(1)}, u32[]{:S(2)}, u32[]{:S(2)}) collective-permute-start(bf16[96,256]{1,0:T(8,128)(2,1)S(1)} %collective-permute-done.17.refs_4_), channel_id=1, source_target_pairs={{0,1},{1,0},{2,3},{3,2},{4,5},{5,4},{6,7},{7,6},{8,9},{9,8},{10,11... | collective-permute-start | bytes 147464 | tf_op jit(solution)/shard_map/ppermute | solution.py:402
  50.7 6.2 %collective-permute-start.19 = (bf16[96,256]{1,0:T(8,128)(2,1)S(1)}, bf16[96,256]{1,0:T(8,128)(2,1)S(1)}, u32[]{:S(2)}, u32[]{:S(2)}) collective-permute-start(bf16[96,256]{1,0:T(8,128)(2,1)S(1)} %collective-permute-done.17.refs_4_), channel_id=1, source_target_pairs={{0,2},{1,3},{2,0},{3,1},{4,6},{5,7},{6,4},{7,5},{8,10},{9,11},{10,... | collective-permute-start | bytes 147464 | tf_op jit(solution)/shard_map/ppermute | solution.py:402
  51.3 5.7 %collective-permute-start.20 = (bf16[96,256]{1,0:T(8,128)(2,1)S(1)}, bf16[96,256]{1,0:T(8,128)(2,1)S(1)}, u32[]{:S(2)}, u32[]{:S(2)}) collective-permute-start(bf16[96,256]{1,0:T(8,128)(2,1)S(1)} %collective-permute-done.17.refs_4_), channel_id=1, source_target_pairs={{0,3},{1,2},{2,1},{3,0},{4,7},{5,6},{6,5},{7,4},{8,11},{9,10},{10,... | collective-permute-start | bytes 147464 | tf_op jit(solution)/shard_map/ppermute | solution.py:402

commit v3 on v2

--- a/solution.py
+++ b/solution.py
@@ -13,15 +13,15 @@
 ROW_BLOCK = 6
 MOST_LAND = 4
 VMEM_LIMIT = 32 * 2 ** 20
-WHOLE_VMEM = 60 * 2 ** 20
-EARLY = 2
+WHOLE_VMEM = 58 * 2 ** 20
+POOL_ROWS = 8
 F32 = jnp.float32
 BF16 = jnp.bfloat16
 VMEM = pl.BlockSpec(memory_space=pltpu.VMEM)
 HBM = pl.BlockSpec(memory_space=pltpu.HBM)
 
 
-def call(body, outs, in_specs, scratch, flops, bytes_accessed, limit=VMEM_LIMIT):
+def call(body, outs, in_specs, scratch, limit=VMEM_LIMIT):
     return pl.pallas_call(
         body,
         out_shape=outs,
@@ -29,9 +29,7 @@
         out_specs=jax.tree.map(lambda _: VMEM, outs),
         scratch_shapes=scratch,
         compiler_params=pltpu.CompilerParams(vmem_limit_bytes=limit),
-        cost_estimate=pl.CostEstimate(
-            flops=flops, bytes_accessed=bytes_accessed, transcendentals=0
-        ),
+        cost_estimate=pl.CostEstimate(flops=1024, bytes_accessed=1024, transcendentals=0),
     )
 
 
@@ -133,152 +131,155 @@
     send[:, pl.ds(index * width, width)] = value[half:]
 
 
-def early_kernel(plan, mask_ref, features_ref, dilated_ref, keep, send, slots_ref, land_ref, rows_ref, taps_ref, mask_sem, row_sems, tap_sems):
-    columns, width = plan.columns, dilated_ref.shape[4]
-    mask_copy = pltpu.make_async_copy(mask_ref, land_ref, mask_sem)
-    mask_copy.start()
-    branches = range(EARLY - 1, len(DILATIONS))
-    tap_copies = []
-    for index, branch in enumerate(branches):
-        tap_copies.append([])
-        for tap in range(3):
-            copy = pltpu.make_async_copy(
-                dilated_ref.at[branch, 1, tap],
-                taps_ref.at[index, :, pl.ds(tap * width, width)],
-                tap_sems.at[index, tap],
-            )
-            copy.start()
-            tap_copies[-1].append(copy)
-    mask_copy.wait()
-    fill_slots(land_ref, slots_ref, plan.batches, plan.row_count)
-    row_copies = []
+def gather(plan, mask, features_ref, slots_ref, rows_ref):
+    fill_slots(mask, slots_ref, plan.batches, plan.row_count)
     sect = lax.axis_index("sect")
     for position in range(plan.sects):
         for image, row, start in plan.rows_of(position, sect, slots_ref):
-            copy = pltpu.make_async_copy(
-                features_ref.at[image, row],
-                rows_ref.at[pl.ds(start, columns)],
-                row_sems.at[start // columns],
-            )
-            copy.start()
-            row_copies.append(copy)
-    for copy in row_copies:
-        copy.wait()
-    for index, branch in enumerate(branches):
-        for copy in tap_copies[index]:
+            rows_ref[pl.ds(start, plan.columns)] = features_ref[image, row]
+
+
+def parts_of(value):
+    high, low, _ = split_three(value)
+    return jnp.concatenate([high.astype(F32), low.astype(F32)], axis=0)
+
+
+def joined_parts(rows):
+    return rows[:POOL_ROWS].astype(F32) + rows[POOL_ROWS:].astype(F32)
+
+
+def pool_kernel(features_ref, weight_ref, out_ref):
+    batches, row_count, columns, channels = features_ref.shape
+    row = lax.broadcasted_iota(jnp.int32, (POOL_ROWS, channels), 0)
+    sums = jnp.zeros((POOL_ROWS, channels), F32)
+    for image in range(batches):
+        cells = features_ref[image].astype(F32).reshape(row_count * columns, channels)
+        sums = jnp.where(row == image, jnp.sum(cells, axis=0, keepdims=True), sums)
+    out_ref[...] = parts_of(precise_dot(sums, weight_ref[...])).astype(BF16)
+
+
+def edge_kernel(plan, low_ref, keep_ref, moved_ref, far_ref, first_ref, second_ref):
+    far = keep_ref[...].astype(F32) + moved_ref[...].astype(F32)
+    far_ref[...] = far.astype(BF16)
+    cells, width = plan.batches * plan.columns, low_ref.shape[3]
+    first_ref[pl.ds(cells, 2 * POOL_ROWS)] = far[plan.share :, :width].astype(BF16)
+    odd = lax.rem(lax.axis_index("band"), 2)
+    last = plan.row_count - 1
+    for image in range(plan.batches):
+        rows = pl.ds(image * plan.columns, plan.columns)
+        first_ref[rows] = low_ref[image, last - odd * last]
+        second_ref[rows] = low_ref[image, odd * last]
+
+
+def fetch_taps(dilated_ref, branch, row_tap, taps_ref, index, sems):
+    width = dilated_ref.shape[4]
+    copies = []
+    for tap in range(3):
+        copy = pltpu.make_async_copy(
+            dilated_ref.at[branch, row_tap, tap],
+            taps_ref.at[index, :, pl.ds(tap * width, width)],
+            sems.at[index, tap],
+        )
+        copy.start()
+        copies.append(copy)
+    return copies
+
+
+def own_kernel(plan, mask_ref, features_ref, one_ref, dilated_ref, keep, send, slots_ref, land_ref, held_ref, rows_ref, ones_ref, taps_ref, sems, tap_sems):
+    copies = [
+        pltpu.make_async_copy(mask_ref, land_ref, sems.at[0]),
+        pltpu.make_async_copy(features_ref, held_ref, sems.at[1]),
+        pltpu.make_async_copy(one_ref, ones_ref, sems.at[2]),
+    ]
+    for copy in copies:
+        copy.start()
+    tap_copies = [
+        fetch_taps(dilated_ref, branch, 1, taps_ref, branch, tap_sems)
+        for branch in range(len(DILATIONS))
+    ]
+    copies[0].wait()
+    copies[1].wait()
+    gather(plan, land_ref, held_ref, slots_ref, rows_ref)
+    copies[2].wait()
+    value = jnp.dot(rows_ref[...], ones_ref[...], preferred_element_type=F32)
+    store_halves(keep, send, 0, value)
+    for branch, waits in enumerate(tap_copies):
+        for copy in waits:
             copy.wait()
-        value = tap_sum(rows_ref[...], taps_ref[index], DILATIONS[branch], columns)
-        store_halves(keep, send, index, value)
-
-
-def early_partials(plan, mask, features, weight_dilated):
-    channels, width = weight_dilated.shape[3:]
-    half = plan.sects // 2 * plan.share
-    branches = len(DILATIONS) + 1 - EARLY
-    out = jax.ShapeDtypeStruct((half, branches * width), BF16)
-    slots = plan.batches * MOST_LAND
-    scratch = [
-        pltpu.SMEM((2, slots), jnp.int32),
-        pltpu.SMEM(mask.shape, jnp.int32),
-        pltpu.VMEM((2 * half, channels), BF16),
-        pltpu.VMEM((branches, channels, 3 * width), BF16),
-        pltpu.SemaphoreType.DMA,
-        pltpu.SemaphoreType.DMA((slots,)),
-        pltpu.SemaphoreType.DMA((branches, 3)),
-    ]
-    return call(
-        functools.partial(early_kernel, plan),
-        (out, out),
-        [HBM, HBM, HBM],
-        scratch,
-        2 * 3 * branches * 2 * half * channels * width,
-        2 * (3 * branches * channels * width + 2 * half * channels),
-        WHOLE_VMEM,
-    )(mask, features, weight_dilated)
-
-
-def late_kernel(plan, needed, mask_ref, far_mask_ref, features_ref, one_ref, *refs):
-    terms = len(plan.terms)
-    dilated = dict(zip(needed, refs[: len(needed)]))
-    refs = refs[len(needed) :]
-    outs = refs[: 2 + (2 if terms else 0)]
-    slots_ref, rows_ref = refs[len(outs) :]
-    sect, band = lax.axis_index("sect"), lax.axis_index("band")
-
-    def gather(mask):
-        fill_slots(mask, slots_ref, plan.batches, plan.row_count)
-        for position in range(plan.sects):
-            for image, row, start in plan.rows_of(position, sect, slots_ref):
-                rows_ref[pl.ds(start, plan.columns)] = features_ref[image, row]
-
-    def taps_of(branch, row_tap):
-        return jnp.concatenate([dilated[branch][row_tap, tap] for tap in range(3)], axis=1)
-
-    for term, (branch, hop, row_tap, _) in enumerate(plan.terms):
-        gather(far_mask_ref.at[term])
-        if row_tap is None:
-            row_tap = jnp.where(band + hop < plan.bands, 0, 2)
-        taps = taps_of(branch, row_tap)
-        value = tap_sum(rows_ref[...], taps, DILATIONS[branch], plan.columns)
-        store_halves(outs[2], outs[3], term, value)
-    gather(mask_ref)
-    value = jnp.dot(rows_ref[...], one_ref[...], preferred_element_type=F32)
-    store_halves(outs[0], outs[1], 0, value)
-    for branch in range(EARLY - 1):
-        value = tap_sum(rows_ref[...], taps_of(branch, 1), DILATIONS[branch], plan.columns)
-        store_halves(outs[0], outs[1], branch + 1, value)
-
-
-def late_partials(plan, mask, far_mask, features, weight_one, weight_dilated):
-    terms = len(plan.terms)
+        value = tap_sum(rows_ref[...], taps_ref[branch], DILATIONS[branch], plan.columns)
+        store_halves(keep, send, branch + 1, value)
+
+
+def own_partials(plan, mask, features, weight_one, weight_dilated):
     channels, width = weight_one.shape
     half = plan.sects // 2 * plan.share
-    own = jax.ShapeDtypeStruct((half, EARLY * width), BF16)
-    outs = [own, own]
-    if terms:
-        far = jax.ShapeDtypeStruct((half, terms * width), BF16)
-        outs += [far, far]
-    needed = sorted({term[0] for term in plan.terms} | set(range(EARLY - 1)))
-    products = 1 + 3 * (EARLY - 1 + terms)
+    out = jax.ShapeDtypeStruct((half, (1 + len(DILATIONS)) * width), BF16)
     return call(
-        functools.partial(late_kernel, plan, needed),
-        tuple(outs),
-        [VMEM] * (4 + len(needed)),
+        functools.partial(own_kernel, plan),
+        (out, out),
+        [HBM, HBM, HBM, HBM],
         [
             pltpu.SMEM((2, plan.batches * MOST_LAND), jnp.int32),
+            pltpu.SMEM(mask.shape, jnp.int32),
+            pltpu.VMEM(features.shape, BF16),
             pltpu.VMEM((2 * half, channels), BF16),
+            pltpu.VMEM((channels, width), BF16),
+            pltpu.VMEM((len(DILATIONS), channels, 3 * width), BF16),
+            pltpu.SemaphoreType.DMA((3,)),
+            pltpu.SemaphoreType.DMA((len(DILATIONS), 3)),
         ],
-        2 * products * 2 * half * channels * width,
-        2 * (9 * len(needed) * channels * width + features.size),
-    )(mask, far_mask, features, weight_one, *[weight_dilated[branch] for branch in needed])
-
-
-def pool_kernel(features_ref, weight_ref, out_ref):
-    batches, row_count, columns, channels = features_ref.shape
-    sums = [
-        jnp.sum(
-            features_ref[image].astype(F32).reshape(row_count * columns, channels),
-            axis=0,
-            keepdims=True,
-        )
-        for image in range(batches)
-    ]
-    row = lax.broadcasted_iota(jnp.int32, (out_ref.shape[0], channels), 0)
-    stacked = jnp.zeros((out_ref.shape[0], channels), F32)
-    for image, value in enumerate(sums):
-        stacked = jnp.where(row == image, value, stacked)
-    out_ref[...] = precise_dot(stacked, weight_ref[...])
+        WHOLE_VMEM,
+    )(mask, features, weight_one, weight_dilated)
+
+
+def far_kernel(plan, far_mask_ref, pool_ref, features_ref, *refs):
+    terms = len(plan.terms)
+    taps_refs, (keep, send, slots_ref, rows_ref) = refs[:terms], refs[terms:]
+    pooled = pool_ref[...]
+    block = plan.share + 2 * POOL_ROWS
+    for term, taps_ref in enumerate(taps_refs):
+        width = taps_ref.shape[2]
+        gather(plan, far_mask_ref.at[term], features_ref, slots_ref, rows_ref)
+        taps = jnp.concatenate([taps_ref[tap] for tap in range(3)], axis=1)
+        dilation = DILATIONS[plan.terms[term][0]]
+        value = tap_sum(rows_ref[...], taps, dilation, plan.columns).astype(BF16)
+        lanes = pl.ds(term * width, width)
+        for position in range(plan.sects):
+            out = keep if position < plan.sects // 2 else send
+            start = position % (plan.sects // 2) * block
+            share = value[position * plan.share : (position + 1) * plan.share]
+            out[pl.ds(start, plan.share), lanes] = share
+            out[pl.ds(start + plan.share, 2 * POOL_ROWS), lanes] = pooled
+
+
+def far_partials(plan, far_mask, pool, features, taps):
+    channels, width = taps[0].shape[1:]
+    rows = plan.sects // 2 * (plan.share + 2 * POOL_ROWS)
+    out = jax.ShapeDtypeStruct((rows, len(taps) * width), BF16)
+    return call(
+        functools.partial(far_kernel, plan),
+        (out, out),
+        [VMEM] * (3 + len(taps)),
+        [
+            pltpu.SMEM((2, plan.batches * MOST_LAND), jnp.int32),
+            pltpu.VMEM((plan.sects * plan.share, channels), BF16),
+        ],
+    )(far_mask, pool, features, *taps)
 
 
 def low_kernel(plan, low_ref, first_ref, second_ref, reduce_ref, bias_reduce_ref, merging_ref, bias_ref, out_ref, framed_ref):
     batches, row_count, columns, depth = low_ref.shape
     band, bands = lax.axis_index("band"), plan.bands
-    wide = reduce_ref.shape[1]
-    reduced = wide // 3
+    reduced = reduce_ref.shape[1]
+    wide = 3 * reduced
     even = lax.rem(band, 2) == 0
+    copied = lax.broadcasted_iota(jnp.int32, (reduced, wide), 1) % reduced
+    copies = (copied == lax.broadcasted_iota(jnp.int32, (reduced, wide), 0)).astype(F32).astype(BF16)
+    weight = jnp.dot(reduce_ref[...], copies, preferred_element_type=F32).astype(BF16)
+    bias = precise_dot(bias_reduce_ref[...], copies)
 
     def reduce(rows):
-        value = jnp.dot(rows, reduce_ref[...], preferred_element_type=F32) + bias_reduce_ref[...]
+        value = jnp.dot(rows, weight, preferred_element_type=F32) + bias
         value = jnp.maximum(value, 0.0).astype(BF16).astype(F32)
         lane = lax.broadcasted_iota(jnp.int32, value.shape, 1)
         return jnp.where(
@@ -290,38 +291,39 @@
     framed_ref[:, 1 : row_count + 1] = (
         reduce(low_ref[...].reshape(-1, depth)).astype(BF16).reshape(batches, row_count, columns, wide)
     )
-    first = reduce(first_ref[...].reshape(-1, depth))
-    second = reduce(second_ref[...].reshape(-1, depth))
+    first = reduce(first_ref[: batches * columns])
+    second = reduce(second_ref[...])
     above = jnp.where(even, second, first) * jnp.where(band > 0, 1.0, 0.0)
     below = jnp.where(even, first, second) * jnp.where(band < bands - 1, 1.0, 0.0)
     framed_ref[:, 0] = above.astype(BF16).reshape(batches, columns, wide)
     framed_ref[:, row_count + 1] = below.astype(BF16).reshape(batches, columns, wide)
+    width = merging_ref.shape[2] - reduced
     for image in range(batches):
         total = jnp.zeros((row_count * columns, out_ref.shape[3]), F32) + bias_ref[...]
         for tap in range(3):
             rows = framed_ref[image, tap : tap + row_count].reshape(-1, wide)
-            total = total + jnp.dot(rows, merging_ref[tap], preferred_element_type=F32)
+            taps = jnp.concatenate([merging_ref[tap, side, width:] for side in range(3)], axis=0)
+            total = total + jnp.dot(rows, taps, preferred_element_type=F32)
         out_ref[image] = total.reshape(row_count, columns, -1)
 
 
-def project_kernel(plan, mask_ref, keep_ref, moved_ref, early_keep_ref, early_moved_ref, bias_branch_ref, pool_ref, bias_pool_ref, weight_ref, bias_ref, *refs):
+def project_kernel(plan, mask_ref, keep_ref, moved_ref, bias_branch_ref, pool_ref, bias_pool_ref, weight_ref, bias_ref, *refs):
     far_refs = refs[: len(plan.terms)]
     out_ref, edge_ref, slots_ref, context_ref = refs[len(plan.terms) :]
     columns, width = plan.columns, weight_ref.shape[1]
     sect = lax.axis_index("sect")
     fill_slots(mask_ref, slots_ref, plan.batches, plan.row_count)
     cells = plan.row_count * plan.bands * columns
-    pooled = jnp.maximum(pool_ref[...] / cells + bias_pool_ref[...], 0.0)
+    pooled = pool_ref[...] / cells
+    pooled = jnp.maximum(pooled + bias_pool_ref[...], 0.0)
     context_ref[...] = precise_dot(pooled, weight_ref[4 * width :]) + bias_ref[...]
     total = jnp.zeros((plan.share, width), F32)
     for branch in range(4):
-        early = branch >= EARLY
-        kept, added = (early_keep_ref, early_moved_ref) if early else (keep_ref, moved_ref)
-        lanes = pl.ds((branch - EARLY if early else branch) * width, width)
-        value = kept[:, lanes].astype(F32) + added[:, lanes].astype(F32)
+        lanes = pl.ds(branch * width, width)
+        value = keep_ref[:, lanes].astype(F32) + moved_ref[:, lanes].astype(F32)
         for term, far in zip(plan.terms, far_refs):
             if term[0] + 1 == branch:
-                value = value + far[...].astype(F32)
+                value = value + far[: plan.share].astype(F32)
         value = jnp.maximum(value + bias_branch_ref[pl.ds(branch, 1)], 0.0).astype(BF16)
         total = total + jnp.dot(
             value, weight_ref[pl.ds(branch * width, width)], preferred_element_type=F32
@@ -408,6 +410,14 @@
     return total[:half], total[half:]
 
 
+def spread_over(value, plan):
+    values = {0: value}
+    for bit in reversed(range(plan.bits)):
+        for offset in list(values):
+            values[offset ^ 1 << bit] = swap(values[offset], "sect", 1 << bit)
+    return [values[offset] for offset in range(plan.sects)]
+
+
 def swap_edges(edge, plan):
     pairs = []
     for image in range(plan.batches):
@@ -420,30 +430,28 @@
     return lax.ppermute(edge, ("band", "sect"), pairs)
 
 
-def swap_low_edges(low_level, band, bands):
-    top, bottom = low_level[:, 0], low_level[:, -1]
-    even = band % 2 == 0
-    first_pairs = [(b, b ^ 1) for b in range(bands) if b ^ 1 < bands]
+def swap_low_edges(first, second, bands):
+    first_pairs = [(b, b ^ 1) for b in range(bands)]
     second_pairs = []
     for b in range(1, bands - 1, 2):
         second_pairs += [(b, b + 1), (b + 1, b)]
-    first = lax.ppermute(jnp.where(even, bottom, top), "band", first_pairs)
-    second = lax.ppermute(jnp.where(even, top, bottom), "band", second_pairs)
-    return first, second
-
-
-def fits(batches, row_count, columns, bands, sects):
+    return lax.ppermute(first, "band", first_pairs), lax.ppermute(second, "band", second_pairs)
+
+
+def fits(batches, row_count, columns, bands, sects, low_depth, width):
     slots = batches * MOST_LAND
     return (
         row_count == ROW_BLOCK
         and all(dilation % row_count == 0 for dilation in DILATIONS)
         and sects > 1
         and sects & (sects - 1) == 0
+        and bands > min(DILATIONS) // row_count
+        and low_depth == width
         and bands & (bands - 1) == 0
         and slots % sects == 0
         and MOST_LAND % (2 * (slots // sects)) == 0
         and columns % 16 == 0
-        and batches <= 8
+        and batches <= POOL_ROWS
     )
 
 
@@ -468,89 +476,89 @@
     plan = Plan(batches, row_count, columns, bands, sects)
     width = weight_one.shape[1]
     band = lax.axis_index("band")
-    early_keep, early_send = early_partials(plan, land_mask, features, weight_dilated)
-    early_keep, early_send, later_mask, later_features, later_low = lax.optimization_barrier(
-        (early_keep, early_send, land_mask, features, low_level)
-    )
-    pool = call(
-        pool_kernel,
-        jax.ShapeDtypeStruct((8, width), F32),
-        [VMEM, VMEM],
-        [],
-        3 * 16 * channels * width,
-        2 * features.size,
-    )(later_features, weight_pool)
-    early_moved = swap(early_send, "sect", 1)
+    keep, send = own_partials(plan, land_mask, features, weight_one, weight_dilated)
+    keep, send, late_mask, late_features, late_low = lax.optimization_barrier(
+        (keep, send, land_mask, features, low_level)
+    )
     far_masks = [
-        lax.ppermute(later_mask, "band", [(target, source) for source, target in pairs])
+        lax.ppermute(late_mask, "band", [(target, source) for source, target in pairs])
         for _, _, _, pairs in plan.terms
     ]
-    pool_bits = list(range(bands.bit_length() - 1))
-    if pool_bits:
-        pool = pool + swap(pool, "band", 1 << pool_bits.pop())
-    far_mask = jnp.stack(far_masks or [land_mask])
-    for bit in range(1, plan.bits):
-        early_keep, early_send = add_halves(early_keep, early_moved)
-        early_moved = swap(early_send, "sect", 1 << bit)
-    for bit in range(1, plan.bits):
-        pool = pool + swap(pool, "sect", 1 << bit)
-    pieces = late_partials(
-        plan, later_mask, far_mask, later_features, weight_one, weight_dilated
-    )
-    keep, send = pieces[:2]
-    far_keep, far_send = pieces[2:] if plan.terms else (None, None)
-    pool = pool + swap(pool, "sect", 1)
-    for bit in range(plan.bits):
-        pattern = 1 << bit
-        last = bit == plan.bits - 1
-        if plan.terms:
-            far_moved = swap(far_send, "sect", pattern)
-            if last:
-                far = (far_keep.astype(F32) + far_moved.astype(F32)).astype(BF16)
-            else:
-                far_keep, far_send = add_halves(far_keep, far_moved)
-        moved = swap(send, "sect", pattern)
-        if not last:
-            keep, send = add_halves(keep, moved)
-    far_terms = [
-        lax.ppermute(far[:, term * width : (term + 1) * width], "band", pairs)
-        for term, (_, _, _, pairs) in enumerate(plan.terms)
-    ]
-    first, second = swap_low_edges(later_low, band, bands)
-    for bit in reversed(pool_bits):
-        pool = pool + swap(pool, "band", 1 << bit)
+    pool = call(
+        pool_kernel, jax.ShapeDtypeStruct((2 * POOL_ROWS, width), BF16), [VMEM, VMEM], []
+    )(late_features, weight_pool)
+    moved = swap(send, "sect", 1)
+    for bit in range(1, plan.bits - 1):
+        keep, send = add_halves(keep, moved)
+        moved = swap(send, "sect", 1 << bit)
+    keep, send = add_halves(keep, moved)
+    moved = swap(send, "sect", plan.sects // 2)
+    far_mask = jnp.stack(far_masks)
+    far_mask, send = lax.optimization_barrier((far_mask, send))
+    taps = []
+    for branch, hop, row_tap, _ in plan.terms:
+        if row_tap is None:
+            row_tap = jnp.where(band + hop < bands, 0, 2)
+        start = (branch, row_tap, 0, 0, 0)
+        size = (1, 1) + weight_dilated.shape[2:]
+        taps.append(lax.dynamic_slice(weight_dilated, start, size)[0, 0])
+    far_keep, far_send = far_partials(plan, far_mask, pool, late_features, taps)
+    for bit in range(plan.bits - 1):
+        far_moved = swap(far_send, "sect", 1 << bit)
+        far_keep, far_send = add_halves(far_keep, far_moved)
+    far_moved = swap(far_send, "sect", plan.sects // 2)
+    far, first, second = call(
+        functools.partial(edge_kernel, plan),
+        (
+            jax.ShapeDtypeStruct(far_keep.shape, BF16),
+            jax.ShapeDtypeStruct((batches * columns + 2 * POOL_ROWS, width), BF16),
+            jax.ShapeDtypeStruct((batches * columns, width), BF16),
+        ),
+        [VMEM] * 3,
+        [],
+    )(late_low, far_keep, far_moved)
+    far_terms = []
+    for term, (_, hop, _, pairs) in enumerate(plan.terms):
+        rows = far if 2 * hop == bands else far[: plan.share]
+        lanes = slice(term * width, (term + 1) * width)
+        far_terms.append(lax.ppermute(rows[:, lanes], "band", pairs))
+    own_pool = far[plan.share :, :width]
+    first, second = swap_low_edges(first, second, bands)
+    pool = joined_parts(own_pool) + joined_parts(first[batches * columns :])
+    if bands == 4 and any(2 * term[1] == bands for term in plan.terms):
+        halves = [term for term, entry in enumerate(plan.terms) if 2 * entry[1] == bands]
+        pool = pool + joined_parts(far_terms[halves[0]][plan.share :])
+        pool = pool + joined_parts(swap(own_pool, "band", 3))
+    else:
+        for bit in range(1, bands.bit_length() - 1):
+            pool = pool + swap(pool, "band", 1 << bit)
     reduced = weight_reduce.shape[1]
     low_part = call(
         functools.partial(low_kernel, plan),
         jax.ShapeDtypeStruct((batches, row_count, columns, weight_merging.shape[3]), F32),
         [VMEM] * 7,
         [pltpu.VMEM((batches, row_count + 2, columns, 3 * reduced), BF16)],
-        2 * 3 * batches * row_count * columns * 256 * 256,
-        4 * low_level.size,
     )(
-        later_low,
+        late_low,
         first,
         second,
-        jnp.concatenate([weight_reduce] * 3, axis=1),
-        jnp.concatenate([bias_reduce] * 3)[None],
-        weight_merging[:, :, width:].reshape(3, 3 * reduced, -1),
+        weight_reduce,
+        bias_reduce[None],
+        weight_merging,
         bias_merging[None],
     )
+    keep, low_part = lax.optimization_barrier((keep, low_part))
     share = jax.ShapeDtypeStruct((plan.share, width), BF16)
     row = jax.ShapeDtypeStruct((columns, width), BF16)
     out, edge = call(
         functools.partial(project_kernel, plan),
         (share, row),
-        [VMEM] * (10 + len(plan.terms)),
+        [VMEM] * (8 + len(plan.terms)),
         [pltpu.SMEM((2, batches * MOST_LAND), jnp.int32), pltpu.VMEM((8, width), F32)],
-        2 * plan.share * 4 * width * width,
-        4 * plan.share * 4 * width + 2 * weight_project.size,
     )(
         land_mask,
         keep,
         moved,
-        early_keep,
-        early_moved,
         bias_branch,
         pool,
         bias_pool[None],
@@ -559,8 +567,7 @@
         *far_terms,
     )
     halo = swap_edges(edge, plan)
-    shares = [out] + [swap(out, "sect", pattern) for pattern in range(1, sects)]
-    halos = [halo] + [swap(halo, "sect", pattern) for pattern in range(1, sects)]
+    shares, halos = spread_over(out, plan), spread_over(halo, plan)
     live = batches * MOST_LAND * columns
     return call(
         functools.partial(merge_kernel, plan),
@@ -572,8 +579,6 @@
             pltpu.VMEM((sects * columns, 3 * width), BF16),
             pltpu.VMEM((batches, row_count + 2, columns, width), F32),
         ],
-        2 * 9 * live * width * width,
-        4 * low_part.size + 2 * weight_merging.size + 4 * live * width,
     )(land_mask, low_part, weight_merging, *shares, *halos)
 
 
@@ -750,11 +755,12 @@
     )
     out_specs = P("grp", "band", None, None)
 
-    def chosen(features, *others):
+    def chosen(features, low_level, land_mask, weight_one, *others):
         batches, row_count, columns, _ = features.shape
+        depths = (low_level.shape[3], weight_one.shape[1])
         sizes = (batches, row_count, columns, mesh.shape["band"], mesh.shape["sect"])
-        body = shards if fits(*sizes) else general_shards
-        return body(features, *others)
+        body = shards if fits(*sizes, *depths) else general_shards
+        return body(features, low_level, land_mask, weight_one, *others)
 
     return jax.shard_map(
         chosen, mesh=mesh, in_specs=in_specs, out_specs=out_specs, check_vma=False

time: 59.8 us -> 48.5 us (0.81)
  waiting for transfers between devices: 14.2 us -> 10.6 us
  other arithmetic: 4.11 us -> 1.49 us
  starting transfers between devices: 23.4 us -> 20.9 us
  local copies, waits for them, and re-layouts: 4.79 us -> 2.52 us
    ppermute x16 -> x11, waiting for transfers between devices: 14.2 us -> 9.41 us  [swap(): return lax.ppermute(value, axis, [(i, i ^ pattern) for i in range(count)])]
    ppermute x16 -> x11, starting transfers between devices: 14.9 us -> 13.5 us  [swap(): return lax.ppermute(value, axis, [(i, i ^ pattern) for i in range(count)])]
    add x4 -> x1, other arithmetic: 1.32 us -> 0.01 us  [shards(): pool = pool + joined_parts(swap(own_pool, 'band', 3))]
    unnamed x29, local copies, waits for them, and re-layouts: 1.54 us -> 0.29 us
    convert_element_type x3 -> x2, other arithmetic: 0.24 us -> 1.48 us  [add_halves(): total = (keep.astype(F32) + moved.astype(F32)).astype(BF16)]
    concatenate x2 -> x0, other arithmetic: 1.17 us -> none  [the longest x1 1.1 us: shards(): jnp.concatenate([weight_reduce] * 3, axis=1)]
    ppermute x4, waiting for transfers between devices: 0.01 us -> 1.15 us  [the longest x1 0.66 us: swap_low_edges(): lax.ppermute(first, 'band', first_pairs)]
    ppermute x4, starting transfers between devices: 7.8 us -> 6.71 us  [the longest x1 3.67 us: shards(): lax.ppermute(late_mask, 'band', [(target, source) for source, target in p...]
  transfers between devices with their start and end apart: 21 -> 16, of which waited for: 9 -> 7; matrix products, arithmetic and copies ran while one was open for 15% -> 8% of each run, Pallas kernels for 5% -> 4%
where the time goes in v3:
time: 48.5 us; the launch traced here: 47.8 us
  starting transfers between devices  20.9 us (43%)
  Pallas kernels  12.2 us (25%)
  waiting for transfers between devices  10.6 us (22%)
  local copies, waits for them, and re-layouts  2.52 us (5%)
  other arithmetic  1.49 us (3%)
    ppermute x11, starting transfers between devices, swap(): return lax.ppermute(value, axis, [(i, i ^ pattern) for i in range(count)])  13.5 us
    ppermute x11, waiting for transfers between devices, swap(): return lax.ppermute(value, axis, [(i, i ^ pattern) for i in range(count)])  9.41 us
    pallas_call x1, Pallas kernels, own_partials(): call(functools.partial(own_kernel, plan), (out, out), [HBM, HBM, HBM, HBM...  6.74 us
    ppermute x1, starting transfers between devices, shards(): lax.ppermute(late_mask, 'band', [(target, source) for source, target in p...  3.67 us
    pallas_call x1, Pallas kernels, shards(): call(functools.partial(merge_kernel, plan), jax.ShapeDtypeStruct(low_part...  2.44 us
    ppermute x1, starting transfers between devices, swap_low_edges(): lax.ppermute(first, 'band', first_pairs)  1.64 us
    convert_element_type x2, other arithmetic, add_halves(): total = (keep.astype(F32) + moved.astype(F32)).astype(BF16)  1.48 us
    pallas_call x1, Pallas kernels, shards(): call(functools.partial(low_kernel, plan), jax.ShapeDtypeStruct((batches,...  1.33 us
  transfers between devices with their start and end apart: 16, of which 7 were waited for; matrix products, arithmetic and copies ran while one was open for 8% of the time, Pallas kernels for 4%

profile of v3, /device:TPU:0, one launch (start us, length us, event | category | flops | bytes accessed | tf_op | source)
XLA Modules:
  0.0 47.8 jit_solution(14253957859518045044)
XLA Ops:
  0.0 6.7 %shard_map.136 = (bf16[384,1024]{1,0:T(8,128)(2,1)}, bf16[384,1024]{1,0:T(8,128)(2,1)}) custom-call(s32[2,6]{1,0:T(2,128)} %mask_ref.5, bf16[2,6,96,512]{3,2,1,0:T(8,128)(2,1)} %features_ref.3, bf16[512,256]{1,0:T(8,128)(2,1)} %one_ref.1, bf16[3,3,3,512,256]{4,3,2,1,0:T(8,128)(2,1)} %dilated_ref.1), custom_call_target="tpu_custom_call" | custom-call | flops 1024 | bytes 1024 | tf_op jit(solution)/shard_map/pallas_call | solution.py:217
  6.8 0.5 %collective-permute-start = (bf16[384,1024]{1,0:T(8,128)(2,1)}, bf16[384,1024]{1,0:T(8,128)(2,1)}, u32[]{:S(2)}, u32[]{:S(2)}) collective-permute-start(bf16[384,1024]{1,0:T(8,128)(2,1)} %get-tuple-element.25), channel_id=1, source_target_pairs={{0,1},{1,0},{2,3},{3,2},{4,5},{5,4},{6,7},{7,6},{8,9},{9,8},{10,11... | collective-permute-start | bytes 2359304 | tf_op jit(solution)/shard_map/ppermute | solution.py:404
  7.3 3.7 %collective-permute-start.1 = (s32[2,6]{1,0:T(2,128)S(1)}, s32[2,6]{1,0:T(2,128)S(1)}, u32[]{:S(2)}, u32[]{:S(2)}) collective-permute-start(s32[2,6]{1,0:T(2,128)S(1)} %copy-done.6), channel_id=1, source_target_pairs={{8,0},{12,4},{0,8},{4,12},{9,1},{13,5},{1,9},{5,13},{10,2},{14,6},... | collective-permute-start | bytes 152 | tf_op jit(solution)/shard_map/ppermute | solution.py:484
  11.0 0.4 shard_map.137.pool_ref
  11.3 0.0 copy-start.12
  11.4 1.3 %dynamic-slice_bitcast_fusion.refs_0_ = bf16[3,512,256]{2,1,0:T(8,128)(2,1)S(1)} fusion(bf16[3,3,3,512,256]{4,3,2,1,0:T(8,128)(2,1)} %dilated_ref.1, s32[]{:T(128)S(6)} %select_n.5), kind=kLoop, calls=%fused_computation.1 | loop fusion | bytes 1572868 | tf_op jit(solution)/shard_map/squeeze | solution.py:504
  12.6 0.0 collective-permute-done
  12.7 0.1 copy-done.12
  12.8 1.4 %add_convert_fusion = bf16[384,1024]{1,0:T(8,128)(2,1)S(1)} fusion(bf16[384,1024]{1,0:T(8,128)(2,1)} %collective-permute-done, bf16[384,1024]{1,0:T(8,128)(2,1)S(1)} %copy-done.12), kind=kLoop, calls=%fused_computation | loop fusion | flops 1572864 | bytes 2359296 | tf_op jit(solution)/shard_map/convert_element_type | solution.py:408
  14.2 0.9 %fusion = (bf16[192,1024]{1,0:T(8,128)(2,1)}, bf16[192,1024]{1,0:T(8,128)(2,1)}) fusion(bf16[384,1024]{1,0:T(8,128)(2,1)S(1)} %add_convert_fusion), kind=kLoop, calls=%fused_computation.4 | loop fusion | bytes 1572864 | tf_op jit(solution)/shard_map/slice | solution.py:410
  15.1 0.0 copy-start.8
  15.1 0.0 copy-start.11
  15.1 0.9 %shard_map.138 = (bf16[416,256]{1,0:T(8,128)(2,1)S(1)}, bf16[416,256]{1,0:T(8,128)(2,1)S(1)}) custom-call(s32[1,2,6]{2,1,0:T(2,128)S(1)} %bitcast.7, bf16[16,256]{1,0:T(8,128)(2,1)S(1)} %shard_map.137.pool_ref, bf16[2,6,96,512]{3,2,1,0:T(8,128)(2,1)S(1)} %copy-done, bf16[3,512,256]{2,1,0:T(8,128)(2,1)S(1)} %dynamic-slice_bitcast_fusion.refs_0_), custom_call_target="tpu_custom_call" | custom-call | flops 1024 | bytes 1024 | tf_op jit(solution)/shard_map/pallas_call | solution.py:259
  16.1 0.2 collective-permute-start.2
  16.3 1.3 %collective-permute-done.2 = bf16[416,256]{1,0:T(8,128)(2,1)S(1)} collective-permute-done((bf16[416,256]{1,0:T(8,128)(2,1)S(1)}, bf16[416,256]{1,0:T(8,128)(2,1)S(1)}, u32[]{:S(2)}, u32[]{:S(2)}) %collective-permute-start.2) | collective-permute-done | bytes 213024 | tf_op jit(solution)/shard_map/ppermute | solution.py:404
  17.6 0.1 add_convert_fusion.1
  17.7 1.6 %collective-permute-start.3 = (bf16[208,256]{1,0:T(8,128)(2,1)S(1)}, bf16[208,256]{1,0:T(8,128)(2,1)S(1)}, u32[]{:S(2)}, u32[]{:S(2)}) collective-permute-start(bf16[208,256]{1,0:T(8,128)(2,1)S(1)} %get-tuple-element.41), channel_id=1, source_target_pairs={{0,2},{1,3},{2,0},{3,1},{4,6},{5,7},{6,4},{7,5},{8,10},{9,11},{10,... | collective-permute-start | bytes 319496 | tf_op jit(solution)/shard_map/ppermute | solution.py:404
  19.2 0.5 %collective-permute-start.6 = (bf16[192,1024]{1,0:T(8,128)(2,1)}, bf16[192,1024]{1,0:T(8,128)(2,1)S(1)}, u32[]{:S(2)}, u32[]{:S(2)}) collective-permute-start(bf16[192,1024]{1,0:T(8,128)(2,1)} %get-tuple-element.39), channel_id=1, source_target_pairs={{0,2},{1,3},{2,0},{3,1},{4,6},{5,7},{6,4},{7,5},{8,10},{9,11},{10,... | collective-permute-start | bytes 1179656 | tf_op jit(solution)/shard_map/ppermute | solution.py:404
  19.8 3.8 %collective-permute-done.3.moved_ref = bf16[208,256]{1,0:T(8,128)(2,1)S(1)} collective-permute-done((bf16[208,256]{1,0:T(8,128)(2,1)S(1)}, bf16[208,256]{1,0:T(8,128)(2,1)S(1)}, u32[]{:S(2)}, u32[]{:S(2)}) %collective-permute-start.3) | collective-permute-done | bytes 106528 | tf_op jit(solution)/shard_map/ppermute | solution.py:404
  23.6 1.6 %collective-permute-start.4 = (bf16[208,256]{1,0:T(8,128)(2,1)S(1)}, bf16[208,256]{1,0:T(8,128)(2,1)S(1)}, u32[]{:S(2)}, u32[]{:S(2)}) collective-permute-start(bf16[208,256]{1,0:T(8,128)(2,1)S(1)} %get-tuple-element.32), channel_id=1, source_target_pairs={{0,4},{4,0},{8,12},{12,8},{1,5},{5,1},{9,13},{13,9},{2,6},{6,2},{1... | collective-permute-start | bytes 319496 | tf_op jit(solution)/shard_map/ppermute | solution.py:438
  25.2 0.7 %collective-permute-start.7 = (bf16[208,256]{1,0:T(8,128)(2,1)S(1)}, bf16[208,256]{1,0:T(8,128)(2,1)S(1)}, u32[]{:S(2)}, u32[]{:S(2)}) collective-permute-start(bf16[208,256]{1,0:T(8,128)(2,1)S(1)} %get-tuple-element.36), channel_id=1, source_target_pairs={{0,8},{4,12},{8,0},{12,4},{1,9},{5,13},{9,1},{13,5},{2,10},{6,14},... | collective-permute-start | bytes 319496 | tf_op jit(solution)/shard_map/ppermute | solution.py:524
  26.0 0.7 %collective-permute-start.5 = (bf16[192,256]{1,0:T(8,128)(2,1)S(1)}, bf16[192,256]{1,0:T(8,128)(2,1)S(1)}, u32[]{:S(2)}, u32[]{:S(2)}) collective-permute-start(bf16[192,256]{1,0:T(8,128)(2,1)S(1)} %get-tuple-element.33), channel_id=1, source_target_pairs={{4,8},{8,4},{5,9},{9,5},{6,10},{10,6},{7,11},{11,7},{20,24},{24,20... | collective-permute-start | bytes 294920 | tf_op jit(solution)/shard_map/ppermute | solution.py:438
  26.7 2.1 %collective-permute-start.8 = (bf16[16,256]{1,0:T(8,128)(2,1)S(1)}, bf16[16,256]{1,0:T(8,128)(2,1)S(1)}, u32[]{:S(2)}, u32[]{:S(2)}) collective-permute-start(bf16[16,256]{1,0:T(8,128)(2,1)S(1)} %slice.57), channel_id=1, source_target_pairs={{0,12},{4,8},{8,4},{12,0},{1,13},{5,9},{9,5},{13,1},{2,14},{6,10},... | collective-permute-start | bytes 24584 | tf_op jit(solution)/shard_map/ppermute | solution.py:404
  28.8 0.1 copy.15.reduce_ref
  28.9 0.0 collective-permute-done.5.second_ref
  28.9 0.7 %collective-permute-done.4.first_ref = bf16[208,256]{1,0:T(8,128)(2,1)S(1)} collective-permute-done((bf16[208,256]{1,0:T(8,128)(2,1)S(1)}, bf16[208,256]{1,0:T(8,128)(2,1)S(1)}, u32[]{:S(2)}, u32[]{:S(2)}) %collective-permute-start.4) | collective-permute-done | bytes 106528 | tf_op jit(solution)/shard_map/ppermute | solution.py:438
  29.6 0.0 copy-start.4
  29.6 0.0 copy-start.7
  29.6 0.0 copy-start.9
  29.6 0.0 copy-start.10
  29.6 1.3 %shard_map.140.low_ref = f32[2,6,96,256]{3,2,1,0:T(8,128)S(1)} custom-call(bf16[2,6,96,256]{3,2,1,0:T(8,128)(2,1)S(1)} %copy-done.2, bf16[208,256]{1,0:T(8,128)(2,1)S(1)} %collective-permute-done.4.first_ref, bf16[192,256]{1,0:T(8,128)(2,1)S(1)} %collective-permute-done.5.second_ref, bf16[256,48]{1,0:T(8,128)(2,1)S(1)} %copy.15.reduce_ref, ...), custom_call_target="tpu_custom_call" | custom-call | flops 1024 | bytes 1024 | tf_op jit(solution)/shard_map/pallas_call | solution.py:536
  31.0 1.3 %collective-permute-done.8 = bf16[16,256]{1,0:T(8,128)(2,1)S(1)} collective-permute-done((bf16[16,256]{1,0:T(8,128)(2,1)S(1)}, bf16[16,256]{1,0:T(8,128)(2,1)S(1)}, u32[]{:S(2)}, u32[]{:S(2)}) %collective-permute-start.8) | collective-permute-done | bytes 8224 | tf_op jit(solution)/shard_map/ppermute | solution.py:404
  32.3 0.5 %collective-permute-done.7.refs_0_ = bf16[208,256]{1,0:T(8,128)(2,1)S(1)} collective-permute-done((bf16[208,256]{1,0:T(8,128)(2,1)S(1)}, bf16[208,256]{1,0:T(8,128)(2,1)S(1)}, u32[]{:S(2)}, u32[]{:S(2)}) %collective-permute-start.7) | collective-permute-done | bytes 106528 | tf_op jit(solution)/shard_map/ppermute | solution.py:524
  32.8 0.0 collective-permute-done.6.moved_ref
  32.8 0.3 shard_map.141
  33.2 1.5 %collective-permute-start.10 = (bf16[192,256]{1,0:T(8,128)(2,1)S(1)}, bf16[192,256]{1,0:T(8,128)(2,1)S(1)}, u32[]{:S(2)}, u32[]{:S(2)}) collective-permute-start(bf16[192,256]{1,0:T(8,128)(2,1)S(1)} %get-tuple-element.37.refs_0_), channel_id=1, source_target_pairs={{0,2},{1,3},{2,0},{3,1},{4,6},{5,7},{6,4},{7,5},{8,10},{9,11},{10,... | collective-permute-start | bytes 294920 | tf_op jit(solution)/shard_map/ppermute | solution.py:404
  34.7 0.7 %collective-permute-start.12 = (bf16[96,256]{1,0:T(8,128)(2,1)S(1)}, bf16[96,256]{1,0:T(8,128)(2,1)S(1)}, u32[]{:S(2)}, u32[]{:S(2)}) collective-permute-start(bf16[96,256]{1,0:T(8,128)(2,1)S(1)} %get-tuple-element.38), channel_id=1, source_target_pairs={{1,4},{4,1},{5,8},{8,5},{9,12},{12,9},{3,6},{6,3},{7,10},{10,7},{1... | collective-permute-start | bytes 147464 | tf_op jit(solution)/shard_map/ppermute | solution.py:430
  35.4 4.5 %collective-permute-start.9 = (bf16[192,256]{1,0:T(8,128)(2,1)S(1)}, bf16[192,256]{1,0:T(8,128)(2,1)S(1)}, u32[]{:S(2)}, u32[]{:S(2)}) collective-permute-start(bf16[192,256]{1,0:T(8,128)(2,1)S(1)} %get-tuple-element.37.refs_0_), channel_id=1, source_target_pairs={{0,1},{1,0},{2,3},{3,2},{4,5},{5,4},{6,7},{7,6},{8,9},{9,8},{10,11... | collective-permute-start | bytes 294920 | tf_op jit(solution)/shard_map/ppermute | solution.py:404
  39.9 0.0 collective-permute-done.12.refs_4_
  39.9 0.5 %collective-permute-start.14 = (bf16[96,256]{1,0:T(8,128)(2,1)S(1)}, bf16[96,256]{1,0:T(8,128)(2,1)S(1)}, u32[]{:S(2)}, u32[]{:S(2)}) collective-permute-start(bf16[96,256]{1,0:T(8,128)(2,1)S(1)} %collective-permute-done.12.refs_4_), channel_id=1, source_target_pairs={{0,2},{1,3},{2,0},{3,1},{4,6},{5,7},{6,4},{7,5},{8,10},{9,11},{10,... | collective-permute-start | bytes 147464 | tf_op jit(solution)/shard_map/ppermute | solution.py:404
  40.4 0.0 collective-permute-done.10.refs_2_
  40.4 1.4 %collective-permute-start.11 = (bf16[192,256]{1,0:T(8,128)(2,1)S(1)}, bf16[192,256]{1,0:T(8,128)(2,1)S(1)}, u32[]{:S(2)}, u32[]{:S(2)}) collective-permute-start(bf16[192,256]{1,0:T(8,128)(2,1)S(1)} %collective-permute-done.10.refs_2_), channel_id=1, source_target_pairs={{0,1},{1,0},{2,3},{3,2},{4,5},{5,4},{6,7},{7,6},{8,9},{9,8},{10,11... | collective-permute-start | bytes 294920 | tf_op jit(solution)/shard_map/ppermute | solution.py:404
  41.8 0.0 collective-permute-start.13
  41.8 2.1 %collective-permute-done.14.refs_6_ = bf16[96,256]{1,0:T(8,128)(2,1)S(1)} collective-permute-done((bf16[96,256]{1,0:T(8,128)(2,1)S(1)}, bf16[96,256]{1,0:T(8,128)(2,1)S(1)}, u32[]{:S(2)}, u32[]{:S(2)}) %collective-permute-start.14) | collective-permute-done | bytes 49184 | tf_op jit(solution)/shard_map/ppermute | solution.py:404
  44.0 0.5 %collective-permute-start.15 = (bf16[96,256]{1,0:T(8,128)(2,1)S(1)}, bf16[96,256]{1,0:T(8,128)(2,1)S(1)}, u32[]{:S(2)}, u32[]{:S(2)}) collective-permute-start(bf16[96,256]{1,0:T(8,128)(2,1)S(1)} %collective-permute-done.14.refs_6_), channel_id=1, source_target_pairs={{0,1},{1,0},{2,3},{3,2},{4,5},{5,4},{6,7},{7,6},{8,9},{9,8},{10,11... | collective-permute-start | bytes 147464 | tf_op jit(solution)/shard_map/ppermute | solution.py:404
  44.5 0.0 collective-permute-done.13.refs_5_
  44.5 0.9 %collective-permute-done.15.refs_7_ = bf16[96,256]{1,0:T(8,128)(2,1)S(1)} collective-permute-done((bf16[96,256]{1,0:T(8,128)(2,1)S(1)}, bf16[96,256]{1,0:T(8,128)(2,1)S(1)}, u32[]{:S(2)}, u32[]{:S(2)}) %collective-permute-start.15) | collective-permute-done | bytes 49184 | tf_op jit(solution)/shard_map/ppermute | solution.py:404
  45.4 2.4 %shard_map.142 = bf16[2,6,96,256]{3,2,1,0:T(8,128)(2,1)} custom-call(s32[2,6]{1,0:T(2,128)S(1)} %copy-done.6, f32[2,6,96,256]{3,2,1,0:T(8,128)S(1)} %shard_map.140.low_ref, bf16[3,3,304,256]{3,2,1,0:T(8,128)(2,1)S(1)} %copy-done.1, bf16[192,256]{1,0:T(8,128)(2,1)S(1)} %get-tuple-element.37.refs_0_, bf16[192,256]{1,0:T(8,128)(2,1)S(1)} %collective-permute-done.9.refs_1_, ...), custom_call_target="tpu_custom_call" | custom-call | flops 1024 | bytes 1024 | tf_op jit(solution)/shard_map/pallas_call | solution.py:572
  (27 shorter events, 0.1 us)
Async XLA Ops:
  0.0 11.0 %copy-start = (bf16[2,6,96,512]{3,2,1,0:T(8,128)(2,1)S(1)}, bf16[2,6,96,512]{3,2,1,0:T(8,128)(2,1)}, u32[]{:S(2)}) copy-start(bf16[2,6,96,512]{3,2,1,0:T(8,128)(2,1)} %features_ref.3) | copy-start | bytes 3538948
  0.0 7.3 %copy-start.6 = (s32[2,6]{1,0:T(2,128)S(1)}, s32[2,6]{1,0:T(2,128)}, u32[]{:S(2)}) copy-start(s32[2,6]{1,0:T(2,128)} %mask_ref.5) | copy-start | bytes 148
  0.0 11.0 %copy-start.5 = (bf16[512,256]{1,0:T(8,128)(2,1)S(1)}, bf16[512,256]{1,0:T(8,128)(2,1)}, u32[]{:S(2)}) copy-start(bf16[512,256]{1,0:T(8,128)(2,1)} %weight_ref.3) | copy-start | bytes 786436
  6.8 5.9 %collective-permute-start = (bf16[384,1024]{1,0:T(8,128)(2,1)}, bf16[384,1024]{1,0:T(8,128)(2,1)}, u32[]{:S(2)}, u32[]{:S(2)}) collective-permute-start(bf16[384,1024]{1,0:T(8,128)(2,1)} %get-tuple-element.25), channel_id=1, source_target_pairs={{0,1},{1,0},{2,3},{3,2},{4,5},{5,4},{6,7},{7,6},{8,9},{9,8},{10,11... | collective-permute-start | bytes 2359304 | tf_op jit(solution)/shard_map/ppermute | solution.py:404
  7.3 7.8 %collective-permute-start.1 = (s32[2,6]{1,0:T(2,128)S(1)}, s32[2,6]{1,0:T(2,128)S(1)}, u32[]{:S(2)}, u32[]{:S(2)}) collective-permute-start(s32[2,6]{1,0:T(2,128)S(1)} %copy-done.6), channel_id=1, source_target_pairs={{8,0},{12,4},{0,8},{4,12},{9,1},{13,5},{1,9},{5,13},{10,2},{14,6},... | collective-permute-start | bytes 152 | tf_op jit(solution)/shard_map/ppermute | solution.py:484
  11.3 1.4 %copy-start.12 = (bf16[384,1024]{1,0:T(8,128)(2,1)S(1)}, bf16[384,1024]{1,0:T(8,128)(2,1)}, u32[]{:S(2)}) copy-start(bf16[384,1024]{1,0:T(8,128)(2,1)} %get-tuple-element.24) | copy-start | bytes 2359300
  15.1 8.4 %copy-start.2 = (bf16[2,6,96,256]{3,2,1,0:T(8,128)(2,1)S(1)}, bf16[2,6,96,256]{3,2,1,0:T(8,128)(2,1)}, u32[]{:S(2)}) copy-start(bf16[2,6,96,256]{3,2,1,0:T(8,128)(2,1)} %low_ref.1) | copy-start | bytes 1769476
  15.1 13.7 %copy-start.13 = (bf16[256,48]{0,1:T(8,128)(2,1)S(1)}, bf16[256,48]{0,1:T(8,128)(2,1)}, u32[]{:S(2)}) copy-start(bf16[256,48]{0,1:T(8,128)(2,1)} %param.24) | copy-start | bytes 73732
  15.1 14.5 %copy-start.1 = (bf16[3,3,304,256]{3,2,1,0:T(8,128)(2,1)S(1)}, bf16[3,3,304,256]{3,2,1,0:T(8,128)(2,1)}, u32[]{:S(2)}) copy-start(bf16[3,3,304,256]{3,2,1,0:T(8,128)(2,1)} %weight_ref.5) | copy-start | bytes 4202500
  15.1 14.5 %copy-start.8 = (f32[256]{0:T(256)S(1)}, f32[256]{0:T(256)}, u32[]{:S(2)}) copy-start(f32[256]{0:T(256)} %param.27) | copy-start | bytes 3076
  15.1 14.4 %copy-start.11 = (f32[48]{0:T(128)S(1)}, f32[48]{0:T(128)}, u32[]{:S(2)}) copy-start(f32[48]{0:T(128)} %param.25) | copy-start | bytes 580
  16.1 1.5 %collective-permute-start.2 = (bf16[416,256]{1,0:T(8,128)(2,1)S(1)}, bf16[416,256]{1,0:T(8,128)(2,1)S(1)}, u32[]{:S(2)}, u32[]{:S(2)}) collective-permute-start(bf16[416,256]{1,0:T(8,128)(2,1)S(1)} %get-tuple-element.31), channel_id=1, source_target_pairs={{0,1},{1,0},{2,3},{3,2},{4,5},{5,4},{6,7},{7,6},{8,9},{9,8},{10,11... | collective-permute-start | bytes 638984 | tf_op jit(solution)/shard_map/ppermute | solution.py:404
  17.7 5.9 %collective-permute-start.3 = (bf16[208,256]{1,0:T(8,128)(2,1)S(1)}, bf16[208,256]{1,0:T(8,128)(2,1)S(1)}, u32[]{:S(2)}, u32[]{:S(2)}) collective-permute-start(bf16[208,256]{1,0:T(8,128)(2,1)S(1)} %get-tuple-element.41), channel_id=1, source_target_pairs={{0,2},{1,3},{2,0},{3,1},{4,6},{5,7},{6,4},{7,5},{8,10},{9,11},{10,... | collective-permute-start | bytes 319496 | tf_op jit(solution)/shard_map/ppermute | solution.py:404
  19.2 13.5 %collective-permute-start.6 = (bf16[192,1024]{1,0:T(8,128)(2,1)}, bf16[192,1024]{1,0:T(8,128)(2,1)S(1)}, u32[]{:S(2)}, u32[]{:S(2)}) collective-permute-start(bf16[192,1024]{1,0:T(8,128)(2,1)} %get-tuple-element.39), channel_id=1, source_target_pairs={{0,2},{1,3},{2,0},{3,1},{4,6},{5,7},{6,4},{7,5},{8,10},{9,11},{10,... | collective-permute-start | bytes 1179656 | tf_op jit(solution)/shard_map/ppermute | solution.py:404
  23.6 6.0 %collective-permute-start.4 = (bf16[208,256]{1,0:T(8,128)(2,1)S(1)}, bf16[208,256]{1,0:T(8,128)(2,1)S(1)}, u32[]{:S(2)}, u32[]{:S(2)}) collective-permute-start(bf16[208,256]{1,0:T(8,128)(2,1)S(1)} %get-tuple-element.32), channel_id=1, source_target_pairs={{0,4},{4,0},{8,12},{12,8},{1,5},{5,1},{9,13},{13,9},{2,6},{6,2},{1... | collective-permute-start | bytes 319496 | tf_op jit(solution)/shard_map/ppermute | solution.py:438
  25.2 7.5 %collective-permute-start.7 = (bf16[208,256]{1,0:T(8,128)(2,1)S(1)}, bf16[208,256]{1,0:T(8,128)(2,1)S(1)}, u32[]{:S(2)}, u32[]{:S(2)}) collective-permute-start(bf16[208,256]{1,0:T(8,128)(2,1)S(1)} %get-tuple-element.36), channel_id=1, source_target_pairs={{0,8},{4,12},{8,0},{12,4},{1,9},{5,13},{9,1},{13,5},{2,10},{6,14},... | collective-permute-start | bytes 319496 | tf_op jit(solution)/shard_map/ppermute | solution.py:524
  26.0 2.9 %collective-permute-start.5 = (bf16[192,256]{1,0:T(8,128)(2,1)S(1)}, bf16[192,256]{1,0:T(8,128)(2,1)S(1)}, u32[]{:S(2)}, u32[]{:S(2)}) collective-permute-start(bf16[192,256]{1,0:T(8,128)(2,1)S(1)} %get-tuple-element.33), channel_id=1, source_target_pairs={{4,8},{8,4},{5,9},{9,5},{6,10},{10,6},{7,11},{11,7},{20,24},{24,20... | collective-permute-start | bytes 294920 | tf_op jit(solution)/shard_map/ppermute | solution.py:438
  26.7 5.6 %collective-permute-start.8 = (bf16[16,256]{1,0:T(8,128)(2,1)S(1)}, bf16[16,256]{1,0:T(8,128)(2,1)S(1)}, u32[]{:S(2)}, u32[]{:S(2)}) collective-permute-start(bf16[16,256]{1,0:T(8,128)(2,1)S(1)} %slice.57), channel_id=1, source_target_pairs={{0,12},{4,8},{8,4},{12,0},{1,13},{5,9},{9,5},{13,1},{2,14},{6,10},... | collective-permute-start | bytes 24584 | tf_op jit(solution)/shard_map/ppermute | solution.py:404
  29.6 3.2 %copy-start.3 = (bf16[192,1024]{1,0:T(8,128)(2,1)S(1)}, bf16[192,1024]{1,0:T(8,128)(2,1)}, u32[]{:S(2)}) copy-start(bf16[192,1024]{1,0:T(8,128)(2,1)} %get-tuple-element.35.keep_ref) | copy-start | bytes 1179652
  29.6 3.2 %copy-start.4 = (bf16[1280,256]{1,0:T(8,128)(2,1)S(1)}, bf16[1280,256]{1,0:T(8,128)(2,1)}, u32[]{:S(2)}) copy-start(bf16[1280,256]{1,0:T(8,128)(2,1)} %weight_ref.4) | copy-start | bytes 1966084
  29.6 3.2 %copy-start.7 = (f32[4,256]{1,0:T(4,128)S(1)}, f32[4,256]{1,0:T(4,128)}, u32[]{:S(2)}) copy-start(f32[4,256]{1,0:T(4,128)} %bias_branch_ref.1) | copy-start | bytes 12292
  29.6 3.2 %copy-start.9 = (f32[256]{0:T(256)S(1)}, f32[256]{0:T(256)}, u32[]{:S(2)}) copy-start(f32[256]{0:T(256)} %param.21) | copy-start | bytes 3076
  29.6 3.2 %copy-start.10 = (f32[256]{0:T(256)S(1)}, f32[256]{0:T(256)}, u32[]{:S(2)}) copy-start(f32[256]{0:T(256)} %param.23) | copy-start | bytes 3076
  33.2 7.2 %collective-permute-start.10 = (bf16[192,256]{1,0:T(8,128)(2,1)S(1)}, bf16[192,256]{1,0:T(8,128)(2,1)S(1)}, u32[]{:S(2)}, u32[]{:S(2)}) collective-permute-start(bf16[192,256]{1,0:T(8,128)(2,1)S(1)} %get-tuple-element.37.refs_0_), channel_id=1, source_target_pairs={{0,2},{1,3},{2,0},{3,1},{4,6},{5,7},{6,4},{7,5},{8,10},{9,11},{10,... | collective-permute-start | bytes 294920 | tf_op jit(solution)/shard_map/ppermute | solution.py:404
  34.7 5.1 %collective-permute-start.12 = (bf16[96,256]{1,0:T(8,128)(2,1)S(1)}, bf16[96,256]{1,0:T(8,128)(2,1)S(1)}, u32[]{:S(2)}, u32[]{:S(2)}) collective-permute-start(bf16[96,256]{1,0:T(8,128)(2,1)S(1)} %get-tuple-element.38), channel_id=1, source_target_pairs={{1,4},{4,1},{5,8},{8,5},{9,12},{12,9},{3,6},{6,3},{7,10},{10,7},{1... | collective-permute-start | bytes 147464 | tf_op jit(solution)/shard_map/ppermute | solution.py:430
  35.4 9.1 %collective-permute-start.9 = (bf16[192,256]{1,0:T(8,128)(2,1)S(1)}, bf16[192,256]{1,0:T(8,128)(2,1)S(1)}, u32[]{:S(2)}, u32[]{:S(2)}) collective-permute-start(bf16[192,256]{1,0:T(8,128)(2,1)S(1)} %get-tuple-element.37.refs_0_), channel_id=1, source_target_pairs={{0,1},{1,0},{2,3},{3,2},{4,5},{5,4},{6,7},{7,6},{8,9},{9,8},{10,11... | collective-permute-start | bytes 294920 | tf_op jit(solution)/shard_map/ppermute | solution.py:404
  39.9 4.1 %collective-permute-start.14 = (bf16[96,256]{1,0:T(8,128)(2,1)S(1)}, bf16[96,256]{1,0:T(8,128)(2,1)S(1)}, u32[]{:S(2)}, u32[]{:S(2)}) collective-permute-start(bf16[96,256]{1,0:T(8,128)(2,1)S(1)} %collective-permute-done.12.refs_4_), channel_id=1, source_target_pairs={{0,2},{1,3},{2,0},{3,1},{4,6},{5,7},{6,4},{7,5},{8,10},{9,11},{10,... | collective-permute-start | bytes 147464 | tf_op jit(solution)/shard_map/ppermute | solution.py:404
  40.4 5.0 %collective-permute-start.11 = (bf16[192,256]{1,0:T(8,128)(2,1)S(1)}, bf16[192,256]{1,0:T(8,128)(2,1)S(1)}, u32[]{:S(2)}, u32[]{:S(2)}) collective-permute-start(bf16[192,256]{1,0:T(8,128)(2,1)S(1)} %collective-permute-done.10.refs_2_), channel_id=1, source_target_pairs={{0,1},{1,0},{2,3},{3,2},{4,5},{5,4},{6,7},{7,6},{8,9},{9,8},{10,11... | collective-permute-start | bytes 294920 | tf_op jit(solution)/shard_map/ppermute | solution.py:404
  41.8 2.7 %collective-permute-start.13 = (bf16[96,256]{1,0:T(8,128)(2,1)S(1)}, bf16[96,256]{1,0:T(8,128)(2,1)S(1)}, u32[]{:S(2)}, u32[]{:S(2)}) collective-permute-start(bf16[96,256]{1,0:T(8,128)(2,1)S(1)} %collective-permute-done.12.refs_4_), channel_id=1, source_target_pairs={{0,1},{1,0},{2,3},{3,2},{4,5},{5,4},{6,7},{7,6},{8,9},{9,8},{10,11... | collective-permute-start | bytes 147464 | tf_op jit(solution)/shard_map/ppermute | solution.py:404
  44.0 1.4 %collective-permute-start.15 = (bf16[96,256]{1,0:T(8,128)(2,1)S(1)}, bf16[96,256]{1,0:T(8,128)(2,1)S(1)}, u32[]{:S(2)}, u32[]{:S(2)}) collective-permute-start(bf16[96,256]{1,0:T(8,128)(2,1)S(1)} %collective-permute-done.14.refs_6_), channel_id=1, source_target_pairs={{0,1},{1,0},{2,3},{3,2},{4,5},{5,4},{6,7},{7,6},{8,9},{9,8},{10,11... | collective-permute-start | bytes 147464 | tf_op jit(solution)/shard_map/ppermute | solution.py:404

commit v4 on v3

--- a/solution.py
+++ b/solution.py
@@ -158,17 +158,23 @@
     out_ref[...] = parts_of(precise_dot(sums, weight_ref[...])).astype(BF16)
 
 
-def edge_kernel(plan, low_ref, keep_ref, moved_ref, far_ref, first_ref, second_ref):
+def copy_edges(plan, low_ref, out_ref, parity):
+    upper = lax.rem(lax.axis_index("band") + parity, 2) == 0
+    row = jnp.where(upper, plan.row_count - 1, 0)
+    for image in range(plan.batches):
+        out_ref[pl.ds(image * plan.columns, plan.columns)] = low_ref[image, row]
+
+
+def second_edge_kernel(plan, low_ref, out_ref):
+    copy_edges(plan, low_ref, out_ref, 1)
+
+
+def edge_kernel(plan, low_ref, keep_ref, moved_ref, far_ref, first_ref):
     far = keep_ref[...].astype(F32) + moved_ref[...].astype(F32)
     far_ref[...] = far.astype(BF16)
     cells, width = plan.batches * plan.columns, low_ref.shape[3]
     first_ref[pl.ds(cells, 2 * POOL_ROWS)] = far[plan.share :, :width].astype(BF16)
-    odd = lax.rem(lax.axis_index("band"), 2)
-    last = plan.row_count - 1
-    for image in range(plan.batches):
-        rows = pl.ds(image * plan.columns, plan.columns)
-        first_ref[rows] = low_ref[image, last - odd * last]
-        second_ref[rows] = low_ref[image, odd * last]
+    copy_edges(plan, low_ref, first_ref, 0)
 
 
 def fetch_taps(dilated_ref, branch, row_tap, taps_ref, index, sems):
@@ -430,12 +436,11 @@
     return lax.ppermute(edge, ("band", "sect"), pairs)
 
 
-def swap_low_edges(first, second, bands):
-    first_pairs = [(b, b ^ 1) for b in range(bands)]
-    second_pairs = []
-    for b in range(1, bands - 1, 2):
-        second_pairs += [(b, b + 1), (b + 1, b)]
-    return lax.ppermute(first, "band", first_pairs), lax.ppermute(second, "band", second_pairs)
+def border_pairs(bands):
+    pairs = []
+    for band in range(1, bands - 1, 2):
+        pairs += [(band, band + 1), (band + 1, band)]
+    return pairs
 
 
 def fits(batches, row_count, columns, bands, sects, low_depth, width):
@@ -503,16 +508,24 @@
         size = (1, 1) + weight_dilated.shape[2:]
         taps.append(lax.dynamic_slice(weight_dilated, start, size)[0, 0])
     far_keep, far_send = far_partials(plan, far_mask, pool, late_features, taps)
+    far_keep, far_send, late_low = lax.optimization_barrier((far_keep, far_send, late_low))
     for bit in range(plan.bits - 1):
         far_moved = swap(far_send, "sect", 1 << bit)
         far_keep, far_send = add_halves(far_keep, far_moved)
     far_moved = swap(far_send, "sect", plan.sects // 2)
-    far, first, second = call(
+    second = call(
+        functools.partial(second_edge_kernel, plan),
+        jax.ShapeDtypeStruct((batches * columns, width), BF16),
+        [VMEM],
+        [],
+    )(late_low)
+    second = lax.ppermute(second, "band", border_pairs(bands))
+    far_moved, second = lax.optimization_barrier((far_moved, second))
+    far, first = call(
         functools.partial(edge_kernel, plan),
         (
             jax.ShapeDtypeStruct(far_keep.shape, BF16),
             jax.ShapeDtypeStruct((batches * columns + 2 * POOL_ROWS, width), BF16),
-            jax.ShapeDtypeStruct((batches * columns, width), BF16),
         ),
         [VMEM] * 3,
         [],
@@ -523,7 +536,7 @@
         lanes = slice(term * width, (term + 1) * width)
         far_terms.append(lax.ppermute(rows[:, lanes], "band", pairs))
     own_pool = far[plan.share :, :width]
-    first, second = swap_low_edges(first, second, bands)
+    first = swap(first, "band", 1)
     pool = joined_parts(own_pool) + joined_parts(first[batches * columns :])
     if bands == 4 and any(2 * term[1] == bands for term in plan.terms):
         halves = [term for term, entry in enumerate(plan.terms) if 2 * entry[1] == bands]

time: 48.5 us -> 45.2 us (0.932)
  waiting for transfers between devices: 10.6 us -> 8.55 us
  other arithmetic: 1.49 us -> 0.37 us
    ppermute x11 -> x12, starting transfers between devices: 13.5 us -> 15.8 us  [swap(): return lax.ppermute(value, axis, [(i, i ^ pattern) for i in range(count)])]
    ppermute x11 -> x12, waiting for transfers between devices: 9.41 us -> 7.5 us  [swap(): return lax.ppermute(value, axis, [(i, i ^ pattern) for i in range(count)])]
    ppermute x2 -> x1, starting transfers between devices: 2.3 us -> 0.67 us  [shards(): second = lax.ppermute(second, 'band', border_pairs(bands))]
    convert_element_type x2, other arithmetic: 1.48 us -> 0.36 us  [add_halves(): total = (keep.astype(F32) + moved.astype(F32)).astype(BF16)]
    ppermute x2 -> x1, waiting for transfers between devices: 0.66 us -> 0.01 us  [shards(): second = lax.ppermute(second, 'band', border_pairs(bands))]
    ppermute x1, waiting for transfers between devices: 0.49 us -> 1.04 us  [shards(): far_terms.append(lax.ppermute(rows[:, lanes], 'band', pairs))]
    ppermute x1, starting transfers between devices: 0.75 us -> 0.22 us  [shards(): far_terms.append(lax.ppermute(rows[:, lanes], 'band', pairs))]
  transfers between devices with their start and end apart: 16 -> 16, of which waited for: 7 -> 7; matrix products, arithmetic and copies ran while one was open for 8% -> 6% of each run, Pallas kernels for 4% -> 4%
where the time goes in v4:
time: 45.2 us; the launch traced here: 44.6 us
  starting transfers between devices  21 us (46%)
  Pallas kernels  12.2 us (27%)
  waiting for transfers between devices  8.55 us (19%)
  local copies, waits for them, and re-layouts  2.23 us (5%)
    ppermute x12, starting transfers between devices, swap(): return lax.ppermute(value, axis, [(i, i ^ pattern) for i in range(count)])  15.8 us
    ppermute x12, waiting for transfers between devices, swap(): return lax.ppermute(value, axis, [(i, i ^ pattern) for i in range(count)])  7.5 us
    pallas_call x1, Pallas kernels, own_partials(): call(functools.partial(own_kernel, plan), (out, out), [HBM, HBM, HBM, HBM...  6.75 us
    ppermute x1, starting transfers between devices, shards(): lax.ppermute(late_mask, 'band', [(target, source) for source, target in p...  3.67 us
    pallas_call x1, Pallas kernels, shards(): call(functools.partial(merge_kernel, plan), jax.ShapeDtypeStruct(low_part...  2.44 us
    pallas_call x1, Pallas kernels, shards(): call(functools.partial(low_kernel, plan), jax.ShapeDtypeStruct((batches,...  1.33 us
    squeeze x1, local copies, waits for them, and re-layouts, shards(): taps.append(lax.dynamic_slice(weight_dilated, start, size)[0, 0])  1.23 us
    ppermute x1, waiting for transfers between devices, shards(): far_terms.append(lax.ppermute(rows[:, lanes], 'band', pairs))  1.04 us
  transfers between devices with their start and end apart: 16, of which 7 were waited for; matrix products, arithmetic and copies ran while one was open for 6% of the time, Pallas kernels for 4%

profile of v4, /device:TPU:0, one launch (start us, length us, event | category | flops | bytes accessed | tf_op | source)
XLA Modules:
  0.0 44.6 jit_solution(16178280326505721721)
XLA Ops:
  0.0 6.7 %shard_map.136 = (bf16[384,1024]{1,0:T(8,128)(2,1)}, bf16[384,1024]{1,0:T(8,128)(2,1)}) custom-call(s32[2,6]{1,0:T(2,128)} %mask_ref.5, bf16[2,6,96,512]{3,2,1,0:T(8,128)(2,1)} %features_ref.3, bf16[512,256]{1,0:T(8,128)(2,1)} %one_ref.1, bf16[3,3,3,512,256]{4,3,2,1,0:T(8,128)(2,1)} %dilated_ref.1), custom_call_target="tpu_custom_call" | custom-call | flops 1024 | bytes 1024 | tf_op jit(solution)/shard_map/pallas_call | solution.py:223
  6.8 0.5 %collective-permute-start = (bf16[384,1024]{1,0:T(8,128)(2,1)}, bf16[384,1024]{1,0:T(8,128)(2,1)S(1)}, u32[]{:S(2)}, u32[]{:S(2)}) collective-permute-start(bf16[384,1024]{1,0:T(8,128)(2,1)} %get-tuple-element.29), channel_id=1, source_target_pairs={{0,1},{1,0},{2,3},{3,2},{4,5},{5,4},{6,7},{7,6},{8,9},{9,8},{10,11... | collective-permute-start | bytes 2359304 | tf_op jit(solution)/shard_map/ppermute | solution.py:410
  7.3 3.7 %collective-permute-start.1 = (s32[2,6]{1,0:T(2,128)S(1)}, s32[2,6]{1,0:T(2,128)S(1)}, u32[]{:S(2)}, u32[]{:S(2)}) collective-permute-start(s32[2,6]{1,0:T(2,128)S(1)} %copy-done.5), channel_id=1, source_target_pairs={{8,0},{12,4},{0,8},{4,12},{9,1},{13,5},{1,9},{5,13},{10,2},{14,6},... | collective-permute-start | bytes 152 | tf_op jit(solution)/shard_map/ppermute | solution.py:489
  11.0 0.4 shard_map.137.pool_ref
  11.4 1.2 %dynamic-slice_bitcast_fusion.refs_0_ = bf16[3,512,256]{2,1,0:T(8,128)(2,1)S(1)} fusion(bf16[3,3,3,512,256]{4,3,2,1,0:T(8,128)(2,1)} %dilated_ref.1, s32[]{:T(128)S(6)} %select_n.5), kind=kLoop, calls=%fused_computation.1 | loop fusion | bytes 1572868 | tf_op jit(solution)/shard_map/squeeze | solution.py:509
  12.6 0.0 collective-permute-done
  12.6 0.3 add_convert_fusion
  12.9 0.8 %fusion = (bf16[192,1024]{1,0:T(8,128)(2,1)}, bf16[192,1024]{1,0:T(8,128)(2,1)S(1)}) fusion(bf16[384,1024]{1,0:T(8,128)(2,1)S(1)} %add_convert_fusion), kind=kLoop, calls=%fused_computation.4 | loop fusion | bytes 1572864 | tf_op jit(solution)/shard_map/slice | solution.py:416
  13.7 0.0 collective-permute-done.1
  13.7 0.9 %shard_map.138 = (bf16[416,256]{1,0:T(8,128)(2,1)S(1)}, bf16[416,256]{1,0:T(8,128)(2,1)S(1)}) custom-call(s32[1,2,6]{2,1,0:T(2,128)S(1)} %bitcast.7, bf16[16,256]{1,0:T(8,128)(2,1)S(1)} %shard_map.137.pool_ref, bf16[2,6,96,512]{3,2,1,0:T(8,128)(2,1)S(1)} %copy-done, bf16[3,512,256]{2,1,0:T(8,128)(2,1)S(1)} %dynamic-slice_bitcast_fusion.refs_0_), custom_call_target="tpu_custom_call" | custom-call | flops 1024 | bytes 1024 | tf_op jit(solution)/shard_map/pallas_call | solution.py:265
  14.6 0.0 copy-start.12
  14.6 0.0 copy-start.1
  14.7 0.0 copy-start.7
  14.7 0.0 copy-start.10
  14.7 0.2 collective-permute-start.2
  14.9 1.3 %collective-permute-done.2 = bf16[416,256]{1,0:T(8,128)(2,1)S(1)} collective-permute-done((bf16[416,256]{1,0:T(8,128)(2,1)S(1)}, bf16[416,256]{1,0:T(8,128)(2,1)S(1)}, u32[]{:S(2)}, u32[]{:S(2)}) %collective-permute-start.2) | collective-permute-done | bytes 213024 | tf_op jit(solution)/shard_map/ppermute | solution.py:410
  16.2 0.1 add_convert_fusion.1
  16.3 1.6 %collective-permute-start.3 = (bf16[208,256]{1,0:T(8,128)(2,1)S(1)}, bf16[208,256]{1,0:T(8,128)(2,1)S(1)}, u32[]{:S(2)}, u32[]{:S(2)}) collective-permute-start(bf16[208,256]{1,0:T(8,128)(2,1)S(1)} %get-tuple-element.49), channel_id=1, source_target_pairs={{0,2},{1,3},{2,0},{3,1},{4,6},{5,7},{6,4},{7,5},{8,10},{9,11},{10,... | collective-permute-start | bytes 319496 | tf_op jit(solution)/shard_map/ppermute | solution.py:410
  17.9 0.7 %collective-permute-start.4 = (bf16[192,256]{1,0:T(8,128)(2,1)S(1)}, bf16[192,256]{1,0:T(8,128)(2,1)S(1)}, u32[]{:S(2)}, u32[]{:S(2)}) collective-permute-start(bf16[192,256]{1,0:T(8,128)(2,1)S(1)} %shard_map.139), channel_id=1, source_target_pairs={{4,8},{8,4},{5,9},{9,5},{6,10},{10,6},{7,11},{11,7},{20,24},{24,20... | collective-permute-start | bytes 294920 | tf_op jit(solution)/shard_map/ppermute | solution.py:522
  18.5 0.6 %collective-permute-start.6 = (bf16[192,1024]{1,0:T(8,128)(2,1)}, bf16[192,1024]{1,0:T(8,128)(2,1)S(1)}, u32[]{:S(2)}, u32[]{:S(2)}) collective-permute-start(bf16[192,1024]{1,0:T(8,128)(2,1)} %get-tuple-element.47), channel_id=1, source_target_pairs={{0,2},{1,3},{2,0},{3,1},{4,6},{5,7},{6,4},{7,5},{8,10},{9,11},{10,... | collective-permute-start | bytes 1179656 | tf_op jit(solution)/shard_map/ppermute | solution.py:410
  19.1 2.3 %collective-permute-done.3.moved_ref = bf16[208,256]{1,0:T(8,128)(2,1)S(1)} collective-permute-done((bf16[208,256]{1,0:T(8,128)(2,1)S(1)}, bf16[208,256]{1,0:T(8,128)(2,1)S(1)}, u32[]{:S(2)}, u32[]{:S(2)}) %collective-permute-start.3) | collective-permute-done | bytes 106528 | tf_op jit(solution)/shard_map/ppermute | solution.py:410
  21.5 4.6 %collective-permute-start.5 = (bf16[208,256]{1,0:T(8,128)(2,1)S(1)}, bf16[208,256]{1,0:T(8,128)(2,1)S(1)}, u32[]{:S(2)}, u32[]{:S(2)}) collective-permute-start(bf16[208,256]{1,0:T(8,128)(2,1)S(1)} %get-tuple-element.40), channel_id=1, source_target_pairs={{0,4},{4,0},{8,12},{12,8},{1,5},{5,1},{9,13},{13,9},{2,6},{6,2},{1... | collective-permute-start | bytes 319496 | tf_op jit(solution)/shard_map/ppermute | solution.py:410
  26.1 0.2 collective-permute-start.7
  26.3 2.2 %collective-permute-start.8 = (bf16[16,256]{1,0:T(8,128)(2,1)S(1)}, bf16[16,256]{1,0:T(8,128)(2,1)S(1)}, u32[]{:S(2)}, u32[]{:S(2)}) collective-permute-start(bf16[16,256]{1,0:T(8,128)(2,1)S(1)} %slice.57), channel_id=1, source_target_pairs={{0,12},{4,8},{8,4},{12,0},{1,13},{5,9},{9,5},{13,1},{2,14},{6,10},... | collective-permute-start | bytes 24584 | tf_op jit(solution)/shard_map/ppermute | solution.py:410
  28.5 0.1 copy.15.reduce_ref
  28.6 0.3 collective-permute-done.5.first_ref
  28.9 0.0 copy-start.3
  28.9 0.0 copy-start.6
  28.9 0.0 copy-start.8
  29.0 0.0 copy-start.9
  29.0 1.3 %shard_map.141.low_ref = f32[2,6,96,256]{3,2,1,0:T(8,128)S(1)} custom-call(bf16[2,6,96,256]{3,2,1,0:T(8,128)(2,1)S(1)} %copy-done.2, bf16[208,256]{1,0:T(8,128)(2,1)S(1)} %collective-permute-done.5.first_ref, bf16[192,256]{1,0:T(8,128)(2,1)S(1)} %collective-permute-done.4.second_ref, bf16[256,48]{1,0:T(8,128)(2,1)S(1)} %copy.15.reduce_ref, ...), custom_call_target="tpu_custom_call" | custom-call | flops 1024 | bytes 1024 | tf_op jit(solution)/shard_map/pallas_call | solution.py:549
  30.3 1.5 %collective-permute-done.8 = bf16[16,256]{1,0:T(8,128)(2,1)S(1)} collective-permute-done((bf16[16,256]{1,0:T(8,128)(2,1)S(1)}, bf16[16,256]{1,0:T(8,128)(2,1)S(1)}, u32[]{:S(2)}, u32[]{:S(2)}) %collective-permute-start.8) | collective-permute-done | bytes 8224 | tf_op jit(solution)/shard_map/ppermute | solution.py:410
  31.8 1.0 %collective-permute-done.7.refs_0_ = bf16[208,256]{1,0:T(8,128)(2,1)S(1)} collective-permute-done((bf16[208,256]{1,0:T(8,128)(2,1)S(1)}, bf16[208,256]{1,0:T(8,128)(2,1)S(1)}, u32[]{:S(2)}, u32[]{:S(2)}) %collective-permute-start.7) | collective-permute-done | bytes 106528 | tf_op jit(solution)/shard_map/ppermute | solution.py:537
  32.9 0.3 shard_map.142
  33.3 0.6 %collective-permute-start.10 = (bf16[192,256]{1,0:T(8,128)(2,1)S(1)}, bf16[192,256]{1,0:T(8,128)(2,1)S(1)}, u32[]{:S(2)}, u32[]{:S(2)}) collective-permute-start(bf16[192,256]{1,0:T(8,128)(2,1)S(1)} %get-tuple-element.45.refs_0_), channel_id=1, source_target_pairs={{0,2},{1,3},{2,0},{3,1},{4,6},{5,7},{6,4},{7,5},{8,10},{9,11},{10,... | collective-permute-start | bytes 294920 | tf_op jit(solution)/shard_map/ppermute | solution.py:410
  33.9 0.7 %collective-permute-start.12 = (bf16[96,256]{1,0:T(8,128)(2,1)S(1)}, bf16[96,256]{1,0:T(8,128)(2,1)S(1)}, u32[]{:S(2)}, u32[]{:S(2)}) collective-permute-start(bf16[96,256]{1,0:T(8,128)(2,1)S(1)} %get-tuple-element.46), channel_id=1, source_target_pairs={{1,4},{4,1},{5,8},{8,5},{9,12},{12,9},{3,6},{6,3},{7,10},{10,7},{1... | collective-permute-start | bytes 147464 | tf_op jit(solution)/shard_map/ppermute | solution.py:436
  34.5 2.1 %collective-permute-start.9 = (bf16[192,256]{1,0:T(8,128)(2,1)S(1)}, bf16[192,256]{1,0:T(8,128)(2,1)S(1)}, u32[]{:S(2)}, u32[]{:S(2)}) collective-permute-start(bf16[192,256]{1,0:T(8,128)(2,1)S(1)} %get-tuple-element.45.refs_0_), channel_id=1, source_target_pairs={{0,1},{1,0},{2,3},{3,2},{4,5},{5,4},{6,7},{7,6},{8,9},{9,8},{10,11... | collective-permute-start | bytes 294920 | tf_op jit(solution)/shard_map/ppermute | solution.py:410
  36.6 0.0 collective-permute-done.12.refs_4_
  36.6 1.5 %collective-permute-start.14 = (bf16[96,256]{1,0:T(8,128)(2,1)S(1)}, bf16[96,256]{1,0:T(8,128)(2,1)S(1)}, u32[]{:S(2)}, u32[]{:S(2)}) collective-permute-start(bf16[96,256]{1,0:T(8,128)(2,1)S(1)} %collective-permute-done.12.refs_4_), channel_id=1, source_target_pairs={{0,2},{1,3},{2,0},{3,1},{4,6},{5,7},{6,4},{7,5},{8,10},{9,11},{10,... | collective-permute-start | bytes 147464 | tf_op jit(solution)/shard_map/ppermute | solution.py:410
  38.1 1.4 %collective-permute-start.11 = (bf16[192,256]{1,0:T(8,128)(2,1)S(1)}, bf16[192,256]{1,0:T(8,128)(2,1)S(1)}, u32[]{:S(2)}, u32[]{:S(2)}) collective-permute-start(bf16[192,256]{1,0:T(8,128)(2,1)S(1)} %collective-permute-done.10.refs_2_), channel_id=1, source_target_pairs={{0,1},{1,0},{2,3},{3,2},{4,5},{5,4},{6,7},{7,6},{8,9},{9,8},{10,11... | collective-permute-start | bytes 294920 | tf_op jit(solution)/shard_map/ppermute | solution.py:410
  39.5 0.0 collective-permute-start.13
  39.5 1.2 %collective-permute-done.14.refs_6_ = bf16[96,256]{1,0:T(8,128)(2,1)S(1)} collective-permute-done((bf16[96,256]{1,0:T(8,128)(2,1)S(1)}, bf16[96,256]{1,0:T(8,128)(2,1)S(1)}, u32[]{:S(2)}, u32[]{:S(2)}) %collective-permute-start.14) | collective-permute-done | bytes 49184 | tf_op jit(solution)/shard_map/ppermute | solution.py:410
  40.7 0.5 %collective-permute-start.15 = (bf16[96,256]{1,0:T(8,128)(2,1)S(1)}, bf16[96,256]{1,0:T(8,128)(2,1)S(1)}, u32[]{:S(2)}, u32[]{:S(2)}) collective-permute-start(bf16[96,256]{1,0:T(8,128)(2,1)S(1)} %collective-permute-done.14.refs_6_), channel_id=1, source_target_pairs={{0,1},{1,0},{2,3},{3,2},{4,5},{5,4},{6,7},{7,6},{8,9},{9,8},{10,11... | collective-permute-start | bytes 147464 | tf_op jit(solution)/shard_map/ppermute | solution.py:410
  41.3 0.0 collective-permute-done.13.refs_5_
  41.3 0.0 collective-permute-done.9.refs_1_
  41.3 0.9 %collective-permute-done.15.refs_7_ = bf16[96,256]{1,0:T(8,128)(2,1)S(1)} collective-permute-done((bf16[96,256]{1,0:T(8,128)(2,1)S(1)}, bf16[96,256]{1,0:T(8,128)(2,1)S(1)}, u32[]{:S(2)}, u32[]{:S(2)}) %collective-permute-start.15) | collective-permute-done | bytes 49184 | tf_op jit(solution)/shard_map/ppermute | solution.py:410
  42.1 0.0 collective-permute-done.11.refs_3_
  42.1 2.4 %shard_map.143 = bf16[2,6,96,256]{3,2,1,0:T(8,128)(2,1)} custom-call(s32[2,6]{1,0:T(2,128)S(1)} %copy-done.5, f32[2,6,96,256]{3,2,1,0:T(8,128)S(1)} %shard_map.141.low_ref, bf16[3,3,304,256]{3,2,1,0:T(8,128)(2,1)S(1)} %copy-done.1, bf16[192,256]{1,0:T(8,128)(2,1)S(1)} %get-tuple-element.45.refs_0_, bf16[192,256]{1,0:T(8,128)(2,1)S(1)} %collective-permute-done.9.refs_1_, ...), custom_call_target="tpu_custom_call" | custom-call | flops 1024 | bytes 1024 | tf_op jit(solution)/shard_map/pallas_call | solution.py:585
  (26 shorter events, 0.1 us)
Async XLA Ops:
  0.0 11.0 %copy-start = (bf16[2,6,96,512]{3,2,1,0:T(8,128)(2,1)S(1)}, bf16[2,6,96,512]{3,2,1,0:T(8,128)(2,1)}, u32[]{:S(2)}) copy-start(bf16[2,6,96,512]{3,2,1,0:T(8,128)(2,1)} %features_ref.3) | copy-start | bytes 3538948
  0.0 7.3 %copy-start.5 = (s32[2,6]{1,0:T(2,128)S(1)}, s32[2,6]{1,0:T(2,128)}, u32[]{:S(2)}) copy-start(s32[2,6]{1,0:T(2,128)} %mask_ref.5) | copy-start | bytes 148
  0.0 11.0 %copy-start.4 = (bf16[512,256]{1,0:T(8,128)(2,1)S(1)}, bf16[512,256]{1,0:T(8,128)(2,1)}, u32[]{:S(2)}) copy-start(bf16[512,256]{1,0:T(8,128)(2,1)} %weight_ref.3) | copy-start | bytes 786436
  6.8 5.8 %copy-start.11 = (bf16[384,1024]{1,0:T(8,128)(2,1)S(1)}, bf16[384,1024]{1,0:T(8,128)(2,1)}, u32[]{:S(2)}) copy-start(bf16[384,1024]{1,0:T(8,128)(2,1)} %get-tuple-element.28) | copy-start | bytes 2359300
  6.8 5.8 %collective-permute-start = (bf16[384,1024]{1,0:T(8,128)(2,1)}, bf16[384,1024]{1,0:T(8,128)(2,1)S(1)}, u32[]{:S(2)}, u32[]{:S(2)}) collective-permute-start(bf16[384,1024]{1,0:T(8,128)(2,1)} %get-tuple-element.29), channel_id=1, source_target_pairs={{0,1},{1,0},{2,3},{3,2},{4,5},{5,4},{6,7},{7,6},{8,9},{9,8},{10,11... | collective-permute-start | bytes 2359304 | tf_op jit(solution)/shard_map/ppermute | solution.py:410
  7.3 6.4 %collective-permute-start.1 = (s32[2,6]{1,0:T(2,128)S(1)}, s32[2,6]{1,0:T(2,128)S(1)}, u32[]{:S(2)}, u32[]{:S(2)}) collective-permute-start(s32[2,6]{1,0:T(2,128)S(1)} %copy-done.5), channel_id=1, source_target_pairs={{8,0},{12,4},{0,8},{4,12},{9,1},{13,5},{1,9},{5,13},{10,2},{14,6},... | collective-permute-start | bytes 152 | tf_op jit(solution)/shard_map/ppermute | solution.py:489
  13.7 4.1 %copy-start.2 = (bf16[2,6,96,256]{3,2,1,0:T(8,128)(2,1)S(1)}, bf16[2,6,96,256]{3,2,1,0:T(8,128)(2,1)}, u32[]{:S(2)}) copy-start(bf16[2,6,96,256]{3,2,1,0:T(8,128)(2,1)} %low_ref.2) | copy-start | bytes 1769476
  14.6 13.9 %copy-start.12 = (bf16[256,48]{0,1:T(8,128)(2,1)S(1)}, bf16[256,48]{0,1:T(8,128)(2,1)}, u32[]{:S(2)}) copy-start(bf16[256,48]{0,1:T(8,128)(2,1)} %param.24) | copy-start | bytes 73732
  14.6 14.3 %copy-start.1 = (bf16[3,3,304,256]{3,2,1,0:T(8,128)(2,1)S(1)}, bf16[3,3,304,256]{3,2,1,0:T(8,128)(2,1)}, u32[]{:S(2)}) copy-start(bf16[3,3,304,256]{3,2,1,0:T(8,128)(2,1)} %weight_ref.5) | copy-start | bytes 4202500
  14.7 14.3 %copy-start.7 = (f32[256]{0:T(256)S(1)}, f32[256]{0:T(256)}, u32[]{:S(2)}) copy-start(f32[256]{0:T(256)} %param.27) | copy-start | bytes 3076
  14.7 14.3 %copy-start.10 = (f32[48]{0:T(128)S(1)}, f32[48]{0:T(128)}, u32[]{:S(2)}) copy-start(f32[48]{0:T(128)} %param.25) | copy-start | bytes 580
  14.7 1.5 %collective-permute-start.2 = (bf16[416,256]{1,0:T(8,128)(2,1)S(1)}, bf16[416,256]{1,0:T(8,128)(2,1)S(1)}, u32[]{:S(2)}, u32[]{:S(2)}) collective-permute-start(bf16[416,256]{1,0:T(8,128)(2,1)S(1)} %get-tuple-element.38), channel_id=1, source_target_pairs={{0,1},{1,0},{2,3},{3,2},{4,5},{5,4},{6,7},{7,6},{8,9},{9,8},{10,11... | collective-permute-start | bytes 638984 | tf_op jit(solution)/shard_map/ppermute | solution.py:410
  16.3 5.2 %collective-permute-start.3 = (bf16[208,256]{1,0:T(8,128)(2,1)S(1)}, bf16[208,256]{1,0:T(8,128)(2,1)S(1)}, u32[]{:S(2)}, u32[]{:S(2)}) collective-permute-start(bf16[208,256]{1,0:T(8,128)(2,1)S(1)} %get-tuple-element.49), channel_id=1, source_target_pairs={{0,2},{1,3},{2,0},{3,1},{4,6},{5,7},{6,4},{7,5},{8,10},{9,11},{10,... | collective-permute-start | bytes 319496 | tf_op jit(solution)/shard_map/ppermute | solution.py:410
  17.9 1.3 %collective-permute-start.4 = (bf16[192,256]{1,0:T(8,128)(2,1)S(1)}, bf16[192,256]{1,0:T(8,128)(2,1)S(1)}, u32[]{:S(2)}, u32[]{:S(2)}) collective-permute-start(bf16[192,256]{1,0:T(8,128)(2,1)S(1)} %shard_map.139), channel_id=1, source_target_pairs={{4,8},{8,4},{5,9},{9,5},{6,10},{10,6},{7,11},{11,7},{20,24},{24,20... | collective-permute-start | bytes 294920 | tf_op jit(solution)/shard_map/ppermute | solution.py:522
  18.5 14.3 %collective-permute-start.6 = (bf16[192,1024]{1,0:T(8,128)(2,1)}, bf16[192,1024]{1,0:T(8,128)(2,1)S(1)}, u32[]{:S(2)}, u32[]{:S(2)}) collective-permute-start(bf16[192,1024]{1,0:T(8,128)(2,1)} %get-tuple-element.47), channel_id=1, source_target_pairs={{0,2},{1,3},{2,0},{3,1},{4,6},{5,7},{6,4},{7,5},{8,10},{9,11},{10,... | collective-permute-start | bytes 1179656 | tf_op jit(solution)/shard_map/ppermute | solution.py:410
  21.5 7.4 %collective-permute-start.5 = (bf16[208,256]{1,0:T(8,128)(2,1)S(1)}, bf16[208,256]{1,0:T(8,128)(2,1)S(1)}, u32[]{:S(2)}, u32[]{:S(2)}) collective-permute-start(bf16[208,256]{1,0:T(8,128)(2,1)S(1)} %get-tuple-element.40), channel_id=1, source_target_pairs={{0,4},{4,0},{8,12},{12,8},{1,5},{5,1},{9,13},{13,9},{2,6},{6,2},{1... | collective-permute-start | bytes 319496 | tf_op jit(solution)/shard_map/ppermute | solution.py:410
  26.1 6.8 %collective-permute-start.7 = (bf16[208,256]{1,0:T(8,128)(2,1)S(1)}, bf16[208,256]{1,0:T(8,128)(2,1)S(1)}, u32[]{:S(2)}, u32[]{:S(2)}) collective-permute-start(bf16[208,256]{1,0:T(8,128)(2,1)S(1)} %get-tuple-element.44), channel_id=1, source_target_pairs={{0,8},{4,12},{8,0},{12,4},{1,9},{5,13},{9,1},{13,5},{2,10},{6,14},... | collective-permute-start | bytes 319496 | tf_op jit(solution)/shard_map/ppermute | solution.py:537
  26.3 5.5 %collective-permute-start.8 = (bf16[16,256]{1,0:T(8,128)(2,1)S(1)}, bf16[16,256]{1,0:T(8,128)(2,1)S(1)}, u32[]{:S(2)}, u32[]{:S(2)}) collective-permute-start(bf16[16,256]{1,0:T(8,128)(2,1)S(1)} %slice.57), channel_id=1, source_target_pairs={{0,12},{4,8},{8,4},{12,0},{1,13},{5,9},{9,5},{13,1},{2,14},{6,10},... | collective-permute-start | bytes 24584 | tf_op jit(solution)/shard_map/ppermute | solution.py:410
  28.9 3.9 %copy-start.3 = (bf16[1280,256]{1,0:T(8,128)(2,1)S(1)}, bf16[1280,256]{1,0:T(8,128)(2,1)}, u32[]{:S(2)}) copy-start(bf16[1280,256]{1,0:T(8,128)(2,1)} %weight_ref.4) | copy-start | bytes 1966084
  28.9 3.9 %copy-start.6 = (f32[4,256]{1,0:T(4,128)S(1)}, f32[4,256]{1,0:T(4,128)}, u32[]{:S(2)}) copy-start(f32[4,256]{1,0:T(4,128)} %bias_branch_ref.1) | copy-start | bytes 12292
  28.9 3.9 %copy-start.8 = (f32[256]{0:T(256)S(1)}, f32[256]{0:T(256)}, u32[]{:S(2)}) copy-start(f32[256]{0:T(256)} %param.21) | copy-start | bytes 3076
  29.0 3.9 %copy-start.9 = (f32[256]{0:T(256)S(1)}, f32[256]{0:T(256)}, u32[]{:S(2)}) copy-start(f32[256]{0:T(256)} %param.23) | copy-start | bytes 3076
  33.3 4.8 %collective-permute-start.10 = (bf16[192,256]{1,0:T(8,128)(2,1)S(1)}, bf16[192,256]{1,0:T(8,128)(2,1)S(1)}, u32[]{:S(2)}, u32[]{:S(2)}) collective-permute-start(bf16[192,256]{1,0:T(8,128)(2,1)S(1)} %get-tuple-element.45.refs_0_), channel_id=1, source_target_pairs={{0,2},{1,3},{2,0},{3,1},{4,6},{5,7},{6,4},{7,5},{8,10},{9,11},{10,... | collective-permute-start | bytes 294920 | tf_op jit(solution)/shard_map/ppermute | solution.py:410
  33.9 2.8 %collective-permute-start.12 = (bf16[96,256]{1,0:T(8,128)(2,1)S(1)}, bf16[96,256]{1,0:T(8,128)(2,1)S(1)}, u32[]{:S(2)}, u32[]{:S(2)}) collective-permute-start(bf16[96,256]{1,0:T(8,128)(2,1)S(1)} %get-tuple-element.46), channel_id=1, source_target_pairs={{1,4},{4,1},{5,8},{8,5},{9,12},{12,9},{3,6},{6,3},{7,10},{10,7},{1... | collective-permute-start | bytes 147464 | tf_op jit(solution)/shard_map/ppermute | solution.py:436
  34.5 6.7 %collective-permute-start.9 = (bf16[192,256]{1,0:T(8,128)(2,1)S(1)}, bf16[192,256]{1,0:T(8,128)(2,1)S(1)}, u32[]{:S(2)}, u32[]{:S(2)}) collective-permute-start(bf16[192,256]{1,0:T(8,128)(2,1)S(1)} %get-tuple-element.45.refs_0_), channel_id=1, source_target_pairs={{0,1},{1,0},{2,3},{3,2},{4,5},{5,4},{6,7},{7,6},{8,9},{9,8},{10,11... | collective-permute-start | bytes 294920 | tf_op jit(solution)/shard_map/ppermute | solution.py:410
  36.6 4.1 %collective-permute-start.14 = (bf16[96,256]{1,0:T(8,128)(2,1)S(1)}, bf16[96,256]{1,0:T(8,128)(2,1)S(1)}, u32[]{:S(2)}, u32[]{:S(2)}) collective-permute-start(bf16[96,256]{1,0:T(8,128)(2,1)S(1)} %collective-permute-done.12.refs_4_), channel_id=1, source_target_pairs={{0,2},{1,3},{2,0},{3,1},{4,6},{5,7},{6,4},{7,5},{8,10},{9,11},{10,... | collective-permute-start | bytes 147464 | tf_op jit(solution)/shard_map/ppermute | solution.py:410
  38.1 4.0 %collective-permute-start.11 = (bf16[192,256]{1,0:T(8,128)(2,1)S(1)}, bf16[192,256]{1,0:T(8,128)(2,1)S(1)}, u32[]{:S(2)}, u32[]{:S(2)}) collective-permute-start(bf16[192,256]{1,0:T(8,128)(2,1)S(1)} %collective-permute-done.10.refs_2_), channel_id=1, source_target_pairs={{0,1},{1,0},{2,3},{3,2},{4,5},{5,4},{6,7},{7,6},{8,9},{9,8},{10,11... | collective-permute-start | bytes 294920 | tf_op jit(solution)/shard_map/ppermute | solution.py:410
  39.5 1.7 %collective-permute-start.13 = (bf16[96,256]{1,0:T(8,128)(2,1)S(1)}, bf16[96,256]{1,0:T(8,128)(2,1)S(1)}, u32[]{:S(2)}, u32[]{:S(2)}) collective-permute-start(bf16[96,256]{1,0:T(8,128)(2,1)S(1)} %collective-permute-done.12.refs_4_), channel_id=1, source_target_pairs={{0,1},{1,0},{2,3},{3,2},{4,5},{5,4},{6,7},{7,6},{8,9},{9,8},{10,11... | collective-permute-start | bytes 147464 | tf_op jit(solution)/shard_map/ppermute | solution.py:410
  40.7 1.4 %collective-permute-start.15 = (bf16[96,256]{1,0:T(8,128)(2,1)S(1)}, bf16[96,256]{1,0:T(8,128)(2,1)S(1)}, u32[]{:S(2)}, u32[]{:S(2)}) collective-permute-start(bf16[96,256]{1,0:T(8,128)(2,1)S(1)} %collective-permute-done.14.refs_6_), channel_id=1, source_target_pairs={{0,1},{1,0},{2,3},{3,2},{4,5},{5,4},{6,7},{7,6},{8,9},{9,8},{10,11... | collective-permute-start | bytes 147464 | tf_op jit(solution)/shard_map/ppermute | solution.py:410

commit v5 on v4

--- a/solution.py
+++ b/solution.py
@@ -116,12 +116,17 @@
     width = taps.shape[1] // 3
     if dilation >= columns:
         return jnp.dot(rows, taps[:, width : 2 * width], preferred_element_type=F32)
-    result = jnp.dot(rows, taps, preferred_element_type=F32)
-    return (
-        result[:, width : 2 * width]
-        + shifted(result[:, :width], dilation, columns)
-        + shifted(result[:, 2 * width :], -dilation, columns)
-    )
+    channels = rows.shape[1]
+    image = rows.reshape(-1, columns, channels)
+    reach = columns - dilation // 16 * 16
+    first = jnp.dot(image[:, :reach].reshape(-1, channels), taps[:, :width], preferred_element_type=F32)
+    last = jnp.dot(image[:, columns - reach :].reshape(-1, channels), taps[:, 2 * width :], preferred_element_type=F32)
+    middle = jnp.dot(rows, taps[:, width : 2 * width], preferred_element_type=F32).reshape(-1, columns, width)
+    first = first.reshape(-1, reach, width)[:, : columns - dilation]
+    last = last.reshape(-1, reach, width)[:, reach - (columns - dilation) :]
+    gap = jnp.zeros((first.shape[0], dilation, width), F32)
+    total = middle + jnp.concatenate([gap, first], axis=1) + jnp.concatenate([last, gap], axis=1)
+    return total.reshape(-1, width)
 
 
 def store_halves(keep, send, index, value):
@@ -191,7 +196,10 @@
     return copies
 
 
-def own_kernel(plan, mask_ref, features_ref, one_ref, dilated_ref, keep, send, slots_ref, land_ref, held_ref, rows_ref, ones_ref, taps_ref, sems, tap_sems):
+def own_kernel(plan, mask_ref, features_ref, one_ref, dilated_ref, keep, send, *refs):
+    terms = len(plan.terms)
+    far_taps, refs = refs[:terms], refs[terms:]
+    slots_ref, land_ref, held_ref, rows_ref, ones_ref, taps_ref, sems, tap_sems, far_sems = refs
     copies = [
         pltpu.make_async_copy(mask_ref, land_ref, sems.at[0]),
         pltpu.make_async_copy(features_ref, held_ref, sems.at[1]),
@@ -199,21 +207,34 @@
     ]
     for copy in copies:
         copy.start()
-    tap_copies = [
-        fetch_taps(dilated_ref, branch, 1, taps_ref, branch, tap_sems)
-        for branch in range(len(DILATIONS))
-    ]
+    tap_copies = [fetch_taps(dilated_ref, 0, 1, taps_ref, 0, tap_sems)]
     copies[0].wait()
     copies[1].wait()
+    for branch in range(1, len(DILATIONS)):
+        tap_copies.append(fetch_taps(dilated_ref, branch, 1, taps_ref, branch, tap_sems))
     gather(plan, land_ref, held_ref, slots_ref, rows_ref)
+    far_copies = []
+    for term, (branch, hop, row_tap, _) in enumerate(plan.terms):
+        if row_tap is None:
+            row_tap = jnp.where(lax.axis_index("band") + hop < plan.bands, 0, 2)
+        far_copies.append(
+            pltpu.make_async_copy(dilated_ref.at[branch, row_tap], far_taps[term], far_sems.at[term])
+        )
+        far_copies[-1].start()
     copies[2].wait()
     value = jnp.dot(rows_ref[...], ones_ref[...], preferred_element_type=F32)
     store_halves(keep, send, 0, value)
     for branch, waits in enumerate(tap_copies):
         for copy in waits:
             copy.wait()
-        value = tap_sum(rows_ref[...], taps_ref[branch], DILATIONS[branch], plan.columns)
-        store_halves(keep, send, branch + 1, value)
+        half = keep.shape[0]
+        width = taps_ref.shape[2] // 3
+        lanes = pl.ds((branch + 1) * width, width)
+        for out, start in ((send, half), (keep, 0)):
+            value = tap_sum(rows_ref[pl.ds(start, half)], taps_ref[branch], DILATIONS[branch], plan.columns)
+            out[:, lanes] = value.astype(BF16)
+    for copy in far_copies:
+        copy.wait()
 
 
 def own_partials(plan, mask, features, weight_one, weight_dilated):
@@ -222,7 +243,7 @@
     out = jax.ShapeDtypeStruct((half, (1 + len(DILATIONS)) * width), BF16)
     return call(
         functools.partial(own_kernel, plan),
-        (out, out),
+        (out, out, *[jax.ShapeDtypeStruct((3, channels, width), BF16) for _ in plan.terms]),
         [HBM, HBM, HBM, HBM],
         [
             pltpu.SMEM((2, plan.batches * MOST_LAND), jnp.int32),
@@ -233,6 +254,7 @@
             pltpu.VMEM((len(DILATIONS), channels, 3 * width), BF16),
             pltpu.SemaphoreType.DMA((3,)),
             pltpu.SemaphoreType.DMA((len(DILATIONS), 3)),
+            pltpu.SemaphoreType.DMA((len(plan.terms),)),
         ],
         WHOLE_VMEM,
     )(mask, features, weight_one, weight_dilated)
@@ -411,9 +433,11 @@
 
 
 def add_halves(keep, moved):
-    total = (keep.astype(F32) + moved.astype(F32)).astype(BF16)
-    half = total.shape[0] // 2
-    return total[:half], total[half:]
+    half = keep.shape[0] // 2
+    return tuple(
+        (keep[rows].astype(F32) + moved[rows].astype(F32)).astype(BF16)
+        for rows in (slice(0, half), slice(half, 2 * half))
+    )
 
 
 def spread_over(value, plan):
@@ -481,7 +505,7 @@
     plan = Plan(batches, row_count, columns, bands, sects)
     width = weight_one.shape[1]
     band = lax.axis_index("band")
-    keep, send = own_partials(plan, land_mask, features, weight_one, weight_dilated)
+    keep, send, *taps = own_partials(plan, land_mask, features, weight_one, weight_dilated)
     keep, send, late_mask, late_features, late_low = lax.optimization_barrier(
         (keep, send, land_mask, features, low_level)
     )
@@ -500,13 +524,6 @@
     moved = swap(send, "sect", plan.sects // 2)
     far_mask = jnp.stack(far_masks)
     far_mask, send = lax.optimization_barrier((far_mask, send))
-    taps = []
-    for branch, hop, row_tap, _ in plan.terms:
-        if row_tap is None:
-            row_tap = jnp.where(band + hop < bands, 0, 2)
-        start = (branch, row_tap, 0, 0, 0)
-        size = (1, 1) + weight_dilated.shape[2:]
-        taps.append(lax.dynamic_slice(weight_dilated, start, size)[0, 0])
     far_keep, far_send = far_partials(plan, far_mask, pool, late_features, taps)
     far_keep, far_send, late_low = lax.optimization_barrier((far_keep, far_send, late_low))
     for bit in range(plan.bits - 1):

time: 45.2 us -> 43.8 us (0.969)
  local copies, waits for them, and re-layouts: 2.23 us -> 0.2 us
  other arithmetic: 0.37 us -> 1.09 us
  Pallas kernels: 12.2 us -> 11.5 us
  starting transfers between devices: 21 us -> 21.6 us
    squeeze x1 -> x0, local copies, waits for them, and re-layouts: 1.23 us -> none  [shards(): taps.append(lax.dynamic_slice(weight_dilated, start, size)[0, 0])]
    ppermute x12, waiting for transfers between devices: 7.5 us -> 8.41 us  [swap(): return lax.ppermute(value, axis, [(i, i ^ pattern) for i in range(count)])]
    ppermute x1, starting transfers between devices: 0.22 us -> 1.09 us  [shards(): far_terms.append(lax.ppermute(rows[:, lanes], 'band', pairs))]
    ppermute x1, waiting for transfers between devices: 1.04 us -> 0.2 us  [shards(): far_terms.append(lax.ppermute(rows[:, lanes], 'band', pairs))]
    slice x2 -> x0, local copies, waits for them, and re-layouts: 0.81 us -> none  [add_halves(): return (total[:half], total[half:])]
    convert_element_type x2, other arithmetic: 0.36 us -> 1.08 us  [add_halves(): (keep[rows].astype(F32) + moved[rows].astype(F32)).astype(BF16)]
    pallas_call x1, Pallas kernels: 6.75 us -> 6.11 us  [own_partials(): call(functools.partial(own_kernel, plan), (out, out, *[jax.ShapeDtypeStru...]
  transfers between devices with their start and end apart: 16 -> 16, of which waited for: 7 -> 8; matrix products, arithmetic and copies ran while one was open for 6% -> 3% of each run, Pallas kernels for 4% -> 4%
where the time goes in v5:
time: 43.8 us; the launch traced here: 43.2 us
  starting transfers between devices  21.6 us (49%)
  Pallas kernels  11.5 us (26%)
  waiting for transfers between devices  8.7 us (20%)
  other arithmetic  1.09 us (2%)
    ppermute x12, starting transfers between devices, swap(): return lax.ppermute(value, axis, [(i, i ^ pattern) for i in range(count)])  15.5 us
    ppermute x12, waiting for transfers between devices, swap(): return lax.ppermute(value, axis, [(i, i ^ pattern) for i in range(count)])  8.41 us
    pallas_call x1, Pallas kernels, own_partials(): call(functools.partial(own_kernel, plan), (out, out, *[jax.ShapeDtypeStru...  6.11 us
    ppermute x1, starting transfers between devices, shards(): lax.ppermute(late_mask, 'band', [(target, source) for source, target in p...  3.66 us
    pallas_call x1, Pallas kernels, shards(): call(functools.partial(merge_kernel, plan), jax.ShapeDtypeStruct(low_part...  2.39 us
    pallas_call x1, Pallas kernels, shards(): call(functools.partial(low_kernel, plan), jax.ShapeDtypeStruct((batches,...  1.33 us
    ppermute x1, starting transfers between devices, shards(): far_terms.append(lax.ppermute(rows[:, lanes], 'band', pairs))  1.09 us
    convert_element_type x2, other arithmetic, add_halves(): (keep[rows].astype(F32) + moved[rows].astype(F32)).astype(BF16)  1.08 us
  transfers between devices with their start and end apart: 16, of which 8 were waited for; matrix products, arithmetic and copies ran while one was open for 3% of the time, Pallas kernels for 4%

profile of v5, /device:TPU:0, one launch (start us, length us, event | category | flops | bytes accessed | tf_op | source)
XLA Modules:
  0.0 43.2 jit_solution(14365155905254939775)
XLA Ops:
  0.0 6.1 %shard_map.136 = (bf16[384,1024]{1,0:T(8,128)(2,1)}, bf16[384,1024]{1,0:T(8,128)(2,1)}, bf16[3,512,256]{2,1,0:T(8,128)(2,1)}) custom-call(s32[2,6]{1,0:T(2,128)} %mask_ref.5, bf16[2,6,96,512]{3,2,1,0:T(8,128)(2,1)} %features_ref.3, bf16[512,256]{1,0:T(8,128)(2,1)} %one_ref.1, bf16[3,3,3,512,256]{4,3,2,1,0:T(8,128)(2,1)} %dilated_ref.1), custom_call_target="tpu_custom_call" | custom-call | flops 1024 | bytes 1024 | tf_op jit(solution)/shard_map/pallas_call | solution.py:244
  6.1 0.5 %collective-permute-start = (bf16[384,1024]{1,0:T(8,128)(2,1)}, bf16[384,1024]{1,0:T(8,128)(2,1)S(1)}, u32[]{:S(2)}, u32[]{:S(2)}) collective-permute-start(bf16[384,1024]{1,0:T(8,128)(2,1)} %get-tuple-element.30), channel_id=1, source_target_pairs={{0,1},{1,0},{2,3},{3,2},{4,5},{5,4},{6,7},{7,6},{8,9},{9,8},{10,11... | collective-permute-start | bytes 2359304 | tf_op jit(solution)/shard_map/ppermute | solution.py:432
  6.7 3.7 %collective-permute-start.1 = (s32[2,6]{1,0:T(2,128)S(1)}, s32[2,6]{1,0:T(2,128)S(1)}, u32[]{:S(2)}, u32[]{:S(2)}) collective-permute-start(s32[2,6]{1,0:T(2,128)S(1)} %copy-done.6), channel_id=1, source_target_pairs={{8,0},{12,4},{0,8},{4,12},{9,1},{13,5},{1,9},{5,13},{10,2},{14,6},... | collective-permute-start | bytes 152 | tf_op jit(solution)/shard_map/ppermute | solution.py:513
  10.3 0.4 shard_map.137.pool_ref
  10.7 0.0 copy-start.3
  10.7 0.0 collective-permute-done
  10.8 1.0 %add_convert_fusion = (bf16[192,1024]{1,0:T(8,128)(2,1)}, bf16[192,1024]{1,0:T(8,128)(2,1)S(1)}) fusion(bf16[384,1024]{1,0:T(8,128)(2,1)S(1)} %collective-permute-done, bf16[384,1024]{1,0:T(8,128)(2,1)S(1)} %copy-done.12), kind=kLoop, calls=%fused_computation | loop fusion | flops 1572864 | bytes 2359296 | tf_op jit(solution)/shard_map/convert_element_type | solution.py:438
  11.8 0.1 collective-permute-done.1
  11.9 0.0 copy-done.3
  11.9 0.9 %shard_map.138 = (bf16[416,256]{1,0:T(8,128)(2,1)S(1)}, bf16[416,256]{1,0:T(8,128)(2,1)S(1)}) custom-call(s32[1,2,6]{2,1,0:T(2,128)S(1)} %bitcast.5, bf16[16,256]{1,0:T(8,128)(2,1)S(1)} %shard_map.137.pool_ref, bf16[2,6,96,512]{3,2,1,0:T(8,128)(2,1)S(1)} %copy-done, bf16[3,512,256]{2,1,0:T(8,128)(2,1)S(1)} %copy-done.3), custom_call_target="tpu_custom_call" | custom-call | flops 1024 | bytes 1024 | tf_op jit(solution)/shard_map/pallas_call | solution.py:287
  12.8 0.0 copy-start.13
  12.8 0.0 copy-start.1
  12.8 0.0 copy-start.8
  12.8 0.0 copy-start.11
  12.8 0.2 collective-permute-start.2
  13.1 1.3 %collective-permute-done.2 = bf16[416,256]{1,0:T(8,128)(2,1)S(1)} collective-permute-done((bf16[416,256]{1,0:T(8,128)(2,1)S(1)}, bf16[416,256]{1,0:T(8,128)(2,1)S(1)}, u32[]{:S(2)}, u32[]{:S(2)}) %collective-permute-start.2) | collective-permute-done | bytes 213024 | tf_op jit(solution)/shard_map/ppermute | solution.py:432
  14.4 0.1 add_convert_fusion.2
  14.4 1.9 %collective-permute-start.3 = (bf16[208,256]{1,0:T(8,128)(2,1)S(1)}, bf16[208,256]{1,0:T(8,128)(2,1)S(1)}, u32[]{:S(2)}, u32[]{:S(2)}) collective-permute-start(bf16[208,256]{1,0:T(8,128)(2,1)S(1)} %get-tuple-element.51), channel_id=1, source_target_pairs={{0,2},{1,3},{2,0},{3,1},{4,6},{5,7},{6,4},{7,5},{8,10},{9,11},{10,... | collective-permute-start | bytes 319496 | tf_op jit(solution)/shard_map/ppermute | solution.py:432
  16.3 0.7 %collective-permute-start.4 = (bf16[192,256]{1,0:T(8,128)(2,1)S(1)}, bf16[192,256]{1,0:T(8,128)(2,1)S(1)}, u32[]{:S(2)}, u32[]{:S(2)}) collective-permute-start(bf16[192,256]{1,0:T(8,128)(2,1)S(1)} %shard_map.139), channel_id=1, source_target_pairs={{4,8},{8,4},{5,9},{9,5},{6,10},{10,6},{7,11},{11,7},{20,24},{24,20... | collective-permute-start | bytes 294920 | tf_op jit(solution)/shard_map/ppermute | solution.py:539
  17.0 0.3 collective-permute-start.6
  17.3 0.0 collective-permute-done.4.second_ref
  17.3 2.4 %collective-permute-done.3.moved_ref = bf16[208,256]{1,0:T(8,128)(2,1)S(1)} collective-permute-done((bf16[208,256]{1,0:T(8,128)(2,1)S(1)}, bf16[208,256]{1,0:T(8,128)(2,1)S(1)}, u32[]{:S(2)}, u32[]{:S(2)}) %collective-permute-start.3) | collective-permute-done | bytes 106528 | tf_op jit(solution)/shard_map/ppermute | solution.py:432
  19.7 4.8 %collective-permute-start.5 = (bf16[208,256]{1,0:T(8,128)(2,1)S(1)}, bf16[208,256]{1,0:T(8,128)(2,1)S(1)}, u32[]{:S(2)}, u32[]{:S(2)}) collective-permute-start(bf16[208,256]{1,0:T(8,128)(2,1)S(1)} %get-tuple-element.42), channel_id=1, source_target_pairs={{0,4},{4,0},{8,12},{12,8},{1,5},{5,1},{9,13},{13,9},{2,6},{6,2},{1... | collective-permute-start | bytes 319496 | tf_op jit(solution)/shard_map/ppermute | solution.py:432
  24.5 1.1 %collective-permute-start.7 = (bf16[208,256]{1,0:T(8,128)(2,1)S(1)}, bf16[208,256]{1,0:T(8,128)(2,1)S(1)}, u32[]{:S(2)}, u32[]{:S(2)}) collective-permute-start(bf16[208,256]{1,0:T(8,128)(2,1)S(1)} %get-tuple-element.46), channel_id=1, source_target_pairs={{0,8},{4,12},{8,0},{12,4},{1,9},{5,13},{9,1},{13,5},{2,10},{6,14},... | collective-permute-start | bytes 319496 | tf_op jit(solution)/shard_map/ppermute | solution.py:554
  25.6 1.4 %collective-permute-start.8 = (bf16[16,256]{1,0:T(8,128)(2,1)S(1)}, bf16[16,256]{1,0:T(8,128)(2,1)S(1)}, u32[]{:S(2)}, u32[]{:S(2)}) collective-permute-start(bf16[16,256]{1,0:T(8,128)(2,1)S(1)} %slice.73), channel_id=1, source_target_pairs={{0,12},{4,8},{8,4},{12,0},{1,13},{5,9},{9,5},{13,1},{2,14},{6,10},... | collective-permute-start | bytes 24584 | tf_op jit(solution)/shard_map/ppermute | solution.py:432
  27.0 0.1 copy.15.reduce_ref
  27.1 1.2 %collective-permute-done.5.first_ref = bf16[208,256]{1,0:T(8,128)(2,1)S(1)} collective-permute-done((bf16[208,256]{1,0:T(8,128)(2,1)S(1)}, bf16[208,256]{1,0:T(8,128)(2,1)S(1)}, u32[]{:S(2)}, u32[]{:S(2)}) %collective-permute-start.5) | collective-permute-done | bytes 106528 | tf_op jit(solution)/shard_map/ppermute | solution.py:432
  28.3 0.0 copy-start.4
  28.3 0.0 copy-start.7
  28.3 0.0 copy-start.9
  28.3 0.0 copy-start.10
  28.3 1.3 %shard_map.141.low_ref = f32[2,6,96,256]{3,2,1,0:T(8,128)S(1)} custom-call(bf16[2,6,96,256]{3,2,1,0:T(8,128)(2,1)S(1)} %copy-done.2, bf16[208,256]{1,0:T(8,128)(2,1)S(1)} %collective-permute-done.5.first_ref, bf16[192,256]{1,0:T(8,128)(2,1)S(1)} %collective-permute-done.4.second_ref, bf16[256,48]{1,0:T(8,128)(2,1)S(1)} %copy.15.reduce_ref, ...), custom_call_target="tpu_custom_call" | custom-call | flops 1024 | bytes 1024 | tf_op jit(solution)/shard_map/pallas_call | solution.py:566
  29.7 1.5 %collective-permute-done.8 = bf16[16,256]{1,0:T(8,128)(2,1)S(1)} collective-permute-done((bf16[16,256]{1,0:T(8,128)(2,1)S(1)}, bf16[16,256]{1,0:T(8,128)(2,1)S(1)}, u32[]{:S(2)}, u32[]{:S(2)}) %collective-permute-start.8) | collective-permute-done | bytes 8224 | tf_op jit(solution)/shard_map/ppermute | solution.py:432
  31.1 0.2 collective-permute-done.7.refs_0_
  31.4 0.3 shard_map.142
  31.7 0.6 %collective-permute-start.10 = (bf16[192,256]{1,0:T(8,128)(2,1)S(1)}, bf16[192,256]{1,0:T(8,128)(2,1)S(1)}, u32[]{:S(2)}, u32[]{:S(2)}) collective-permute-start(bf16[192,256]{1,0:T(8,128)(2,1)S(1)} %get-tuple-element.47.refs_0_), channel_id=1, source_target_pairs={{0,2},{1,3},{2,0},{3,1},{4,6},{5,7},{6,4},{7,5},{8,10},{9,11},{10,... | collective-permute-start | bytes 294920 | tf_op jit(solution)/shard_map/ppermute | solution.py:432
  32.3 0.7 %collective-permute-start.12 = (bf16[96,256]{1,0:T(8,128)(2,1)S(1)}, bf16[96,256]{1,0:T(8,128)(2,1)S(1)}, u32[]{:S(2)}, u32[]{:S(2)}) collective-permute-start(bf16[96,256]{1,0:T(8,128)(2,1)S(1)} %get-tuple-element.48), channel_id=1, source_target_pairs={{1,4},{4,1},{5,8},{8,5},{9,12},{12,9},{3,6},{6,3},{7,10},{10,7},{1... | collective-permute-start | bytes 147464 | tf_op jit(solution)/shard_map/ppermute | solution.py:460
  33.0 2.3 %collective-permute-start.9 = (bf16[192,256]{1,0:T(8,128)(2,1)S(1)}, bf16[192,256]{1,0:T(8,128)(2,1)S(1)}, u32[]{:S(2)}, u32[]{:S(2)}) collective-permute-start(bf16[192,256]{1,0:T(8,128)(2,1)S(1)} %get-tuple-element.47.refs_0_), channel_id=1, source_target_pairs={{0,1},{1,0},{2,3},{3,2},{4,5},{5,4},{6,7},{7,6},{8,9},{9,8},{10,11... | collective-permute-start | bytes 294920 | tf_op jit(solution)/shard_map/ppermute | solution.py:432
  35.3 0.0 collective-permute-done.12.refs_4_
  35.3 1.5 %collective-permute-start.14 = (bf16[96,256]{1,0:T(8,128)(2,1)S(1)}, bf16[96,256]{1,0:T(8,128)(2,1)S(1)}, u32[]{:S(2)}, u32[]{:S(2)}) collective-permute-start(bf16[96,256]{1,0:T(8,128)(2,1)S(1)} %collective-permute-done.12.refs_4_), channel_id=1, source_target_pairs={{0,2},{1,3},{2,0},{3,1},{4,6},{5,7},{6,4},{7,5},{8,10},{9,11},{10,... | collective-permute-start | bytes 147464 | tf_op jit(solution)/shard_map/ppermute | solution.py:432
  36.8 1.4 %collective-permute-start.11 = (bf16[192,256]{1,0:T(8,128)(2,1)S(1)}, bf16[192,256]{1,0:T(8,128)(2,1)S(1)}, u32[]{:S(2)}, u32[]{:S(2)}) collective-permute-start(bf16[192,256]{1,0:T(8,128)(2,1)S(1)} %collective-permute-done.10.refs_2_), channel_id=1, source_target_pairs={{0,1},{1,0},{2,3},{3,2},{4,5},{5,4},{6,7},{7,6},{8,9},{9,8},{10,11... | collective-permute-start | bytes 294920 | tf_op jit(solution)/shard_map/ppermute | solution.py:432
  38.2 0.0 collective-permute-start.13
  38.2 1.2 %collective-permute-done.14.refs_6_ = bf16[96,256]{1,0:T(8,128)(2,1)S(1)} collective-permute-done((bf16[96,256]{1,0:T(8,128)(2,1)S(1)}, bf16[96,256]{1,0:T(8,128)(2,1)S(1)}, u32[]{:S(2)}, u32[]{:S(2)}) %collective-permute-start.14) | collective-permute-done | bytes 49184 | tf_op jit(solution)/shard_map/ppermute | solution.py:432
  39.4 0.5 %collective-permute-start.15 = (bf16[96,256]{1,0:T(8,128)(2,1)S(1)}, bf16[96,256]{1,0:T(8,128)(2,1)S(1)}, u32[]{:S(2)}, u32[]{:S(2)}) collective-permute-start(bf16[96,256]{1,0:T(8,128)(2,1)S(1)} %collective-permute-done.14.refs_6_), channel_id=1, source_target_pairs={{0,1},{1,0},{2,3},{3,2},{4,5},{5,4},{6,7},{7,6},{8,9},{9,8},{10,11... | collective-permute-start | bytes 147464 | tf_op jit(solution)/shard_map/ppermute | solution.py:432
  39.9 0.0 collective-permute-done.13.refs_5_
  39.9 0.0 collective-permute-done.9.refs_1_
  40.0 0.9 %collective-permute-done.15.refs_7_ = bf16[96,256]{1,0:T(8,128)(2,1)S(1)} collective-permute-done((bf16[96,256]{1,0:T(8,128)(2,1)S(1)}, bf16[96,256]{1,0:T(8,128)(2,1)S(1)}, u32[]{:S(2)}, u32[]{:S(2)}) %collective-permute-start.15) | collective-permute-done | bytes 49184 | tf_op jit(solution)/shard_map/ppermute | solution.py:432
  40.8 2.4 %shard_map.143 = bf16[2,6,96,256]{3,2,1,0:T(8,128)(2,1)} custom-call(s32[2,6]{1,0:T(2,128)S(1)} %copy-done.6, f32[2,6,96,256]{3,2,1,0:T(8,128)S(1)} %shard_map.141.low_ref, bf16[3,3,304,256]{3,2,1,0:T(8,128)(2,1)S(1)} %copy-done.1, bf16[192,256]{1,0:T(8,128)(2,1)S(1)} %get-tuple-element.47.refs_0_, bf16[192,256]{1,0:T(8,128)(2,1)S(1)} %collective-permute-done.9.refs_1_, ...), custom_call_target="tpu_custom_call" | custom-call | flops 1024 | bytes 1024 | tf_op jit(solution)/shard_map/pallas_call | solution.py:602
  (25 shorter events, 0.1 us)
Async XLA Ops:
  0.0 10.3 %copy-start = (bf16[2,6,96,512]{3,2,1,0:T(8,128)(2,1)S(1)}, bf16[2,6,96,512]{3,2,1,0:T(8,128)(2,1)}, u32[]{:S(2)}) copy-start(bf16[2,6,96,512]{3,2,1,0:T(8,128)(2,1)} %features_ref.3) | copy-start | bytes 3538948
  0.0 6.7 %copy-start.6 = (s32[2,6]{1,0:T(2,128)S(1)}, s32[2,6]{1,0:T(2,128)}, u32[]{:S(2)}) copy-start(s32[2,6]{1,0:T(2,128)} %mask_ref.5) | copy-start | bytes 148
  0.0 10.3 %copy-start.5 = (bf16[512,256]{1,0:T(8,128)(2,1)S(1)}, bf16[512,256]{1,0:T(8,128)(2,1)}, u32[]{:S(2)}) copy-start(bf16[512,256]{1,0:T(8,128)(2,1)} %weight_ref.3) | copy-start | bytes 786436
  6.1 4.6 %copy-start.12 = (bf16[384,1024]{1,0:T(8,128)(2,1)S(1)}, bf16[384,1024]{1,0:T(8,128)(2,1)}, u32[]{:S(2)}) copy-start(bf16[384,1024]{1,0:T(8,128)(2,1)} %get-tuple-element.29) | copy-start | bytes 2359300
  6.1 4.6 %collective-permute-start = (bf16[384,1024]{1,0:T(8,128)(2,1)}, bf16[384,1024]{1,0:T(8,128)(2,1)S(1)}, u32[]{:S(2)}, u32[]{:S(2)}) collective-permute-start(bf16[384,1024]{1,0:T(8,128)(2,1)} %get-tuple-element.30), channel_id=1, source_target_pairs={{0,1},{1,0},{2,3},{3,2},{4,5},{5,4},{6,7},{7,6},{8,9},{9,8},{10,11... | collective-permute-start | bytes 2359304 | tf_op jit(solution)/shard_map/ppermute | solution.py:432
  6.7 5.2 %collective-permute-start.1 = (s32[2,6]{1,0:T(2,128)S(1)}, s32[2,6]{1,0:T(2,128)S(1)}, u32[]{:S(2)}, u32[]{:S(2)}) collective-permute-start(s32[2,6]{1,0:T(2,128)S(1)} %copy-done.6), channel_id=1, source_target_pairs={{8,0},{12,4},{0,8},{4,12},{9,1},{13,5},{1,9},{5,13},{10,2},{14,6},... | collective-permute-start | bytes 152 | tf_op jit(solution)/shard_map/ppermute | solution.py:513
  10.7 1.2 %copy-start.3 = (bf16[3,512,256]{2,1,0:T(8,128)(2,1)S(1)}, bf16[3,512,256]{2,1,0:T(8,128)(2,1)}, u32[]{:S(2)}) copy-start(bf16[3,512,256]{2,1,0:T(8,128)(2,1)} %get-tuple-element.34.refs_0_) | copy-start | bytes 2359300
  11.8 4.5 %copy-start.2 = (bf16[2,6,96,256]{3,2,1,0:T(8,128)(2,1)S(1)}, bf16[2,6,96,256]{3,2,1,0:T(8,128)(2,1)}, u32[]{:S(2)}) copy-start(bf16[2,6,96,256]{3,2,1,0:T(8,128)(2,1)} %low_ref.2) | copy-start | bytes 1769476
  12.8 14.2 %copy-start.13 = (bf16[256,48]{0,1:T(8,128)(2,1)S(1)}, bf16[256,48]{0,1:T(8,128)(2,1)}, u32[]{:S(2)}) copy-start(bf16[256,48]{0,1:T(8,128)(2,1)} %param.24) | copy-start | bytes 73732
  12.8 15.5 %copy-start.1 = (bf16[3,3,304,256]{3,2,1,0:T(8,128)(2,1)S(1)}, bf16[3,3,304,256]{3,2,1,0:T(8,128)(2,1)}, u32[]{:S(2)}) copy-start(bf16[3,3,304,256]{3,2,1,0:T(8,128)(2,1)} %weight_ref.5) | copy-start | bytes 4202500
  12.8 15.5 %copy-start.8 = (f32[256]{0:T(256)S(1)}, f32[256]{0:T(256)}, u32[]{:S(2)}) copy-start(f32[256]{0:T(256)} %param.27) | copy-start | bytes 3076
  12.8 15.4 %copy-start.11 = (f32[48]{0:T(128)S(1)}, f32[48]{0:T(128)}, u32[]{:S(2)}) copy-start(f32[48]{0:T(128)} %param.25) | copy-start | bytes 580
  12.8 1.5 %collective-permute-start.2 = (bf16[416,256]{1,0:T(8,128)(2,1)S(1)}, bf16[416,256]{1,0:T(8,128)(2,1)S(1)}, u32[]{:S(2)}, u32[]{:S(2)}) collective-permute-start(bf16[416,256]{1,0:T(8,128)(2,1)S(1)} %get-tuple-element.40), channel_id=1, source_target_pairs={{0,1},{1,0},{2,3},{3,2},{4,5},{5,4},{6,7},{7,6},{8,9},{9,8},{10,11... | collective-permute-start | bytes 638984 | tf_op jit(solution)/shard_map/ppermute | solution.py:432
  14.4 5.2 %collective-permute-start.3 = (bf16[208,256]{1,0:T(8,128)(2,1)S(1)}, bf16[208,256]{1,0:T(8,128)(2,1)S(1)}, u32[]{:S(2)}, u32[]{:S(2)}) collective-permute-start(bf16[208,256]{1,0:T(8,128)(2,1)S(1)} %get-tuple-element.51), channel_id=1, source_target_pairs={{0,2},{1,3},{2,0},{3,1},{4,6},{5,7},{6,4},{7,5},{8,10},{9,11},{10,... | collective-permute-start | bytes 319496 | tf_op jit(solution)/shard_map/ppermute | solution.py:432
  16.3 0.9 %collective-permute-start.4 = (bf16[192,256]{1,0:T(8,128)(2,1)S(1)}, bf16[192,256]{1,0:T(8,128)(2,1)S(1)}, u32[]{:S(2)}, u32[]{:S(2)}) collective-permute-start(bf16[192,256]{1,0:T(8,128)(2,1)S(1)} %shard_map.139), channel_id=1, source_target_pairs={{4,8},{8,4},{5,9},{9,5},{6,10},{10,6},{7,11},{11,7},{20,24},{24,20... | collective-permute-start | bytes 294920 | tf_op jit(solution)/shard_map/ppermute | solution.py:539
  17.0 14.4 %collective-permute-start.6 = (bf16[192,1024]{1,0:T(8,128)(2,1)}, bf16[192,1024]{1,0:T(8,128)(2,1)S(1)}, u32[]{:S(2)}, u32[]{:S(2)}) collective-permute-start(bf16[192,1024]{1,0:T(8,128)(2,1)} %get-tuple-element.49), channel_id=1, source_target_pairs={{0,2},{1,3},{2,0},{3,1},{4,6},{5,7},{6,4},{7,5},{8,10},{9,11},{10,... | collective-permute-start | bytes 1179656 | tf_op jit(solution)/shard_map/ppermute | solution.py:432
  19.7 8.6 %collective-permute-start.5 = (bf16[208,256]{1,0:T(8,128)(2,1)S(1)}, bf16[208,256]{1,0:T(8,128)(2,1)S(1)}, u32[]{:S(2)}, u32[]{:S(2)}) collective-permute-start(bf16[208,256]{1,0:T(8,128)(2,1)S(1)} %get-tuple-element.42), channel_id=1, source_target_pairs={{0,4},{4,0},{8,12},{12,8},{1,5},{5,1},{9,13},{13,9},{2,6},{6,2},{1... | collective-permute-start | bytes 319496 | tf_op jit(solution)/shard_map/ppermute | solution.py:432
  24.5 6.8 %collective-permute-start.7 = (bf16[208,256]{1,0:T(8,128)(2,1)S(1)}, bf16[208,256]{1,0:T(8,128)(2,1)S(1)}, u32[]{:S(2)}, u32[]{:S(2)}) collective-permute-start(bf16[208,256]{1,0:T(8,128)(2,1)S(1)} %get-tuple-element.46), channel_id=1, source_target_pairs={{0,8},{4,12},{8,0},{12,4},{1,9},{5,13},{9,1},{13,5},{2,10},{6,14},... | collective-permute-start | bytes 319496 | tf_op jit(solution)/shard_map/ppermute | solution.py:554
  25.6 5.5 %collective-permute-start.8 = (bf16[16,256]{1,0:T(8,128)(2,1)S(1)}, bf16[16,256]{1,0:T(8,128)(2,1)S(1)}, u32[]{:S(2)}, u32[]{:S(2)}) collective-permute-start(bf16[16,256]{1,0:T(8,128)(2,1)S(1)} %slice.73), channel_id=1, source_target_pairs={{0,12},{4,8},{8,4},{12,0},{1,13},{5,9},{9,5},{13,1},{2,14},{6,10},... | collective-permute-start | bytes 24584 | tf_op jit(solution)/shard_map/ppermute | solution.py:432
  28.3 3.1 %copy-start.4 = (bf16[1280,256]{1,0:T(8,128)(2,1)S(1)}, bf16[1280,256]{1,0:T(8,128)(2,1)}, u32[]{:S(2)}) copy-start(bf16[1280,256]{1,0:T(8,128)(2,1)} %weight_ref.4) | copy-start | bytes 1966084
  28.3 3.1 %copy-start.7 = (f32[4,256]{1,0:T(4,128)S(1)}, f32[4,256]{1,0:T(4,128)}, u32[]{:S(2)}) copy-start(f32[4,256]{1,0:T(4,128)} %bias_branch_ref.1) | copy-start | bytes 12292
  28.3 3.1 %copy-start.9 = (f32[256]{0:T(256)S(1)}, f32[256]{0:T(256)}, u32[]{:S(2)}) copy-start(f32[256]{0:T(256)} %param.21) | copy-start | bytes 3076
  28.3 3.1 %copy-start.10 = (f32[256]{0:T(256)S(1)}, f32[256]{0:T(256)}, u32[]{:S(2)}) copy-start(f32[256]{0:T(256)} %param.23) | copy-start | bytes 3076
  31.7 5.1 %collective-permute-start.10 = (bf16[192,256]{1,0:T(8,128)(2,1)S(1)}, bf16[192,256]{1,0:T(8,128)(2,1)S(1)}, u32[]{:S(2)}, u32[]{:S(2)}) collective-permute-start(bf16[192,256]{1,0:T(8,128)(2,1)S(1)} %get-tuple-element.47.refs_0_), channel_id=1, source_target_pairs={{0,2},{1,3},{2,0},{3,1},{4,6},{5,7},{6,4},{7,5},{8,10},{9,11},{10,... | collective-permute-start | bytes 294920 | tf_op jit(solution)/shard_map/ppermute | solution.py:432
  32.3 3.0 %collective-permute-start.12 = (bf16[96,256]{1,0:T(8,128)(2,1)S(1)}, bf16[96,256]{1,0:T(8,128)(2,1)S(1)}, u32[]{:S(2)}, u32[]{:S(2)}) collective-permute-start(bf16[96,256]{1,0:T(8,128)(2,1)S(1)} %get-tuple-element.48), channel_id=1, source_target_pairs={{1,4},{4,1},{5,8},{8,5},{9,12},{12,9},{3,6},{6,3},{7,10},{10,7},{1... | collective-permute-start | bytes 147464 | tf_op jit(solution)/shard_map/ppermute | solution.py:460
  33.0 7.0 %collective-permute-start.9 = (bf16[192,256]{1,0:T(8,128)(2,1)S(1)}, bf16[192,256]{1,0:T(8,128)(2,1)S(1)}, u32[]{:S(2)}, u32[]{:S(2)}) collective-permute-start(bf16[192,256]{1,0:T(8,128)(2,1)S(1)} %get-tuple-element.47.refs_0_), channel_id=1, source_target_pairs={{0,1},{1,0},{2,3},{3,2},{4,5},{5,4},{6,7},{7,6},{8,9},{9,8},{10,11... | collective-permute-start | bytes 294920 | tf_op jit(solution)/shard_map/ppermute | solution.py:432
  35.3 4.1 %collective-permute-start.14 = (bf16[96,256]{1,0:T(8,128)(2,1)S(1)}, bf16[96,256]{1,0:T(8,128)(2,1)S(1)}, u32[]{:S(2)}, u32[]{:S(2)}) collective-permute-start(bf16[96,256]{1,0:T(8,128)(2,1)S(1)} %collective-permute-done.12.refs_4_), channel_id=1, source_target_pairs={{0,2},{1,3},{2,0},{3,1},{4,6},{5,7},{6,4},{7,5},{8,10},{9,11},{10,... | collective-permute-start | bytes 147464 | tf_op jit(solution)/shard_map/ppermute | solution.py:432
  36.8 4.0 %collective-permute-start.11 = (bf16[192,256]{1,0:T(8,128)(2,1)S(1)}, bf16[192,256]{1,0:T(8,128)(2,1)S(1)}, u32[]{:S(2)}, u32[]{:S(2)}) collective-permute-start(bf16[192,256]{1,0:T(8,128)(2,1)S(1)} %collective-permute-done.10.refs_2_), channel_id=1, source_target_pairs={{0,1},{1,0},{2,3},{3,2},{4,5},{5,4},{6,7},{7,6},{8,9},{9,8},{10,11... | collective-permute-start | bytes 294920 | tf_op jit(solution)/shard_map/ppermute | solution.py:432
  38.2 1.7 %collective-permute-start.13 = (bf16[96,256]{1,0:T(8,128)(2,1)S(1)}, bf16[96,256]{1,0:T(8,128)(2,1)S(1)}, u32[]{:S(2)}, u32[]{:S(2)}) collective-permute-start(bf16[96,256]{1,0:T(8,128)(2,1)S(1)} %collective-permute-done.12.refs_4_), channel_id=1, source_target_pairs={{0,1},{1,0},{2,3},{3,2},{4,5},{5,4},{6,7},{7,6},{8,9},{9,8},{10,11... | collective-permute-start | bytes 147464 | tf_op jit(solution)/shard_map/ppermute | solution.py:432
  39.4 1.4 %collective-permute-start.15 = (bf16[96,256]{1,0:T(8,128)(2,1)S(1)}, bf16[96,256]{1,0:T(8,128)(2,1)S(1)}, u32[]{:S(2)}, u32[]{:S(2)}) collective-permute-start(bf16[96,256]{1,0:T(8,128)(2,1)S(1)} %collective-permute-done.14.refs_6_), channel_id=1, source_target_pairs={{0,1},{1,0},{2,3},{3,2},{4,5},{5,4},{6,7},{7,6},{8,9},{9,8},{10,11... | collective-permute-start | bytes 147464 | tf_op jit(solution)/shard_map/ppermute | solution.py:432
